TPU v7x, 32 devices: a whole 2x2x4 slice. The times are simulated.
32 devices in a mesh: groups: 2 (over x), expert: 16 (over z, y, core).
Axes of the slice: x: 2, y: 2, z: 4, core: 2. Of those that a mesh axis runs over, the one named last changes fastest.
Arguments:
- tokens: bfloat16 [4096, 3584], P(('groups', 'expert')), parts along dimension 0, may hold values from -6 to 6
- expert_gate_up: bfloat16 [28672, 2048], P('expert'), may hold values from -0.09375 to 0.09375
- expert_down: bfloat16 [1024, 28672], P(None, 'expert'), may hold values from -0.1875 to 0.1875
- shared_gate_up: bfloat16 [3584, 2048], P('expert'), may hold values from -0.09375 to 0.09375
- shared_down: bfloat16 [1024, 3584], P(None, 'expert'), may hold values from -0.1875 to 0.1875
- host_expert: int32 [8], replicated, may hold values from 0 to 7, each once
- pair_picks: int32 [4096, 2], P(('groups', 'expert')), parts along dimension 0, may hold values from 0 to 7, all different within a row; in each aligned block of 128 rows (0 to 127, 128 to 255, ...) at most 56 rows name the same one
- affinity: float32 [4096, 8], P(('groups', 'expert')), parts along dimension 0, may hold values from 0.02 to 1
Outputs:
- mixed_rows: bfloat16 [4096, 3584], P(('groups', 'expert')), parts along dimension 0
There are 2 independent parts, one for each index of `groups`. A program takes and returns all parts, laid end to end along the dimension named above; an argument that names none is the same for every part. Nothing has to cross between parts.
Inputs may be any that keep to these rules, and one draw needn't show every extreme that they name: host_expert names every expert id once. `pair_picks`: the 2 pairs of a token differ. Among the rows of one device no pair is named more than 56 times, a bound that some block reaches.
All inputs are finite; a program needn't handle non-finite values.
Results may differ from a plain program's by a relative error of at most 0.015.
Values may be sent and summed in bfloat16 or wider, within the bound.
No kernel may reach another device: no remote copies, remote signals or barrier semaphores. Data moves between devices by JAX's collectives and lax.ppermute only.
A program may use at most 128 MiB of HBM per device.

v0:
```python
import jax
import jax.numpy as jnp
from jax import lax
from jax.sharding import PartitionSpec as P

route_scale = 2.5


def from_partner(block, axis, stride):
    count = lax.axis_size(axis)
    route = []
    for low in range(count):
        high = low | 1 << stride
        if high != low and high < count:
            route += [(low, high), (high, low)]
    return lax.ppermute(block, axis, route)


def activate(summed, hidden_units):
    return (jax.nn.silu(summed[:, :hidden_units]) * summed[:, hidden_units:]).astype(jnp.bfloat16)


def ordered(is_upper, own_part, other_part, axis_dim):
    return jnp.where(
        is_upper,
        jnp.concatenate([other_part, own_part], axis_dim),
        jnp.concatenate([own_part, other_part], axis_dim),
    )


def local(
    tokens,
    expert_gate_up,
    expert_down,
    shared_gate_up,
    shared_down,
    host_expert,
    pair_picks,
    affinity,
):
    devices = lax.axis_size("expert")
    pair_count = devices // 2
    top_bit = devices.bit_length() - 2
    dev_index = lax.axis_index("expert")
    pair_side = dev_index // pair_count
    is_upper = pair_side == 1
    tok_rows, width = tokens.shape
    half_width = width // 2
    hidden_units = expert_down.shape[0]
    pick_count = pair_picks.shape[1]
    capacity = 7 * tok_rows * pick_count // (4 * pair_count)
    gate_rows = shared_gate_up
    down_cols = shared_down
    for level_bit in range(top_bit):
        other_rows, other_cols = from_partner((gate_rows, down_cols), "expert", level_bit)
        bit_upper = dev_index >> level_bit & 1 == 1
        gate_rows = ordered(bit_upper, gate_rows, other_rows, 0)
        down_cols = ordered(bit_upper, down_cols, other_cols, 1)
    mine_half = lax.dynamic_slice_in_dim(tokens, pair_side * half_width, half_width, 1)
    their_half = lax.dynamic_slice_in_dim(tokens, (1 - pair_side) * half_width, half_width, 1)
    partner_half = from_partner(their_half, "expert", top_bit)
    shared_in = ordered(is_upper, mine_half, partner_half, 0)
    flat_picks = pair_picks.reshape(-1)
    pair_iota = jnp.arange(pair_count, dtype=jnp.int32)
    pick_hits = (flat_picks[:, None] == pair_iota[None, :]).astype(jnp.int32)
    pick_ranks = jnp.sum(pick_hits * (jnp.cumsum(pick_hits, 0) - 1), 1)
    slot_ids = flat_picks * capacity + pick_ranks
    slot_iota = jnp.arange(pair_count * capacity, dtype=jnp.int32)
    matches = slot_ids[:, None] == slot_iota[None, :]
    token_ids = jnp.arange(tok_rows * pick_count, dtype=jnp.int32) // pick_count
    slot_token = jnp.sum(jnp.where(matches, token_ids[:, None], 0), 0)
    slot_used = jnp.any(matches, 0)
    halves = tokens.reshape(tok_rows, 2, half_width).transpose(1, 0, 2)
    outgoing = jnp.where(
        slot_used[None, :, None], halves[:, slot_token], jnp.zeros((), jnp.bfloat16)
    )
    outgoing = outgoing.reshape(devices, capacity, half_width)
    incoming = lax.all_to_all(outgoing, "expert", split_axis=0, concat_axis=0, tiled=True)
    routed_count = devices * capacity
    routed_in = incoming.reshape(routed_count, half_width)
    home_part = jnp.dot(routed_in, expert_gate_up, preferred_element_type=jnp.float32)
    shared_part = jnp.dot(shared_in, gate_rows, preferred_element_type=jnp.float32)
    partial_value = jnp.concatenate([home_part, shared_part], 0)
    received = from_partner(partial_value.astype(jnp.bfloat16), "expert", top_bit).astype(
        partial_value.dtype
    )
    hidden = activate(partial_value + received, hidden_units)
    routed_out = jnp.dot(
        hidden[:routed_count], expert_down, preferred_element_type=jnp.float32
    ).astype(jnp.bfloat16)
    shared_out = jnp.dot(
        hidden[routed_count:], down_cols, preferred_element_type=jnp.float32
    ).astype(jnp.bfloat16)
    returned = lax.all_to_all(
        routed_out.reshape(devices, capacity, half_width),
        "expert",
        split_axis=0,
        concat_axis=0,
        tiled=True,
    )
    keep_shared = lax.dynamic_slice_in_dim(shared_out, pair_side * tok_rows, tok_rows, 0)
    send_shared = lax.dynamic_slice_in_dim(shared_out, (1 - pair_side) * tok_rows, tok_rows, 0)
    back_shared = from_partner(send_shared, "expert", top_bit)
    shared_halves = jnp.where(
        is_upper, jnp.stack([back_shared, keep_shared]), jnp.stack([keep_shared, back_shared])
    )
    expert_ids = jnp.sum(pick_hits * host_expert[None, :], 1)
    chosen = (expert_ids[:, None] == pair_iota[None, :]).reshape(tok_rows, pick_count, pair_count)
    scores = jnp.sum(jnp.where(chosen, affinity[:, None, :], 0.0), 2)
    gate_weights = route_scale * scores / jnp.sum(scores, 1, keepdims=True)
    picked = returned.reshape(2, pair_count * capacity, half_width)[:, slot_ids]
    picked = picked.reshape(2, tok_rows, pick_count, half_width).astype(jnp.float32)
    mixed_halves = jnp.einsum("sjkd,jk->sjd", picked, gate_weights) + shared_halves.astype(
        jnp.float32
    )
    return mixed_halves.transpose(1, 0, 2).reshape(tok_rows, width).astype(jnp.bfloat16)


def solution(mesh):
    in_specs = (
        P(("groups", "expert"), None),
        P("expert", None),
        P(None, "expert"),
        P("expert", None),
        P(None, "expert"),
        P(),
        P(("groups", "expert"), None),
        P(("groups", "expert"), None),
    )
    out_specs = P(("groups", "expert"), None)
    return jax.shard_map(local, mesh=mesh, in_specs=in_specs, out_specs=out_specs, check_vma=False)
```

profile of v0, /device:TPU:0, one launch (start us, length us, event | category | flops | bytes accessed | tf_op | source)
XLA Modules:
  0.0 587.6 jit_solution(18173616355972837511)
XLA Ops:
  0.0 0.8 copy.24
  1.1 0.6 reduce-window.6
  1.7 0.2 slice_reduce_fusion
  1.9 0.8 fusion.30
  2.7 0.2 fusion.29
  2.8 0.2 select_reduce_fusion
  3.0 2.5 reshape.117
  5.5 20.0 %gather_fusion = bf16[448,2,1792]{2,1,0:T(2,128)(2,1)} fusion(bf16[2,128,1792]{2,0,1:T(2,128)(2,1)S(1)} %bitcast.41, s32[1024]{0:T(1024)S(1)} %pad_clamp_fusion.1), kind=kCustom, calls=%fused_computation | custom fusion | bytes 6424320 | tf_op jit(solution)/shard_map/gather | solution.py:75
  25.5 2.3 copy.27
  27.9 2.0 broadcast_select_fusion
  29.9 7.6 %all-to-all-start = ((bf16[16,56,1792]{2,1,0:T(8,128)(2,1)}), bf16[16,56,1792]{2,1,0:T(8,128)(2,1)}, u32[]{:S(2)}, u32[]{:S(2)}) async-start(bf16[16,56,1792]{2,1,0:T(8,128)(2,1)} %broadcast_select_fusion), calls=%async_computation | async-start | bytes 6422528 | tf_op jit(solution)/shard_map/all_to_all | solution.py:78
  37.5 0.4 collective-permute-start.1
  37.9 2.3 collective-permute-done.1
  40.3 2.3 maximum_select_fusion.7
  42.6 1.9 collective-permute-start.2
  44.4 70.0 %collective-permute-done.2 = bf16[448,2048]{1,0:T(8,128)(2,1)} collective-permute-done((bf16[448,2048]{1,0:T(8,128)(2,1)S(1)}, bf16[448,2048]{1,0:T(8,128)(2,1)}, u32[]{:S(2)}, u32[]{:S(2)}) %collective-permute-start.2) | collective-permute-done | bytes 1835040 | tf_op jit(solution)/shard_map/ppermute | solution.py:16
  114.4 4.7 maximum_select_fusion.2
  119.1 1.5 collective-permute-start.3
  120.6 2.4 collective-permute-start
  123.1 11.8 %fusion.34 = f32[896,2048]{1,0:T(8,128)} fusion(bf16[896,1792]{1,0:T(8,128)(2,1)} %bitcast.9, bf16[1792,2048]{1,0:T(8,128)(2,1)} %param.9), kind=kOutput, calls=%fused_computation.76 | convolution fusion | flops 6576668672 | bytes 17891328 | tf_op jit(solution)/shard_map/dot_general | solution.py:81
  134.9 74.2 %collective-permute-done = bf16[128,1792]{1,0:T(8,128)(2,1)S(1)} collective-permute-done((bf16[128,1792]{1,0:T(8,128)(2,1)S(1)}, bf16[128,1792]{1,0:T(8,128)(2,1)S(1)}, u32[]{:S(2)}, u32[]{:S(2)}) %collective-permute-start) | collective-permute-done | bytes 458784 | tf_op jit(solution)/shard_map/ppermute | solution.py:16
  209.0 1.1 collective-permute-done.3
  210.1 6.7 %fusion.1 = f32[256,2048]{1,0:T(8,128)S(1)} fusion(bf16[896,2048]{1,0:T(8,128)(2,1)} %maximum_select_fusion.2, bf16[896,2048]{1,0:T(8,128)(2,1)} %collective-permute-done.3, pred[]{:T(512)S(6)} %eq.82, bf16[128,1792]{1,0:T(8,128)(2,1)S(1)} %get-tuple-element.12, bf16[128,1792]{1,0:T(8,128)(2,1)S(1)} %collective-permute-done, pred[]{:T(512)S(6)} %eq.81), kind=kOutput, calls=%fused_computation.6 | convolution fusion | flops 1916207104 | bytes 10354690 | tf_op jit(solution)/shard_map/dot_general | solution.py:82
  216.8 5.9 %fusion = bf16[1152,2048]{1,0:T(8,128)(2,1)} fusion(f32[256,2048]{1,0:T(8,128)S(1)} %fusion.1, f32[896,2048]{1,0:T(8,128)} %fusion.34), kind=kLoop, calls=%fused_computation.4 | loop fusion | flops 9437184 | bytes 14155776 | tf_op jit(solution)/shard_map/convert_element_type | solution.py:84
  222.7 2.3 collective-permute-start.4
  225.0 202.5 %collective-permute-done.4 = bf16[1152,2048]{1,0:T(8,128)(2,1)} collective-permute-done((bf16[1152,2048]{1,0:T(8,128)(2,1)}, bf16[1152,2048]{1,0:T(8,128)(2,1)}, u32[]{:S(2)}, u32[]{:S(2)}) %collective-permute-start.4) | collective-permute-done | bytes 4718624 | tf_op jit(solution)/shard_map/ppermute | solution.py:16
  427.5 10.3 %convert_add_fusion = f32[1152,2048]{1,0:T(8,128)} fusion(bf16[1152,2048]{1,0:T(8,128)(2,1)} %collective-permute-done.4, f32[256,2048]{1,0:T(8,128)S(1)} %fusion.1, f32[896,2048]{1,0:T(8,128)} %fusion.34), kind=kLoop, calls=%fused_computation.3 | loop fusion | flops 7077888 | bytes 23592960 | tf_op jit(solution)/shard_map/add | solution.py:87
  437.9 4.6 fusion.8
  442.5 0.2 copy-done.6
  442.7 4.8 convolution_convert_fusion
  447.5 4.8 all-to-all-start.1
  452.3 0.3 collective-permute-start.5
  452.6 1.8 collective-permute-done.5
  454.4 1.6 maximum_select_fusion.11
  456.0 1.8 collective-permute-start.6
  457.8 45.1 %collective-permute-done.6 = bf16[1024,448]{0,1:T(8,128)(2,1)S(1)} collective-permute-done((bf16[1024,448]{0,1:T(8,128)(2,1)S(1)}, bf16[1024,448]{0,1:T(8,128)(2,1)S(1)}, u32[]{:S(2)}, u32[]{:S(2)}) %collective-permute-start.6) | collective-permute-done | bytes 917536 | tf_op jit(solution)/shard_map/ppermute | solution.py:16
  502.8 2.1 maximum_select_fusion.8
  505.5 50.1 %collective-permute-done.7 = bf16[1024,896]{0,1:T(8,128)(2,1)} collective-permute-done((bf16[1024,896]{0,1:T(8,128)(2,1)}, bf16[1024,896]{0,1:T(8,128)(2,1)}, u32[]{:S(2)}, u32[]{:S(2)}) %collective-permute-start.7) | collective-permute-done | bytes 1835040 | tf_op jit(solution)/shard_map/ppermute | solution.py:16
  555.6 4.5 fusion.16
  560.1 1.0 constant_dynamic-slice_fusion
  561.1 3.4 collective-permute-start.8
  564.6 5.0 copy.29
  569.6 6.3 %gather_fusion.1 = bf16[256,2,1792]{2,1,0:T(2,128)(2,1)S(1)} fusion(bf16[2,448,1792]{2,0,1:T(2,128)(2,1)} %copy.29, s32[1024]{0:T(1024)S(1)} %pad_clamp_fusion), kind=kCustom, calls=%fused_computation.1 | custom fusion | bytes 3671040 | tf_op jit(solution)/shard_map/gather | solution.py:111
  576.0 2.0 fusion.19
  578.0 6.3 %collective-permute-done.8 = bf16[128,1792]{1,0:T(8,128)(2,1)} collective-permute-done((bf16[128,1792]{1,0:T(8,128)(2,1)}, bf16[128,1792]{1,0:T(8,128)(2,1)}, u32[]{:S(2)}, u32[]{:S(2)}) %collective-permute-start.8) | collective-permute-done | bytes 458784 | tf_op jit(solution)/shard_map/ppermute | solution.py:16
  584.3 1.4 fusion.21
  585.7 0.6 copy.30
  586.3 1.3 copy.31
  (37 shorter events, 1.2 us)
Async XLA Ops:
  29.9 7.6 %copy-start.3 = (bf16[224,2048]{1,0:T(8,128)(2,1)S(1)}, bf16[224,2048]{1,0:T(8,128)(2,1)}, u32[]{:S(2)}) copy-start(bf16[224,2048]{1,0:T(8,128)(2,1)} %param.11) | copy-start | bytes 2752516
  29.9 93.2 %all-to-all-start = ((bf16[16,56,1792]{2,1,0:T(8,128)(2,1)}), bf16[16,56,1792]{2,1,0:T(8,128)(2,1)}, u32[]{:S(2)}, u32[]{:S(2)}) async-start(bf16[16,56,1792]{2,1,0:T(8,128)(2,1)} %broadcast_select_fusion), calls=%async_computation | async-start | bytes 6422528 | tf_op jit(solution)/shard_map/all_to_all | solution.py:78
  37.5 2.7 collective-permute-start.1
  42.6 71.9 %collective-permute-start.2 = (bf16[448,2048]{1,0:T(8,128)(2,1)S(1)}, bf16[448,2048]{1,0:T(8,128)(2,1)}, u32[]{:S(2)}, u32[]{:S(2)}) collective-permute-start(bf16[448,2048]{1,0:T(8,128)(2,1)S(1)} %maximum_select_fusion.7), channel_id=1, source_target_pairs={{0,2},{2,0},{1,3},{3,1},{4,6},{6,4},{5,7},{7,5},{8,10},{10,8},{9,1... | collective-permute-start | bytes 5505032 | tf_op jit(solution)/shard_map/ppermute | solution.py:16
  44.4 76.2 %copy-start = (bf16[128,3584]{1,0:T(8,128)(2,1)S(1)}, bf16[128,3584]{1,0:T(8,128)(2,1)}, u32[]{:S(2)}) copy-start(bf16[128,3584]{1,0:T(8,128)(2,1)} %param.8) | copy-start | bytes 2752516
  119.1 91.0 %collective-permute-start.3 = (bf16[896,2048]{1,0:T(8,128)(2,1)}, bf16[896,2048]{1,0:T(8,128)(2,1)}, u32[]{:S(2)}, u32[]{:S(2)}) collective-permute-start(bf16[896,2048]{1,0:T(8,128)(2,1)} %maximum_select_fusion.2), channel_id=1, source_target_pairs={{0,4},{4,0},{1,5},{5,1},{2,6},{6,2},{3,7},{7,3},{8,12},{12,8},{9,1... | collective-permute-start | bytes 11010056 | tf_op jit(solution)/shard_map/ppermute | solution.py:16
  120.6 88.4 %collective-permute-start = (bf16[128,1792]{1,0:T(8,128)(2,1)S(1)}, bf16[128,1792]{1,0:T(8,128)(2,1)S(1)}, u32[]{:S(2)}, u32[]{:S(2)}) collective-permute-start(bf16[128,1792]{1,0:T(8,128)(2,1)S(1)} %get-tuple-element.11), channel_id=1, source_target_pairs={{0,8},{8,0},{1,9},{9,1},{2,10},{10,2},{3,11},{11,3},{4,12},{12,4},... | collective-permute-start | bytes 1376264 | tf_op jit(solution)/shard_map/ppermute | solution.py:16
  222.7 204.8 %collective-permute-start.4 = (bf16[1152,2048]{1,0:T(8,128)(2,1)}, bf16[1152,2048]{1,0:T(8,128)(2,1)}, u32[]{:S(2)}, u32[]{:S(2)}) collective-permute-start(bf16[1152,2048]{1,0:T(8,128)(2,1)} %fusion), channel_id=1, source_target_pairs={{0,8},{8,0},{1,9},{9,1},{2,10},{10,2},{3,11},{11,3},{4,12},{12,4},... | collective-permute-start | bytes 14155784 | tf_op jit(solution)/shard_map/ppermute | solution.py:16
  437.9 4.8 copy-start.6
  442.7 4.8 copy-start.1
  447.5 117.1 %all-to-all-start.1 = ((bf16[16,56,1792]{2,1,0:T(8,128)(2,1)}), bf16[16,56,1792]{2,1,0:T(8,128)(2,1)S(1)}, u32[]{:S(2)}, u32[]{:S(2)}) async-start(bf16[16,56,1792]{2,1,0:T(8,128)(2,1)} %bitcast.46), calls=%async_computation.1 | async-start | bytes 6422528 | tf_op jit(solution)/shard_map/all_to_all | solution.py:94
  452.3 52.7 %copy-start.4 = (s32[128,2]{0,1:T(2,128)S(1)}, s32[128,2]{0,1:T(2,128)}, u32[]{:S(2)}) copy-start(s32[128,2]{0,1:T(2,128)} %param.14) | copy-start | bytes 3076
  452.3 53.2 %copy-start.5 = (f32[128,8]{0,1:T(8,128)S(1)}, f32[128,8]{0,1:T(8,128)}, u32[]{:S(2)}) copy-start(f32[128,8]{0,1:T(8,128)} %param.15) | copy-start | bytes 12292
  452.3 2.1 collective-permute-start.5
  456.0 46.9 %collective-permute-start.6 = (bf16[1024,448]{0,1:T(8,128)(2,1)S(1)}, bf16[1024,448]{0,1:T(8,128)(2,1)S(1)}, u32[]{:S(2)}, u32[]{:S(2)}) collective-permute-start(bf16[1024,448]{0,1:T(8,128)(2,1)S(1)} %maximum_select_fusion.11), channel_id=1, source_target_pairs={{0,2},{2,0},{1,3},{3,1},{4,6},{6,4},{5,7},{7,5},{8,10},{10,8},{9,1... | collective-permute-start | bytes 2752520 | tf_op jit(solution)/shard_map/ppermute | solution.py:16
  505.0 50.6 %collective-permute-start.7 = (bf16[1024,896]{0,1:T(8,128)(2,1)}, bf16[1024,896]{0,1:T(8,128)(2,1)}, u32[]{:S(2)}, u32[]{:S(2)}) collective-permute-start(bf16[1024,896]{0,1:T(8,128)(2,1)} %maximum_select_fusion.8), channel_id=1, source_target_pairs={{0,4},{4,0},{1,5},{5,1},{2,6},{6,2},{3,7},{7,3},{8,12},{12,8},{9,1... | collective-permute-start | bytes 5505032 | tf_op jit(solution)/shard_map/ppermute | solution.py:16
  561.1 23.1 %collective-permute-start.8 = (bf16[128,1792]{1,0:T(8,128)(2,1)}, bf16[128,1792]{1,0:T(8,128)(2,1)}, u32[]{:S(2)}, u32[]{:S(2)}) collective-permute-start(bf16[128,1792]{1,0:T(8,128)(2,1)} %get-tuple-element.9), channel_id=1, source_target_pairs={{0,8},{8,0},{1,9},{9,1},{2,10},{10,2},{3,11},{11,3},{4,12},{12,4},... | collective-permute-start | bytes 1376264 | tf_op jit(solution)/shard_map/ppermute | solution.py:16
  575.9 8.3 %copy-start.2 = (bf16[1,128,1792]{2,1,0:T(8,128)(2,1)S(1)}, bf16[1,128,1792]{2,1,0:T(8,128)(2,1)}, u32[]{:S(2)}) copy-start(bf16[1,128,1792]{2,1,0:T(8,128)(2,1)} %get-tuple-element.10) | copy-start | bytes 1376260
where the time goes:
time: 588 us
  waiting for transfers between devices  453 us (77%)
  local copies, waits for them, and re-layouts  41.2 us (7%)
  other arithmetic  36.8 us (6%)
  matrix products  29.8 us (5%)
  starting transfers between devices  26.2 us (4%)
    ppermute x9, waiting for transfers between devices, from_partner(): return lax.ppermute(block, axis, route)  453 us
    gather x2, local copies, waits for them, and re-layouts, local(): halves[:, slot_token]  22.3 us
    ppermute x9, starting transfers between devices, from_partner(): return lax.ppermute(block, axis, route)  13.8 us
    dot_general x1, matrix products, local(): jnp.dot(routed_in, expert_gate_up, preferred_element_type=jnp.float32)  11.8 us
  transfers between devices with their start and end apart: 11, of which 9 were waited for; matrix products, arithmetic and copies ran while one was open for 7% of the time, Pallas kernels for 0%

commit v1 on v0

v1 whole, which is shorter than its diff:
```python
import functools

import jax
import jax.numpy as jnp
from jax import lax
from jax.experimental import pallas as pl
from jax.experimental.pallas import tpu as pltpu
from jax.sharding import PartitionSpec as P

route_scale = 2.5
meta_lanes = 128
vmem_bytes = 48 * 1024 * 1024
f32 = jnp.float32
bf16 = jnp.bfloat16


def hop(block, mask, axis="expert"):
    count = lax.axis_size(axis)
    return lax.ppermute(block, axis, [(d, d ^ mask) for d in range(count)])


def low_bit(mask):
    return mask & -mask


def ordered(is_upper, own_part, other_part, axis_dim):
    return jnp.where(
        is_upper,
        jnp.concatenate([other_part, own_part], axis_dim),
        jnp.concatenate([own_part, other_part], axis_dim),
    )


def silu(v):
    return v / (1.0 + jnp.exp(-v))


def slots_of(meta, pair, lanes):
    m = meta.astype(f32)
    rows = m.shape[0]
    first = m[:, 0:1] == pair
    second = m[:, 1:2] == pair
    gate = jnp.where(first, m[:, 2:3] + m[:, 3:4], 0.0) + jnp.where(
        second, m[:, 4:5] + m[:, 5:6], 0.0
    )
    hit = jnp.where(first, 1.0, 0.0) + jnp.where(second, 1.0, 0.0)
    before = lax.broadcasted_iota(jnp.int32, (rows, rows), 1) < lax.broadcasted_iota(
        jnp.int32, (rows, rows), 0
    )
    wide_hit = jnp.broadcast_to(hit, (rows, lanes))
    rank = jnp.dot(
        jnp.where(before, 1.0, 0.0).astype(bf16), wide_hit.astype(bf16), preferred_element_type=f32
    )
    slot = lax.broadcasted_iota(jnp.int32, (rows, lanes), 1).astype(f32)
    one_hot = jnp.where(rank == slot, wide_hit, 0.0).astype(bf16)
    return one_hot, gate


def pick_rows(pair_ref, tok_ref, rows_ref):
    width = rows_ref.shape[1]
    pair = pair_ref[0].astype(f32)
    one_hot, _ = slots_of(tok_ref[:, width:], pair, rows_ref.shape[0])
    rows_ref[...] = lax.dot_general(
        one_hot, tok_ref[:, :width], (((0,), (0,)), ((), ())), preferred_element_type=f32
    ).astype(bf16)


def partial_kernel(pair_ref, tok_ref, w_ref, out_ref, rows_ref):
    @pl.when(pl.program_id(0) == 0)
    def _():
        pick_rows(pair_ref, tok_ref, rows_ref)

    out_ref[...] = jnp.dot(rows_ref[...], w_ref[...], preferred_element_type=f32)[
        : out_ref.shape[0]
    ].astype(bf16)


def hidden_kernel(pair_ref, tok_ref, wg_ref, wu_ref, rg_ref, ru_ref, out_ref, rows_ref):
    @pl.when(pl.program_id(0) == 0)
    def _():
        pick_rows(pair_ref, tok_ref, rows_ref)

    cap = out_ref.shape[0]
    rows = rows_ref[...]
    gate = jnp.dot(rows, wg_ref[...], preferred_element_type=f32)[:cap] + rg_ref[...].astype(f32)
    up = jnp.dot(rows, wu_ref[...], preferred_element_type=f32)[:cap] + ru_ref[...].astype(f32)
    out_ref[...] = (silu(gate) * up).astype(bf16)


def down_kernel(pair_ref, meta_ref, hid_ref, w_ref, out_ref, hit_ref, gate_ref, rows_ref):
    @pl.when(pl.program_id(0) == 0)
    def _():
        one_hot, gate = slots_of(meta_ref[...], pair_ref[0].astype(f32), hit_ref.shape[1])
        hit_ref[...] = one_hot
        gate_ref[...] = jnp.broadcast_to(gate, gate_ref.shape)
        rows_ref[...] = jnp.zeros_like(rows_ref)

    cap = hid_ref.shape[0]
    rows_ref[:cap, :] = jnp.dot(hid_ref[...], w_ref[...], preferred_element_type=f32).astype(bf16)
    picked = jnp.dot(hit_ref[...], rows_ref[...], preferred_element_type=f32)
    out_ref[...] = (picked * gate_ref[:, 0:1]).astype(bf16)


def params():
    return pltpu.CompilerParams(
        vmem_limit_bytes=vmem_bytes, dimension_semantics=("arbitrary",)
    )


def smem():
    return pl.BlockSpec(memory_space=pltpu.SMEM)


def whole(array):
    return pl.BlockSpec(array.shape, lambda j: (0, 0))


def cost(m, k, n):
    return pl.CostEstimate(flops=2 * m * k * n, bytes_accessed=2 * k * n, transcendentals=0)


def partial_sums(pair, tok, weights, cap, cap_lanes):
    width, columns = weights.shape
    steps = 4
    return pl.pallas_call(
        partial_kernel,
        grid=(steps,),
        in_specs=[
            smem(),
            whole(tok),
            pl.BlockSpec((width, columns // steps), lambda j: (0, j)),
        ],
        out_specs=pl.BlockSpec((cap, columns // steps), lambda j: (0, j)),
        out_shape=jax.ShapeDtypeStruct((cap, columns), bf16),
        scratch_shapes=[pltpu.VMEM((cap_lanes, width), bf16)],
        compiler_params=params(),
        cost_estimate=cost(cap_lanes, width, columns),
    )(pair, tok, weights)


def hidden_rows(pair, tok, weights, received, cap_lanes):
    width, columns = weights.shape
    units = columns // 2
    cap = received.shape[0]
    steps = 4
    block = units // steps
    return pl.pallas_call(
        hidden_kernel,
        grid=(steps,),
        in_specs=[
            smem(),
            whole(tok),
            pl.BlockSpec((width, block), lambda j: (0, j)),
            pl.BlockSpec((width, block), lambda j: (0, j + steps)),
            pl.BlockSpec((cap, block), lambda j: (0, j)),
            pl.BlockSpec((cap, block), lambda j: (0, j + steps)),
        ],
        out_specs=pl.BlockSpec((cap, block), lambda j: (0, j)),
        out_shape=jax.ShapeDtypeStruct((cap, units), bf16),
        scratch_shapes=[pltpu.VMEM((cap_lanes, width), bf16)],
        compiler_params=params(),
        cost_estimate=cost(cap_lanes, width, columns),
    )(pair, tok, weights, weights, received, received)


def weighted_rows(pair, tok, hidden, weights, cap_lanes):
    units, width = weights.shape
    cap = hidden.shape[0]
    count = tok.shape[0]
    steps = 2
    block = width // steps
    return pl.pallas_call(
        down_kernel,
        grid=(steps,),
        in_specs=[
            smem(),
            pl.BlockSpec((count, meta_lanes), lambda j: (0, width // meta_lanes)),
            whole(hidden),
            pl.BlockSpec((units, block), lambda j: (0, j)),
        ],
        out_specs=pl.BlockSpec((count, block), lambda j: (0, j)),
        out_shape=jax.ShapeDtypeStruct((count, width), bf16),
        scratch_shapes=[
            pltpu.VMEM((count, cap_lanes), bf16),
            pltpu.VMEM((count, meta_lanes), f32),
            pltpu.VMEM((cap_lanes, block), bf16),
        ],
        compiler_params=params(),
        cost_estimate=cost(cap_lanes, units, width),
    )(pair, tok, hidden, weights)


def shared_gate_kernel(parts, spots_ref, own_ref, other_ref, *refs):
    blocks, (mine_ref, theirs_ref, w_ref, sems) = refs[: len(parts)], refs[len(parts) :]
    copies = []
    for block, (row_spot, column_spot) in zip(blocks, parts):
        for i in range(block.shape[0]):
            rows, columns = block.shape[1:]
            row = pl.multiple_of(spots_ref[row_spot + i] * rows, rows)
            column = pl.multiple_of(spots_ref[column_spot] * columns, columns)
            copies.append(
                pltpu.make_async_copy(
                    block.at[i],
                    w_ref.at[pl.ds(row, rows), pl.ds(column, columns)],
                    sems.at[len(copies)],
                )
            )
    for copy in copies:
        copy.start()
    for copy in copies:
        copy.wait()
    width, columns = w_ref.shape
    step = 512

    @pl.loop(0, columns // step)
    def _(j):
        at = pl.ds(pl.multiple_of(j * step, step), step)
        w = w_ref[:, at]
        mine_ref[:, at] = jnp.dot(own_ref[:, :width], w, preferred_element_type=f32).astype(bf16)
        theirs_ref[:, at] = jnp.dot(other_ref[:, :width], w, preferred_element_type=f32)


def shared_partial(spots, own, other, blocks, parts, width, columns):
    rows = own.shape[0]
    vmem = pl.BlockSpec(memory_space=pltpu.VMEM)
    return pl.pallas_call(
        functools.partial(shared_gate_kernel, parts),
        in_specs=[smem(), vmem, vmem] + [pl.BlockSpec(memory_space=pl.ANY)] * len(blocks),
        out_specs=[vmem, vmem],
        out_shape=[
            jax.ShapeDtypeStruct((rows, columns), bf16),
            jax.ShapeDtypeStruct((rows, columns), f32),
        ],
        scratch_shapes=[
            pltpu.VMEM((width, columns), bf16),
            pltpu.SemaphoreType.DMA((sum(b.shape[0] for b in blocks),)),
        ],
        compiler_params=pltpu.CompilerParams(vmem_limit_bytes=vmem_bytes),
        cost_estimate=cost(2 * rows, width, columns),
    )(spots, own, other, *blocks)


def shared_down_kernel(parts, spots_ref, mine_ref, theirs_ref, *refs):
    blocks, (out_ref, d_ref, sems) = refs[: len(parts)], refs[len(parts) :]
    copies = []
    for block, (spot, row_spot) in zip(blocks, parts):
        for i in range(block.shape[0]):
            rows = block.shape[1]
            row = pl.multiple_of(spots_ref[row_spot] * rows, rows)
            copies.append(
                pltpu.make_async_copy(
                    block.at[i],
                    d_ref.at[spots_ref[spot + i], pl.ds(row, rows), :],
                    sems.at[len(copies)],
                )
            )
    for copy in copies:
        copy.start()
    for copy in copies:
        copy.wait()
    count = mine_ref.shape[0]

    @pl.loop(0, d_ref.shape[0])
    def _(i):
        d = d_ref[i]
        out_ref[i, :count, :] = jnp.dot(mine_ref[...], d, preferred_element_type=f32).astype(bf16)
        out_ref[i, count:, :] = jnp.dot(theirs_ref[...], d, preferred_element_type=f32).astype(bf16)


def shared_rows(spots, mine, theirs, blocks, parts, shards):
    rows, units = mine.shape
    columns = blocks[0].shape[2]
    vmem = pl.BlockSpec(memory_space=pltpu.VMEM)
    return pl.pallas_call(
        functools.partial(shared_down_kernel, parts),
        in_specs=[smem(), vmem, vmem] + [pl.BlockSpec(memory_space=pl.ANY)] * len(blocks),
        out_specs=vmem,
        out_shape=jax.ShapeDtypeStruct((shards, 2 * rows, columns), bf16),
        scratch_shapes=[
            pltpu.VMEM((shards, units, columns), bf16),
            pltpu.SemaphoreType.DMA((sum(b.shape[0] for b in blocks),)),
        ],
        compiler_params=pltpu.CompilerParams(vmem_limit_bytes=vmem_bytes),
        cost_estimate=cost(2 * rows, units, shards * columns),
    )(spots, mine, theirs, *blocks)


def gather_blocks(block, hops, groups):
    stack = block[None]
    for bit in hops:
        stack = jnp.concatenate([stack, hop(stack, bit)], 0)
    stacks = [stack]
    bit = 1
    while bit < groups:
        stacks = stacks + [hop(s, bit, "groups") for s in stacks]
        bit *= 2
    return stacks + [hop(s, 1) for s in stacks]


def in_order(blocks, stack_masks, place, group_index):
    chips = len(stack_masks)
    groups = len(blocks) // 2
    stacked = jnp.stack(blocks).reshape((2, groups, chips) + blocks[0].shape[1:])
    spot = [0] * chips
    for i, mask in enumerate(stack_masks):
        spot[mask // 2] = i
    mask = jnp.arange(2 * chips, dtype=jnp.int32) ^ place
    by_core = stacked.transpose(0, 2, 1, 3, 4).reshape((2 * chips, groups) + blocks[0].shape[1:])
    by_shard = by_core[(mask & 1) * chips + jnp.array(spot, jnp.int32)[mask // 2]]
    return by_shard[:, group_index ^ jnp.arange(groups, dtype=jnp.int32)]


def local(
    tokens,
    expert_gate_up,
    expert_down,
    shared_gate_up,
    shared_down,
    host_expert,
    pair_picks,
    affinity,
):
    devices = lax.axis_size("expert")
    groups = lax.axis_size("groups")
    half = devices // 2
    dev_index = lax.axis_index("expert")
    group_index = lax.axis_index("groups")
    place = dev_index % half
    is_upper = dev_index >= half
    pair = jnp.reshape(place, (1,)).astype(jnp.int32)
    tok_rows, full_width = tokens.shape
    width = full_width // 2
    units = expert_down.shape[0]
    pick_count = pair_picks.shape[1]
    capacity = 7 * tok_rows * pick_count // (4 * half)
    cap = -(-2 * capacity // 16) * 16
    cap_lanes = -(-cap // 128) * 128
    chips = list(range(0, half, 2))
    hops = []
    bit = half // 2
    while bit > 1:
        hops.append(bit)
        bit //= 2

    pair_iota = jnp.arange(half, dtype=jnp.int32)
    expert_ids = jnp.sum(
        jnp.where(pair_picks[:, :, None] == pair_iota, host_expert[None, None, :], 0), 2
    )
    scores = jnp.sum(
        jnp.where(expert_ids[:, :, None] == pair_iota, affinity[:, None, :], 0.0), 2
    )
    gates = route_scale * scores / jnp.sum(scores, 1, keepdims=True)
    gates_high = lax.reduce_precision(gates, 8, 7)
    gates_low = gates - gates_high
    meta = jnp.concatenate(
        [
            pair_picks.astype(f32),
            jnp.stack([gates_high, gates_low], 2).reshape(tok_rows, 2 * pick_count),
            jnp.zeros((tok_rows, meta_lanes - 3 * pick_count), f32),
        ],
        1,
    ).astype(bf16)
    low, high = tokens[:, :width], tokens[:, width:]
    mine = jnp.concatenate([jnp.where(is_upper, high, low), meta], 1)
    theirs = jnp.concatenate([jnp.where(is_upper, low, high), meta], 1)

    cross = hop(theirs, half)

    def spread(block):
        got = {0: block}
        for mask in sorted(chips[1:], key=lambda m: (bin(m).count("1"), -m)):
            got[mask] = hop(got[mask ^ low_bit(mask)], low_bit(mask))
        return {m: jnp.concatenate([b, hop(b, 1)], 0) for m, b in got.items()}

    order = sorted(chips[1:], key=lambda m: (bin(m).count("1"), -m)) + [0]
    home = spread(mine)
    sums_out = {m: partial_sums(pair, home[m], expert_gate_up, cap, cap_lanes) for m in order}
    sums_in = {m: hop(sums_out[m], half) for m in order}
    away = spread(cross)
    away_hidden = {
        m: hidden_rows(pair, away[m], expert_gate_up, sums_in[m], cap_lanes) for m in order
    }
    home_hidden = {m: hop(away_hidden[m], half) for m in order}

    gate_columns = shared_gate_up.shape[1] // groups
    down_rows = units // groups
    gate_blocks = gather_blocks(
        lax.dynamic_slice_in_dim(shared_gate_up, group_index * gate_columns, gate_columns, 1),
        hops,
        groups,
    )
    down_blocks = gather_blocks(
        lax.dynamic_slice_in_dim(shared_down, group_index * down_rows, down_rows, 0), hops, groups
    )
    stack_masks = [0]
    for bit in hops:
        stack_masks = stack_masks + [m | bit for m in stack_masks]
    chip_count = len(chips)
    masks = jnp.array(stack_masks, jnp.int32)
    spots = jnp.concatenate(
        [place ^ masks, place ^ 1 ^ masks, group_index ^ jnp.arange(groups, dtype=jnp.int32)]
    ).astype(jnp.int32)
    parts = [(core * chip_count, 2 * chip_count + g) for core in (0, 1) for g in range(groups)]
    by_kernel = shared_gate_up.shape[0] % 16 == 0
    if by_kernel:
        own_sums, other_sums = shared_partial(
            spots, mine, cross, gate_blocks, parts, width, shared_gate_up.shape[1]
        )
    else:
        gate_rows = in_order(gate_blocks, stack_masks, place, group_index)
        gate_rows = gate_rows.transpose(0, 2, 1, 3).reshape(width, 2 * units)
        own_sums = jnp.dot(mine[:, :width], gate_rows, preferred_element_type=f32).astype(bf16)
        other_sums = jnp.dot(cross[:, :width], gate_rows, preferred_element_type=f32)
    total = other_sums + hop(own_sums, half).astype(f32)
    other_hidden = (silu(total[:, :units]) * total[:, units:]).astype(bf16)
    own_hidden = hop(other_hidden, half)
    if by_kernel:
        shared_out = shared_rows(spots, own_hidden, other_hidden, down_blocks, parts, half)
        shared_out = shared_out.transpose(1, 0, 2).reshape(2 * tok_rows, width).astype(f32)
    else:
        down_columns = in_order(down_blocks, stack_masks, place, group_index)
        down_columns = down_columns.transpose(1, 2, 0, 3).reshape(units, width)
        both = jnp.concatenate([own_hidden, other_hidden], 0)
        shared_out = jnp.dot(both, down_columns, preferred_element_type=f32)
        shared_out = shared_out.astype(bf16).astype(f32)

    def collect(tok, hidden):
        total = {}
        for m in order:
            rows = weighted_rows(pair, tok[m], hidden[m], expert_down, cap_lanes)
            total[m] = rows[:tok_rows].astype(f32) + hop(rows[tok_rows:], 1).astype(f32)
        for bit in hops[::-1]:
            for m in [m for m in order if m in total and low_bit(m) == bit]:
                sent = hop(total.pop(m).astype(bf16), bit)
                total[m ^ bit] = total[m ^ bit] + sent.astype(f32)
        return total[0]

    away_rows = (collect(away, away_hidden) + shared_out[tok_rows:]).astype(bf16)
    far_half = hop(away_rows, half)
    near_half = (collect(home, home_hidden) + shared_out[:tok_rows]).astype(bf16)
    return ordered(is_upper, near_half, far_half, 1)


def solution(mesh):
    in_specs = (
        P(("groups", "expert"), None),
        P("expert", None),
        P(None, "expert"),
        P("expert", None),
        P(None, "expert"),
        P(),
        P(("groups", "expert"), None),
        P(("groups", "expert"), None),
    )
    out_specs = P(("groups", "expert"), None)
    return jax.shard_map(local, mesh=mesh, in_specs=in_specs, out_specs=out_specs, check_vma=False)
```

time: 588 us -> 340 us (0.58)
  waiting for transfers between devices: 453 us -> 173 us
  Pallas kernels: 0 us -> 74.7 us
  matrix products: 29.8 us -> 0 us
  other arithmetic: 36.8 us -> 20 us
  starting transfers between devices: 26.2 us -> 36.3 us
  local copies, waits for them, and re-layouts: 41.2 us -> 33.7 us
    ppermute x9 -> x50, waiting for transfers between devices: 453 us -> 173 us  [hop(): return lax.ppermute(block, axis, [(d, d ^ mask) for d in range(count)])]
    pallas_call x0 -> x18, Pallas kernels: none -> 74.7 us  [the longest x4 22.4 us: hidden_rows(): pl.pallas_call(hidden_kernel, grid=(steps,), in_specs=[smem(), whole(tok)...]
    dot_general x5 -> x0, matrix products: 29.8 us -> none  [the longest x1 11.8 us: local(): jnp.dot(routed_in, expert_gate_up, preferred_element_type=jnp.float32)]
    gather x3 -> x0, local copies, waits for them, and re-layouts: 28.6 us -> none  [the longest x2 22.3 us: local(): halves[:, slot_token]]
    ppermute x9 -> x50, starting transfers between devices: 13.8 us -> 36.3 us  [hop(): return lax.ppermute(block, axis, [(d, d ^ mask) for d in range(count)])]
    all_to_all x2 -> x0, starting transfers between devices: 12.4 us -> none  [the longest x1 7.59 us: local(): lax.all_to_all(outgoing, 'expert', split_axis=0, concat_axis=0, tiled=True)]
    unnamed x15 -> x81, local copies, waits for them, and re-layouts: 0.98 us -> 11.9 us
    add x1, other arithmetic: 10.3 us -> 0.1 us  [local(): total = other_sums + hop(own_sums, half).astype(f32)]
  transfers between devices with their start and end apart: 11 -> 50, of which waited for: 9 -> 16; matrix products, arithmetic and copies ran while one was open for 7% -> 13% of each run, Pallas kernels for 0% -> 22%
where the time goes in v1:
time: 340 us; the launch traced here: 338 us
  waiting for transfers between devices  173 us (51%)
  Pallas kernels  74.7 us (22%)
  starting transfers between devices  36.3 us (11%)
  local copies, waits for them, and re-layouts  33.7 us (10%)
  other arithmetic  20 us (6%)
    ppermute x50, waiting for transfers between devices, hop(): return lax.ppermute(block, axis, [(d, d ^ mask) for d in range(count)])  173 us
    ppermute x50, starting transfers between devices, hop(): return lax.ppermute(block, axis, [(d, d ^ mask) for d in range(count)])  36.3 us
    pallas_call x4, Pallas kernels, hidden_rows(): pl.pallas_call(hidden_kernel, grid=(steps,), in_specs=[smem(), whole(tok)...  22.4 us
    pallas_call x4, Pallas kernels, partial_sums(): pl.pallas_call(partial_kernel, grid=(steps,), in_specs=[smem(), whole(tok...  21.7 us
    pallas_call x8, Pallas kernels, weighted_rows(): pl.pallas_call(down_kernel, grid=(steps,), in_specs=[smem(), pl.BlockSpec...  20.1 us
    unnamed x81, local copies, waits for them, and re-layouts  11.9 us
    pallas_call x1, Pallas kernels, shared_partial(): pl.pallas_call(functools.partial(shared_gate_kernel, parts), in_specs=[sm...  6.94 us
  transfers between devices with their start and end apart: 50, of which 16 were waited for; matrix products, arithmetic and copies ran while one was open for 13% of the time, Pallas kernels for 22%

profile of v1, /device:TPU:0, one launch (start us, length us, event | category | flops | bytes accessed | tf_op | source)
XLA Modules:
  0.0 338.4 jit_solution(8830644230207528373)
XLA Ops:
  3.9 3.1 collective-permute-start.14
  12.1 21.6 %collective-permute-done.33 = bf16[1,512,224]{2,1,0:T(8,128)(2,1)S(1)} collective-permute-done((bf16[1,512,224]{2,1,0:T(8,128)(2,1)S(1)}, bf16[1,512,224]{2,1,0:T(8,128)(2,1)S(1)}, u32[]{:S(2)}, u32[]{:S(2)}) %collective-permute-start.33) | collective-permute-done | bytes 229408 | tf_op jit(solution)/shard_map/ppermute | solution.py:19
  33.7 2.8 collective-permute-start
  40.9 6.0 %shard_map.91 = bf16[112,2048]{1,0:T(8,128)(2,1)} custom-call(s32[1]{0:T(128)} %bitcast.pair_ref, bf16[256,1920]{1,0:T(8,128)(2,1)S(1)} %pad_maximum_fusion.2.tok_ref.meta_ref, bf16[1792,2048]{1,0:T(8,128)(2,1)} %wu_ref.7), custom_call_target="tpu_custom_call" | custom-call | flops 939524096 | bytes 7340032 | tf_op jit(solution)/shard_map/pallas_call | solution.py:125
  47.0 1.9 constant_dynamic-update-slice_fusion.9
  52.4 16.1 %collective-permute-done.other_ref = bf16[128,1920]{1,0:T(8,128)(2,1)} collective-permute-done((bf16[128,1920]{1,0:T(8,128)(2,1)S(1)}, bf16[128,1920]{1,0:T(8,128)(2,1)}, u32[]{:S(2)}, u32[]{:S(2)}) %collective-permute-start) | collective-permute-done | bytes 491552 | tf_op jit(solution)/shard_map/ppermute | solution.py:19
  68.5 1.9 constant_dynamic-update-slice_fusion.1
  72.4 7.1 %collective-permute-done.20 = bf16[128,1920]{1,0:T(8,128)(2,1)} collective-permute-done((bf16[128,1920]{1,0:T(8,128)(2,1)}, bf16[128,1920]{1,0:T(8,128)(2,1)}, u32[]{:S(2)}, u32[]{:S(2)}) %collective-permute-start.20) | collective-permute-done | bytes 491552 | tf_op jit(solution)/shard_map/ppermute | solution.py:19
  83.7 1.9 constant_dynamic-update-slice_fusion.4.tok_ref.meta_ref
  87.8 5.2 %shard_map.94 = bf16[112,2048]{1,0:T(8,128)(2,1)S(1)} custom-call(s32[1]{0:T(128)} %bitcast.pair_ref, bf16[256,1920]{1,0:T(8,128)(2,1)S(1)} %copy-done.10, bf16[1792,2048]{1,0:T(8,128)(2,1)} %wu_ref.7), custom_call_target="tpu_custom_call" | custom-call | flops 939524096 | bytes 7340032 | tf_op jit(solution)/shard_map/pallas_call | solution.py:125
  93.5 5.3 %shard_map.92.hid_ref = bf16[112,1024]{1,0:T(8,128)(2,1)S(1)} custom-call(s32[1]{0:T(128)} %bitcast.pair_ref, bf16[256,1920]{1,0:T(8,128)(2,1)S(1)} %constant_dynamic-update-slice_fusion.tok_ref.meta_ref, bf16[1792,2048]{1,0:T(8,128)(2,1)} %wu_ref.7, bf16[1792,2048]{1,0:T(8,128)(2,1)} %wu_ref.7, bf16[112,2048]{1,0:T(8,128)(2,1)} %collective-permute-done.3.rg_ref.ru_ref, ...), custom_call_target="tpu_custom_call" | custom-call | flops 939524096 | bytes 7340032 | tf_op jit(solution)/shard_map/pallas_call | solution.py:147
  98.8 2.6 collective-permute-start.39
  101.6 2.7 pad_maximum_fusion.refs_0_
  106.2 2.1 shard_map.93
  109.2 5.2 %shard_map.97 = bf16[112,2048]{1,0:T(8,128)(2,1)S(1)} custom-call(s32[1]{0:T(128)} %bitcast.pair_ref, bf16[256,1920]{1,0:T(8,128)(2,1)S(1)} %constant_dynamic-update-slice_fusion.8.tok_ref.meta_ref, bf16[1792,2048]{1,0:T(8,128)(2,1)} %wu_ref.7), custom_call_target="tpu_custom_call" | custom-call | flops 939524096 | bytes 7340032 | tf_op jit(solution)/shard_map/pallas_call | solution.py:125
  114.5 12.1 %collective-permute-done.39.hid_ref = bf16[112,1024]{1,0:T(8,128)(2,1)S(1)} collective-permute-done((bf16[112,1024]{1,0:T(8,128)(2,1)S(1)}, bf16[112,1024]{1,0:T(8,128)(2,1)S(1)}, u32[]{:S(2)}, u32[]{:S(2)}) %collective-permute-start.39) | collective-permute-done | bytes 229408 | tf_op jit(solution)/shard_map/ppermute | solution.py:19
  128.0 2.1 shard_map.105
  131.6 5.9 %shard_map.95.hid_ref = bf16[112,1024]{1,0:T(8,128)(2,1)} custom-call(s32[1]{0:T(128)} %bitcast.pair_ref, bf16[256,1920]{1,0:T(8,128)(2,1)S(1)} %constant_dynamic-update-slice_fusion.2.tok_ref.meta_ref, bf16[1792,2048]{1,0:T(8,128)(2,1)} %wu_ref.7, bf16[1792,2048]{1,0:T(8,128)(2,1)} %wu_ref.7, bf16[112,2048]{1,0:T(8,128)(2,1)S(1)} %collective-permute-done.9.rg_ref.ru_ref, ...), custom_call_target="tpu_custom_call" | custom-call | flops 939524096 | bytes 7340032 | tf_op jit(solution)/shard_map/pallas_call | solution.py:147
  138.3 2.9 shard_map.96
  142.0 16.5 %collective-permute-done.16.rg_ref.ru_ref = bf16[112,2048]{1,0:T(8,128)(2,1)S(1)} collective-permute-done((bf16[112,2048]{1,0:T(8,128)(2,1)S(1)}, bf16[112,2048]{1,0:T(8,128)(2,1)S(1)}, u32[]{:S(2)}, u32[]{:S(2)}) %collective-permute-start.16) | collective-permute-done | bytes 458784 | tf_op jit(solution)/shard_map/ppermute | solution.py:19
  158.5 5.9 %shard_map.98.hid_ref = bf16[112,1024]{1,0:T(8,128)(2,1)} custom-call(s32[1]{0:T(128)} %bitcast.pair_ref, bf16[256,1920]{1,0:T(8,128)(2,1)S(1)} %constant_dynamic-update-slice_fusion.6.tok_ref.meta_ref, bf16[1792,2048]{1,0:T(8,128)(2,1)} %wu_ref.7, bf16[1792,2048]{1,0:T(8,128)(2,1)} %wu_ref.7, bf16[112,2048]{1,0:T(8,128)(2,1)S(1)} %collective-permute-done.16.rg_ref.ru_ref, ...), custom_call_target="tpu_custom_call" | custom-call | flops 939524096 | bytes 7340032 | tf_op jit(solution)/shard_map/pallas_call | solution.py:147
  164.4 2.9 shard_map.99
  168.2 5.4 %shard_map.100 = bf16[112,2048]{1,0:T(8,128)(2,1)S(1)} custom-call(s32[1]{0:T(128)} %bitcast.pair_ref, bf16[256,1920]{1,0:T(8,128)(2,1)S(1)} %constant_dynamic-update-slice_fusion.12.tok_ref.meta_ref, bf16[1792,2048]{1,0:T(8,128)(2,1)} %wu_ref.7), custom_call_target="tpu_custom_call" | custom-call | flops 939524096 | bytes 7340032 | tf_op jit(solution)/shard_map/pallas_call | solution.py:125
  173.7 2.9 collective-permute-start.41
  177.4 2.4 copy.50.refs_1_
  179.8 2.3 copy.51.refs_2_
  182.1 10.7 %collective-permute-done.44.hid_ref = bf16[112,1024]{1,0:T(8,128)(2,1)} collective-permute-done((bf16[112,1024]{1,0:T(8,128)(2,1)}, bf16[112,1024]{1,0:T(8,128)(2,1)}, u32[]{:S(2)}, u32[]{:S(2)}) %collective-permute-start.44) | collective-permute-done | bytes 229408 | tf_op jit(solution)/shard_map/ppermute | solution.py:19
  192.8 2.0 copy-done.3
  194.8 3.0 shard_map.107
  197.8 9.7 %collective-permute-done.41.hid_ref = bf16[112,1024]{1,0:T(8,128)(2,1)} collective-permute-done((bf16[112,1024]{1,0:T(8,128)(2,1)}, bf16[112,1024]{1,0:T(8,128)(2,1)}, u32[]{:S(2)}, u32[]{:S(2)}) %collective-permute-start.41) | collective-permute-done | bytes 229408 | tf_op jit(solution)/shard_map/ppermute | solution.py:19
  207.5 3.0 shard_map.106
  212.0 1.9 add_convert_fusion.7
  214.4 2.8 collective-permute-done.22.rg_ref.ru_ref
  217.2 5.4 %shard_map.101.hid_ref = bf16[112,1024]{1,0:T(8,128)(2,1)S(1)} custom-call(s32[1]{0:T(128)} %bitcast.pair_ref, bf16[256,1920]{1,0:T(8,128)(2,1)S(1)} %constant_dynamic-update-slice_fusion.10.tok_ref.meta_ref, bf16[1792,2048]{1,0:T(8,128)(2,1)} %wu_ref.7, bf16[1792,2048]{1,0:T(8,128)(2,1)} %wu_ref.7, ...), custom_call_target="tpu_custom_call" | custom-call | flops 939524096 | bytes 7340032 | tf_op jit(solution)/shard_map/pallas_call | solution.py:147
  222.7 2.1 shard_map.102
  225.9 8.7 %collective-permute-done.46.hid_ref = bf16[112,1024]{1,0:T(8,128)(2,1)S(1)} collective-permute-done((bf16[112,1024]{1,0:T(8,128)(2,1)S(1)}, bf16[112,1024]{1,0:T(8,128)(2,1)S(1)}, u32[]{:S(2)}, u32[]{:S(2)}) %collective-permute-start.46) | collective-permute-done | bytes 229408 | tf_op jit(solution)/shard_map/ppermute | solution.py:19
  234.6 2.1 shard_map.108
  242.5 6.9 %shard_map.103 = (bf16[128,2048]{1,0:T(8,128)(2,1)S(1)}, f32[128,2048]{1,0:T(8,128)S(1)}) custom-call(s32[10]{0:T(128)S(1)} %pad_add_fusion.spots_ref, bf16[128,1920]{1,0:T(8,128)(2,1)S(1)} %concatenate.59.own_ref, bf16[128,1920]{1,0:T(8,128)(2,1)} %collective-permute-done.other_ref, bf16[4,224,1024]{2,1,0:T(8,128)(2,1)} %pad_maximum_fusion.refs_0_, ...), custom_call_target="tpu_custom_call" | custom-call | flops 1879048192 | bytes 7340032 | tf_op jit(solution)/shard_map/pallas_call | solution.py:226
  250.8 3.9 %collective-permute-done.24 = bf16[128,1792]{1,0:T(8,128)(2,1)S(1)} collective-permute-done((bf16[128,1792]{1,0:T(8,128)(2,1)}, bf16[128,1792]{1,0:T(8,128)(2,1)S(1)}, u32[]{:S(2)}, u32[]{:S(2)}) %collective-permute-start.24) | collective-permute-done | bytes 458784 | tf_op jit(solution)/shard_map/ppermute | solution.py:19
  256.2 19.3 %collective-permute-done.31 = bf16[128,2048]{1,0:T(8,128)(2,1)S(1)} collective-permute-done((bf16[128,2048]{1,0:T(8,128)(2,1)S(1)}, bf16[128,2048]{1,0:T(8,128)(2,1)S(1)}, u32[]{:S(2)}, u32[]{:S(2)}) %collective-permute-start.31) | collective-permute-done | bytes 524320 | tf_op jit(solution)/shard_map/ppermute | solution.py:19
  277.9 11.0 %collective-permute-done.48 = bf16[128,1792]{1,0:T(8,128)(2,1)S(1)} collective-permute-done((bf16[128,1792]{1,0:T(8,128)(2,1)S(1)}, bf16[128,1792]{1,0:T(8,128)(2,1)S(1)}, u32[]{:S(2)}, u32[]{:S(2)}) %collective-permute-start.48) | collective-permute-done | bytes 458784 | tf_op jit(solution)/shard_map/ppermute | solution.py:19
  289.8 10.6 %collective-permute-done.32.mine_ref = bf16[128,1024]{1,0:T(8,128)(2,1)S(1)} collective-permute-done((bf16[128,1024]{1,0:T(8,128)(2,1)S(1)}, bf16[128,1024]{1,0:T(8,128)(2,1)S(1)}, u32[]{:S(2)}, u32[]{:S(2)}) %collective-permute-start.32) | collective-permute-done | bytes 262176 | tf_op jit(solution)/shard_map/ppermute | solution.py:19
  300.4 3.5 %shard_map.104 = bf16[8,256,224]{2,1,0:T(8,128)(2,1)S(1)} custom-call(s32[10]{0:T(128)S(1)} %pad_add_fusion.spots_ref, bf16[128,1024]{1,0:T(8,128)(2,1)S(1)} %collective-permute-done.32.mine_ref, bf16[128,1024]{1,0:T(8,128)(2,1)S(1)} %fusion.theirs_ref, bf16[4,512,224]{2,1,0:T(8,128)(2,1)S(1)} %pad_maximum_fusion.1.refs_0_, ...), custom_call_target="tpu_custom_call" | custom-call | flops 939524096 | bytes 3670016 | tf_op jit(solution)/shard_map/pallas_call | solution.py:274
  305.5 2.4 copy.56
  308.6 2.1 collective-permute-start.49
  310.7 3.4 collective-permute-done.25
  316.5 12.7 %collective-permute-done.49 = bf16[128,1792]{1,0:T(8,128)(2,1)S(1)} collective-permute-done((bf16[128,1792]{1,0:T(8,128)(2,1)}, bf16[128,1792]{1,0:T(8,128)(2,1)S(1)}, u32[]{:S(2)}, u32[]{:S(2)}) %collective-permute-start.49) | collective-permute-done | bytes 458784 | tf_op jit(solution)/shard_map/ppermute | solution.py:19
  330.5 6.7 %collective-permute-done.38 = bf16[128,1792]{1,0:T(8,128)(2,1)S(1)} collective-permute-done((bf16[128,1792]{1,0:T(8,128)(2,1)S(1)}, bf16[128,1792]{1,0:T(8,128)(2,1)S(1)}, u32[]{:S(2)}, u32[]{:S(2)}) %collective-permute-start.38) | collective-permute-done | bytes 458784 | tf_op jit(solution)/shard_map/ppermute | solution.py:19
  (210 shorter events, 57.3 us)
Async XLA Ops:
  3.9 42.9 %collective-permute-start.14 = (bf16[128,1920]{1,0:T(8,128)(2,1)S(1)}, bf16[128,1920]{1,0:T(8,128)(2,1)}, u32[]{:S(2)}, u32[]{:S(2)}) collective-permute-start(bf16[128,1920]{1,0:T(8,128)(2,1)S(1)} %concatenate.59.own_ref), channel_id=1, source_target_pairs={{0,4},{1,5},{2,6},{3,7},{4,0},{5,1},{6,2},{7,3},{8,12},{9,13},{10,... | collective-permute-start | bytes 1474568 | tf_op jit(solution)/shard_map/ppermute | solution.py:19
  7.0 41.8 %collective-permute-start.7 = (bf16[128,1920]{1,0:T(8,128)(2,1)S(1)}, bf16[128,1920]{1,0:T(8,128)(2,1)}, u32[]{:S(2)}, u32[]{:S(2)}) collective-permute-start(bf16[128,1920]{1,0:T(8,128)(2,1)S(1)} %concatenate.59.own_ref), channel_id=1, source_target_pairs={{0,2},{1,3},{2,0},{3,1},{4,6},{5,7},{6,4},{7,5},{8,10},{9,11},{10,... | collective-permute-start | bytes 1474568 | tf_op jit(solution)/shard_map/ppermute | solution.py:19
  8.5 30.6 %collective-permute-start.2 = (bf16[128,1920]{1,0:T(8,128)(2,1)S(1)}, bf16[128,1920]{1,0:T(8,128)(2,1)}, u32[]{:S(2)}, u32[]{:S(2)}) collective-permute-start(bf16[128,1920]{1,0:T(8,128)(2,1)S(1)} %concatenate.59.own_ref), channel_id=1, source_target_pairs={{0,1},{1,0},{2,3},{3,2},{4,5},{5,4},{6,7},{7,6},{8,9},{9,8},{10,11... | collective-permute-start | bytes 1474568 | tf_op jit(solution)/shard_map/ppermute | solution.py:19
  8.6 28.0 %collective-permute-start.26 = (bf16[1,224,1024]{2,1,0:T(8,128)(2,1)S(1)}, bf16[1,224,1024]{2,1,0:T(8,128)(2,1)S(1)}, u32[]{:S(2)}, u32[]{:S(2)}) collective-permute-start(bf16[1,224,1024]{2,1,0:T(8,128)(2,1)S(1)} %dynamic-slice_bitcast_fusion), channel_id=1, source_target_pairs={{0,4},{1,5},{2,6},{3,7},{4,0},{5,1},{6,2},{7,3},{8,12},{9,13},{10,... | collective-permute-start | bytes 1376264 | tf_op jit(solution)/shard_map/ppermute | solution.py:19
  10.2 23.5 %collective-permute-start.33 = (bf16[1,512,224]{2,1,0:T(8,128)(2,1)S(1)}, bf16[1,512,224]{2,1,0:T(8,128)(2,1)S(1)}, u32[]{:S(2)}, u32[]{:S(2)}) collective-permute-start(bf16[1,512,224]{2,1,0:T(8,128)(2,1)S(1)} %bitcast.17), channel_id=1, source_target_pairs={{0,4},{1,5},{2,6},{3,7},{4,0},{5,1},{6,2},{7,3},{8,12},{9,13},{10,... | collective-permute-start | bytes 688136 | tf_op jit(solution)/shard_map/ppermute | solution.py:19
  33.7 34.8 %collective-permute-start = (bf16[128,1920]{1,0:T(8,128)(2,1)S(1)}, bf16[128,1920]{1,0:T(8,128)(2,1)}, u32[]{:S(2)}, u32[]{:S(2)}) collective-permute-start(bf16[128,1920]{1,0:T(8,128)(2,1)S(1)} %concatenate.57), channel_id=1, source_target_pairs={{0,8},{1,9},{2,10},{3,11},{4,12},{5,13},{6,14},{7,15},{8,0},{9,1},... | collective-permute-start | bytes 1474568 | tf_op jit(solution)/shard_map/ppermute | solution.py:19
  36.6 33.8 %collective-permute-start.34 = (bf16[2,512,224]{2,1,0:T(8,128)(2,1)S(1)}, bf16[2,512,224]{2,1,0:T(8,128)(2,1)S(1)}, u32[]{:S(2)}, u32[]{:S(2)}) collective-permute-start(bf16[2,512,224]{2,1,0:T(8,128)(2,1)S(1)} %pad_maximum_fusion.4), channel_id=1, source_target_pairs={{0,2},{1,3},{2,0},{3,1},{4,6},{5,7},{6,4},{7,5},{8,10},{9,11},{10,... | collective-permute-start | bytes 1376264 | tf_op jit(solution)/shard_map/ppermute | solution.py:19
  39.2 62.3 %collective-permute-start.27 = (bf16[2,224,1024]{2,1,0:T(8,128)(2,1)}, bf16[2,224,1024]{2,1,0:T(8,128)(2,1)}, u32[]{:S(2)}, u32[]{:S(2)}) collective-permute-start(bf16[2,224,1024]{2,1,0:T(8,128)(2,1)} %pad_maximum_fusion.3), channel_id=1, source_target_pairs={{0,2},{1,3},{2,0},{3,1},{4,6},{5,7},{6,4},{7,5},{8,10},{9,11},{10,... | collective-permute-start | bytes 2752520 | tf_op jit(solution)/shard_map/ppermute | solution.py:19
  46.8 46.3 %collective-permute-start.3 = (bf16[112,2048]{1,0:T(8,128)(2,1)}, bf16[112,2048]{1,0:T(8,128)(2,1)}, u32[]{:S(2)}, u32[]{:S(2)}) collective-permute-start(bf16[112,2048]{1,0:T(8,128)(2,1)} %shard_map.91), channel_id=1, source_target_pairs={{0,8},{1,9},{2,10},{3,11},{4,12},{5,13},{6,14},{7,15},{8,0},{9,1},... | collective-permute-start | bytes 1376264 | tf_op jit(solution)/shard_map/ppermute | solution.py:19
  48.8 30.6 %collective-permute-start.20 = (bf16[128,1920]{1,0:T(8,128)(2,1)}, bf16[128,1920]{1,0:T(8,128)(2,1)}, u32[]{:S(2)}, u32[]{:S(2)}) collective-permute-start(bf16[128,1920]{1,0:T(8,128)(2,1)} %collective-permute-done.14), channel_id=1, source_target_pairs={{0,2},{1,3},{2,0},{3,1},{4,6},{5,7},{6,4},{7,5},{8,10},{9,11},{10,... | collective-permute-start | bytes 1474568 | tf_op jit(solution)/shard_map/ppermute | solution.py:19
  68.5 13.6 %collective-permute-start.8 = (bf16[128,1920]{1,0:T(8,128)(2,1)}, bf16[128,1920]{1,0:T(8,128)(2,1)}, u32[]{:S(2)}, u32[]{:S(2)}) collective-permute-start(bf16[128,1920]{1,0:T(8,128)(2,1)} %collective-permute-done.7), channel_id=1, source_target_pairs={{0,1},{1,0},{2,3},{3,2},{4,5},{5,4},{6,7},{7,6},{8,9},{9,8},{10,11... | collective-permute-start | bytes 1474568 | tf_op jit(solution)/shard_map/ppermute | solution.py:19
  70.4 15.2 %collective-permute-start.1 = (bf16[128,1920]{1,0:T(8,128)(2,1)}, bf16[128,1920]{1,0:T(8,128)(2,1)}, u32[]{:S(2)}, u32[]{:S(2)}) collective-permute-start(bf16[128,1920]{1,0:T(8,128)(2,1)} %collective-permute-done.other_ref), channel_id=1, source_target_pairs={{0,1},{1,0},{2,3},{3,2},{4,5},{5,4},{6,7},{7,6},{8,9},{9,8},{10,11... | collective-permute-start | bytes 1474568 | tf_op jit(solution)/shard_map/ppermute | solution.py:19
  79.5 24.9 %collective-permute-start.12 = (bf16[128,1920]{1,0:T(8,128)(2,1)}, bf16[128,1920]{1,0:T(8,128)(2,1)S(1)}, u32[]{:S(2)}, u32[]{:S(2)}) collective-permute-start(bf16[128,1920]{1,0:T(8,128)(2,1)} %collective-permute-done.other_ref), channel_id=1, source_target_pairs={{0,4},{1,5},{2,6},{3,7},{4,0},{5,1},{6,2},{7,3},{8,12},{9,13},{10,... | collective-permute-start | bytes 1474568 | tf_op jit(solution)/shard_map/ppermute | solution.py:19
  82.1 16.7 %collective-permute-start.5 = (bf16[128,1920]{1,0:T(8,128)(2,1)}, bf16[128,1920]{1,0:T(8,128)(2,1)S(1)}, u32[]{:S(2)}, u32[]{:S(2)}) collective-permute-start(bf16[128,1920]{1,0:T(8,128)(2,1)} %collective-permute-done.other_ref), channel_id=1, source_target_pairs={{0,2},{1,3},{2,0},{3,1},{4,6},{5,7},{6,4},{7,5},{8,10},{9,11},{10,... | collective-permute-start | bytes 1474568 | tf_op jit(solution)/shard_map/ppermute | solution.py:19
  85.6 20.3 %collective-permute-start.15 = (bf16[128,1920]{1,0:T(8,128)(2,1)}, bf16[128,1920]{1,0:T(8,128)(2,1)S(1)}, u32[]{:S(2)}, u32[]{:S(2)}) collective-permute-start(bf16[128,1920]{1,0:T(8,128)(2,1)} %collective-permute-done.14), channel_id=1, source_target_pairs={{0,1},{1,0},{2,3},{3,2},{4,5},{5,4},{6,7},{7,6},{8,9},{9,8},{10,11... | collective-permute-start | bytes 1474568 | tf_op jit(solution)/shard_map/ppermute | solution.py:19
  93.1 38.0 %collective-permute-start.9 = (bf16[112,2048]{1,0:T(8,128)(2,1)S(1)}, bf16[112,2048]{1,0:T(8,128)(2,1)S(1)}, u32[]{:S(2)}, u32[]{:S(2)}) collective-permute-start(bf16[112,2048]{1,0:T(8,128)(2,1)S(1)} %shard_map.94), channel_id=1, source_target_pairs={{0,8},{1,9},{2,10},{3,11},{4,12},{5,13},{6,14},{7,15},{8,0},{9,1},... | collective-permute-start | bytes 1376264 | tf_op jit(solution)/shard_map/ppermute | solution.py:19
  98.8 27.7 %collective-permute-start.39 = (bf16[112,1024]{1,0:T(8,128)(2,1)S(1)}, bf16[112,1024]{1,0:T(8,128)(2,1)S(1)}, u32[]{:S(2)}, u32[]{:S(2)}) collective-permute-start(bf16[112,1024]{1,0:T(8,128)(2,1)S(1)} %shard_map.92.hid_ref), channel_id=1, source_target_pairs={{0,8},{1,9},{2,10},{3,11},{4,12},{5,13},{6,14},{7,15},{8,0},{9,1},... | collective-permute-start | bytes 688136 | tf_op jit(solution)/shard_map/ppermute | solution.py:19
  101.5 29.5 %collective-permute-start.6 = (bf16[128,1920]{1,0:T(8,128)(2,1)S(1)}, bf16[128,1920]{1,0:T(8,128)(2,1)S(1)}, u32[]{:S(2)}, u32[]{:S(2)}) collective-permute-start(bf16[128,1920]{1,0:T(8,128)(2,1)S(1)} %collective-permute-done.5), channel_id=1, source_target_pairs={{0,1},{1,0},{2,3},{3,2},{4,5},{5,4},{6,7},{7,6},{8,9},{9,8},{10,11... | collective-permute-start | bytes 1474568 | tf_op jit(solution)/shard_map/ppermute | solution.py:19
  104.4 107.6 %collective-permute-start.28 = (bf16[4,224,1024]{2,1,0:T(8,128)(2,1)}, bf16[4,224,1024]{2,1,0:T(8,128)(2,1)}, u32[]{:S(2)}, u32[]{:S(2)}) collective-permute-start(bf16[4,224,1024]{2,1,0:T(8,128)(2,1)} %pad_maximum_fusion.refs_0_), channel_id=1, source_target_pairs={{0,16},{16,0},{1,17},{17,1},{2,18},{18,2},{3,19},{19,3},{4,20},{20... | collective-permute-start | bytes 5505032 | tf_op jit(solution)/shard_map/ppermute | solution.py:19
  105.9 31.6 %collective-permute-start.21 = (bf16[128,1920]{1,0:T(8,128)(2,1)}, bf16[128,1920]{1,0:T(8,128)(2,1)S(1)}, u32[]{:S(2)}, u32[]{:S(2)}) collective-permute-start(bf16[128,1920]{1,0:T(8,128)(2,1)} %collective-permute-done.20), channel_id=1, source_target_pairs={{0,1},{1,0},{2,3},{3,2},{4,5},{5,4},{6,7},{7,6},{8,9},{9,8},{10,11... | collective-permute-start | bytes 1474568 | tf_op jit(solution)/shard_map/ppermute | solution.py:19
  126.5 47.2 %collective-permute-start.35 = (bf16[4,512,224]{1,2,0:T(8,128)(2,1)}, bf16[4,512,224]{1,2,0:T(8,128)(2,1)}, u32[]{:S(2)}, u32[]{:S(2)}) collective-permute-start(bf16[4,512,224]{1,2,0:T(8,128)(2,1)} %copy.48), channel_id=1, source_target_pairs={{0,16},{16,0},{1,17},{17,1},{2,18},{18,2},{3,19},{19,3},{4,20},{20... | collective-permute-start | bytes 2752520 | tf_op jit(solution)/shard_map/ppermute | solution.py:19
  131.1 48.8 %collective-permute-start.36 = (bf16[4,512,224]{1,2,0:T(8,128)(2,1)}, bf16[4,512,224]{1,2,0:T(8,128)(2,1)}, u32[]{:S(2)}, u32[]{:S(2)}) collective-permute-start(bf16[4,512,224]{1,2,0:T(8,128)(2,1)} %copy.48), channel_id=1, source_target_pairs={{0,1},{1,0},{2,3},{3,2},{4,5},{5,4},{6,7},{7,6},{8,9},{9,8},{10,11... | collective-permute-start | bytes 2752520 | tf_op jit(solution)/shard_map/ppermute | solution.py:19
  137.5 21.0 %collective-permute-start.16 = (bf16[112,2048]{1,0:T(8,128)(2,1)S(1)}, bf16[112,2048]{1,0:T(8,128)(2,1)S(1)}, u32[]{:S(2)}, u32[]{:S(2)}) collective-permute-start(bf16[112,2048]{1,0:T(8,128)(2,1)S(1)} %shard_map.97), channel_id=1, source_target_pairs={{0,8},{1,9},{2,10},{3,11},{4,12},{5,13},{6,14},{7,15},{8,0},{9,1},... | collective-permute-start | bytes 1376264 | tf_op jit(solution)/shard_map/ppermute | solution.py:19
  137.7 35.9 %collective-permute-start.18 = (bf16[128,1920]{1,0:T(8,128)(2,1)S(1)}, bf16[128,1920]{1,0:T(8,128)(2,1)S(1)}, u32[]{:S(2)}, u32[]{:S(2)}) collective-permute-start(bf16[128,1920]{1,0:T(8,128)(2,1)S(1)} %collective-permute-done.12), channel_id=1, source_target_pairs={{0,2},{1,3},{2,0},{3,1},{4,6},{5,7},{6,4},{7,5},{8,10},{9,11},{10,... | collective-permute-start | bytes 1474568 | tf_op jit(solution)/shard_map/ppermute | solution.py:19
  158.5 52.9 %collective-permute-start.10 = (bf16[128,1792]{1,0:T(8,128)(2,1)}, bf16[128,1792]{1,0:T(8,128)(2,1)}, u32[]{:S(2)}, u32[]{:S(2)}) collective-permute-start(bf16[128,1792]{1,0:T(8,128)(2,1)} %slice.99), channel_id=1, source_target_pairs={{0,1},{1,0},{2,3},{3,2},{4,5},{5,4},{6,7},{7,6},{8,9},{9,8},{10,11... | collective-permute-start | bytes 1376264 | tf_op jit(solution)/shard_map/ppermute | solution.py:19
  173.6 19.1 %collective-permute-start.44 = (bf16[112,1024]{1,0:T(8,128)(2,1)}, bf16[112,1024]{1,0:T(8,128)(2,1)}, u32[]{:S(2)}, u32[]{:S(2)}) collective-permute-start(bf16[112,1024]{1,0:T(8,128)(2,1)} %shard_map.98.hid_ref), channel_id=1, source_target_pairs={{0,8},{1,9},{2,10},{3,11},{4,12},{5,13},{6,14},{7,15},{8,0},{9,1},... | collective-permute-start | bytes 688136 | tf_op jit(solution)/shard_map/ppermute | solution.py:19
  173.7 33.8 %collective-permute-start.41 = (bf16[112,1024]{1,0:T(8,128)(2,1)}, bf16[112,1024]{1,0:T(8,128)(2,1)}, u32[]{:S(2)}, u32[]{:S(2)}) collective-permute-start(bf16[112,1024]{1,0:T(8,128)(2,1)} %shard_map.95.hid_ref), channel_id=1, source_target_pairs={{0,8},{1,9},{2,10},{3,11},{4,12},{5,13},{6,14},{7,15},{8,0},{9,1},... | collective-permute-start | bytes 688136 | tf_op jit(solution)/shard_map/ppermute | solution.py:19
  179.8 61.6 %collective-permute-start.29 = (bf16[4,224,1024]{2,1,0:T(8,128)(2,1)}, bf16[4,224,1024]{2,1,0:T(8,128)(2,1)}, u32[]{:S(2)}, u32[]{:S(2)}) collective-permute-start(bf16[4,224,1024]{2,1,0:T(8,128)(2,1)} %pad_maximum_fusion.refs_0_), channel_id=1, source_target_pairs={{0,1},{1,0},{2,3},{3,2},{4,5},{5,4},{6,7},{7,6},{8,9},{9,8},{10,11... | collective-permute-start | bytes 5505032 | tf_op jit(solution)/shard_map/ppermute | solution.py:19
  192.8 24.4 %collective-permute-start.22 = (bf16[112,2048]{1,0:T(8,128)(2,1)}, bf16[112,2048]{1,0:T(8,128)(2,1)S(1)}, u32[]{:S(2)}, u32[]{:S(2)}) collective-permute-start(bf16[112,2048]{1,0:T(8,128)(2,1)} %copy-done.26), channel_id=1, source_target_pairs={{0,8},{1,9},{2,10},{3,11},{4,12},{5,13},{6,14},{7,15},{8,0},{9,1},... | collective-permute-start | bytes 1376264 | tf_op jit(solution)/shard_map/ppermute | solution.py:19
  211.4 13.4 %collective-permute-start.42 = (bf16[128,1792]{1,0:T(8,128)(2,1)S(1)}, bf16[128,1792]{1,0:T(8,128)(2,1)S(1)}, u32[]{:S(2)}, u32[]{:S(2)}) collective-permute-start(bf16[128,1792]{1,0:T(8,128)(2,1)S(1)} %slice.110), channel_id=1, source_target_pairs={{0,1},{1,0},{2,3},{3,2},{4,5},{5,4},{6,7},{7,6},{8,9},{9,8},{10,11... | collective-permute-start | bytes 1376264 | tf_op jit(solution)/shard_map/ppermute | solution.py:19
  211.9 30.1 %collective-permute-start.30 = (bf16[4,224,1024]{2,1,0:T(8,128)(2,1)}, bf16[4,224,1024]{2,1,0:T(8,128)(2,1)}, u32[]{:S(2)}, u32[]{:S(2)}) collective-permute-start(bf16[4,224,1024]{2,1,0:T(8,128)(2,1)} %collective-permute-done.28.refs_1_), channel_id=1, source_target_pairs={{0,1},{1,0},{2,3},{3,2},{4,5},{5,4},{6,7},{7,6},{8,9},{9,8},{10,11... | collective-permute-start | bytes 5505032 | tf_op jit(solution)/shard_map/ppermute | solution.py:19
  213.9 25.0 %collective-permute-start.37 = (bf16[4,512,224]{1,2,0:T(8,128)(2,1)}, bf16[4,512,224]{1,2,0:T(8,128)(2,1)S(1)}, u32[]{:S(2)}, u32[]{:S(2)}) collective-permute-start(bf16[4,512,224]{1,2,0:T(8,128)(2,1)} %collective-permute-done.35), channel_id=1, source_target_pairs={{0,1},{1,0},{2,3},{3,2},{4,5},{5,4},{6,7},{7,6},{8,9},{9,8},{10,11... | collective-permute-start | bytes 2752520 | tf_op jit(solution)/shard_map/ppermute | solution.py:19
  222.6 12.0 %collective-permute-start.46 = (bf16[112,1024]{1,0:T(8,128)(2,1)S(1)}, bf16[112,1024]{1,0:T(8,128)(2,1)S(1)}, u32[]{:S(2)}, u32[]{:S(2)}) collective-permute-start(bf16[112,1024]{1,0:T(8,128)(2,1)S(1)} %shard_map.101.hid_ref), channel_id=1, source_target_pairs={{0,8},{1,9},{2,10},{3,11},{4,12},{5,13},{6,14},{7,15},{8,0},{9,1},... | collective-permute-start | bytes 688136 | tf_op jit(solution)/shard_map/ppermute | solution.py:19
  224.8 12.8 %collective-permute-start.23 = (bf16[128,1792]{1,0:T(8,128)(2,1)S(1)}, bf16[128,1792]{1,0:T(8,128)(2,1)S(1)}, u32[]{:S(2)}, u32[]{:S(2)}) collective-permute-start(bf16[128,1792]{1,0:T(8,128)(2,1)S(1)} %slice.103), channel_id=1, source_target_pairs={{0,1},{1,0},{2,3},{3,2},{4,5},{5,4},{6,7},{7,6},{8,9},{9,8},{10,11... | collective-permute-start | bytes 1376264 | tf_op jit(solution)/shard_map/ppermute | solution.py:19
  234.6 74.0 %collective-permute-start.4 = (bf16[128,1792]{1,0:T(8,128)(2,1)}, bf16[128,1792]{1,0:T(8,128)(2,1)}, u32[]{:S(2)}, u32[]{:S(2)}) collective-permute-start(bf16[128,1792]{1,0:T(8,128)(2,1)} %slice.97), channel_id=1, source_target_pairs={{0,1},{1,0},{2,3},{3,2},{4,5},{5,4},{6,7},{7,6},{8,9},{9,8},{10,11... | collective-permute-start | bytes 1376264 | tf_op jit(solution)/shard_map/ppermute | solution.py:19
  237.6 11.8 %collective-permute-start.47 = (bf16[128,1792]{1,0:T(8,128)(2,1)}, bf16[128,1792]{1,0:T(8,128)(2,1)}, u32[]{:S(2)}, u32[]{:S(2)}) collective-permute-start(bf16[128,1792]{1,0:T(8,128)(2,1)} %slice.114), channel_id=1, source_target_pairs={{0,1},{1,0},{2,3},{3,2},{4,5},{5,4},{6,7},{7,6},{8,9},{9,8},{10,11... | collective-permute-start | bytes 1376264 | tf_op jit(solution)/shard_map/ppermute | solution.py:19
  239.9 76.6 %collective-permute-start.40 = (bf16[128,1792]{1,0:T(8,128)(2,1)}, bf16[128,1792]{1,0:T(8,128)(2,1)}, u32[]{:S(2)}, u32[]{:S(2)}) collective-permute-start(bf16[128,1792]{1,0:T(8,128)(2,1)} %slice.108), channel_id=1, source_target_pairs={{0,1},{1,0},{2,3},{3,2},{4,5},{5,4},{6,7},{7,6},{8,9},{9,8},{10,11... | collective-permute-start | bytes 1376264 | tf_op jit(solution)/shard_map/ppermute | solution.py:19
  241.4 9.3 %collective-permute-start.17 = (bf16[128,1792]{1,0:T(8,128)(2,1)}, bf16[128,1792]{1,0:T(8,128)(2,1)S(1)}, u32[]{:S(2)}, u32[]{:S(2)}) collective-permute-start(bf16[128,1792]{1,0:T(8,128)(2,1)} %slice.101), channel_id=1, source_target_pairs={{0,1},{1,0},{2,3},{3,2},{4,5},{5,4},{6,7},{7,6},{8,9},{9,8},{10,11... | collective-permute-start | bytes 1376264 | tf_op jit(solution)/shard_map/ppermute | solution.py:19
  242.0 12.7 %collective-permute-start.24 = (bf16[128,1792]{1,0:T(8,128)(2,1)}, bf16[128,1792]{1,0:T(8,128)(2,1)S(1)}, u32[]{:S(2)}, u32[]{:S(2)}) collective-permute-start(bf16[128,1792]{1,0:T(8,128)(2,1)} %add_convert_fusion.6), channel_id=1, source_target_pairs={{0,2},{1,3},{2,0},{3,1},{4,6},{5,7},{6,4},{7,5},{8,10},{9,11},{10,... | collective-permute-start | bytes 1376264 | tf_op jit(solution)/shard_map/ppermute | solution.py:19
  249.4 26.0 %collective-permute-start.31 = (bf16[128,2048]{1,0:T(8,128)(2,1)S(1)}, bf16[128,2048]{1,0:T(8,128)(2,1)S(1)}, u32[]{:S(2)}, u32[]{:S(2)}) collective-permute-start(bf16[128,2048]{1,0:T(8,128)(2,1)S(1)} %get-tuple-element.8), channel_id=1, source_target_pairs={{0,8},{1,9},{2,10},{3,11},{4,12},{5,13},{6,14},{7,15},{8,0},{9,1},... | collective-permute-start | bytes 1572872 | tf_op jit(solution)/shard_map/ppermute | solution.py:19
  250.7 26.4 %collective-permute-start.45 = (bf16[128,1792]{1,0:T(8,128)(2,1)S(1)}, bf16[128,1792]{1,0:T(8,128)(2,1)S(1)}, u32[]{:S(2)}, u32[]{:S(2)}) collective-permute-start(bf16[128,1792]{1,0:T(8,128)(2,1)S(1)} %copy-done.35), channel_id=1, source_target_pairs={{0,1},{1,0},{2,3},{3,2},{4,5},{5,4},{6,7},{7,6},{8,9},{9,8},{10,11... | collective-permute-start | bytes 1376264 | tf_op jit(solution)/shard_map/ppermute | solution.py:19
  254.7 56.0 %collective-permute-start.11 = (bf16[128,1792]{1,0:T(8,128)(2,1)}, bf16[128,1792]{1,0:T(8,128)(2,1)}, u32[]{:S(2)}, u32[]{:S(2)}) collective-permute-start(bf16[128,1792]{1,0:T(8,128)(2,1)} %add_convert_fusion.7), channel_id=1, source_target_pairs={{0,2},{1,3},{2,0},{3,1},{4,6},{5,7},{6,4},{7,5},{8,10},{9,11},{10,... | collective-permute-start | bytes 1376264 | tf_op jit(solution)/shard_map/ppermute | solution.py:19
  275.5 13.4 %collective-permute-start.48 = (bf16[128,1792]{1,0:T(8,128)(2,1)S(1)}, bf16[128,1792]{1,0:T(8,128)(2,1)S(1)}, u32[]{:S(2)}, u32[]{:S(2)}) collective-permute-start(bf16[128,1792]{1,0:T(8,128)(2,1)S(1)} %add_convert_fusion.2), channel_id=1, source_target_pairs={{0,2},{1,3},{2,0},{3,1},{4,6},{5,7},{6,4},{7,5},{8,10},{9,11},{10,... | collective-permute-start | bytes 1376264 | tf_op jit(solution)/shard_map/ppermute | solution.py:19
  277.1 39.4 %collective-permute-start.43 = (bf16[128,1792]{1,0:T(8,128)(2,1)}, bf16[128,1792]{1,0:T(8,128)(2,1)S(1)}, u32[]{:S(2)}, u32[]{:S(2)}) collective-permute-start(bf16[128,1792]{1,0:T(8,128)(2,1)} %add_convert_fusion.3), channel_id=1, source_target_pairs={{0,2},{1,3},{2,0},{3,1},{4,6},{5,7},{6,4},{7,5},{8,10},{9,11},{10,... | collective-permute-start | bytes 1376264 | tf_op jit(solution)/shard_map/ppermute | solution.py:19
  288.9 11.5 %collective-permute-start.32 = (bf16[128,1024]{1,0:T(8,128)(2,1)S(1)}, bf16[128,1024]{1,0:T(8,128)(2,1)S(1)}, u32[]{:S(2)}, u32[]{:S(2)}) collective-permute-start(bf16[128,1024]{1,0:T(8,128)(2,1)S(1)} %fusion.theirs_ref), channel_id=1, source_target_pairs={{0,8},{1,9},{2,10},{3,11},{4,12},{5,13},{6,14},{7,15},{8,0},{9,1},... | collective-permute-start | bytes 786440 | tf_op jit(solution)/shard_map/ppermute | solution.py:19
  300.4 13.7 %collective-permute-start.25 = (bf16[128,1792]{1,0:T(8,128)(2,1)}, bf16[128,1792]{1,0:T(8,128)(2,1)}, u32[]{:S(2)}, u32[]{:S(2)}) collective-permute-start(bf16[128,1792]{1,0:T(8,128)(2,1)} %add_convert_fusion.5), channel_id=1, source_target_pairs={{0,4},{1,5},{2,6},{3,7},{4,0},{5,1},{6,2},{7,3},{8,12},{9,13},{10,... | collective-permute-start | bytes 1376264 | tf_op jit(solution)/shard_map/ppermute | solution.py:19
  308.6 20.6 %collective-permute-start.49 = (bf16[128,1792]{1,0:T(8,128)(2,1)}, bf16[128,1792]{1,0:T(8,128)(2,1)S(1)}, u32[]{:S(2)}, u32[]{:S(2)}) collective-permute-start(bf16[128,1792]{1,0:T(8,128)(2,1)} %add_convert_fusion.1), channel_id=1, source_target_pairs={{0,4},{1,5},{2,6},{3,7},{4,0},{5,1},{6,2},{7,3},{8,12},{9,13},{10,... | collective-permute-start | bytes 1376264 | tf_op jit(solution)/shard_map/ppermute | solution.py:19
  315.7 21.5 %collective-permute-start.38 = (bf16[128,1792]{1,0:T(8,128)(2,1)S(1)}, bf16[128,1792]{1,0:T(8,128)(2,1)S(1)}, u32[]{:S(2)}, u32[]{:S(2)}) collective-permute-start(bf16[128,1792]{1,0:T(8,128)(2,1)S(1)} %add_convert_fusion.4), channel_id=1, source_target_pairs={{0,8},{1,9},{2,10},{3,11},{4,12},{5,13},{6,14},{7,15},{8,0},{9,1},... | collective-permute-start | bytes 1376264 | tf_op jit(solution)/shard_map/ppermute | solution.py:19
  (39 other events, 384.3 us)

commit v2 on v1

v2 whole, which is shorter than its diff:
```python
import functools

import jax
import jax.numpy as jnp
from jax import lax
from jax.experimental import pallas as pl
from jax.experimental.pallas import tpu as pltpu
from jax.sharding import PartitionSpec as P

route_scale = 2.5
meta_lanes = 128
vmem_bytes = 48 * 1024 * 1024
f32 = jnp.float32
bf16 = jnp.bfloat16


def hop(block, mask, axis="expert"):
    count = lax.axis_size(axis)
    return lax.ppermute(block, axis, [(d, d ^ mask) for d in range(count)])


def settle(*values):
    return lax.optimization_barrier(values)


def ordered(is_upper, own_part, other_part, axis_dim):
    return jnp.where(
        is_upper,
        jnp.concatenate([other_part, own_part], axis_dim),
        jnp.concatenate([own_part, other_part], axis_dim),
    )


def silu(v):
    return v / (1.0 + jnp.exp(-v))


def slots_of(meta, pair, lanes):
    m = meta.astype(f32)
    rows = m.shape[0]
    first = m[:, 0:1] == pair
    second = m[:, 1:2] == pair
    gate = jnp.where(first, m[:, 2:3] + m[:, 3:4], 0.0) + jnp.where(
        second, m[:, 4:5] + m[:, 5:6], 0.0
    )
    hit = jnp.where(first, 1.0, 0.0) + jnp.where(second, 1.0, 0.0)
    before = lax.broadcasted_iota(jnp.int32, (rows, rows), 1) < lax.broadcasted_iota(
        jnp.int32, (rows, rows), 0
    )
    wide_hit = jnp.broadcast_to(hit, (rows, lanes))
    rank = jnp.dot(
        jnp.where(before, 1.0, 0.0).astype(bf16), wide_hit.astype(bf16), preferred_element_type=f32
    )
    slot = lax.broadcasted_iota(jnp.int32, (rows, lanes), 1).astype(f32)
    one_hot = jnp.where(rank == slot, wide_hit, 0.0).astype(bf16)
    return one_hot, gate


def pick_rows(pair_ref, first_ref, second_ref, rows_ref, cap):
    width = rows_ref.shape[1]
    count = first_ref.shape[1]
    pair = pair_ref[0].astype(f32)
    lanes = -(-cap // 128) * 128
    dims = (((0,), (0,)), ((), ()))
    for q in range(first_ref.shape[0]):
        meta = jnp.concatenate([first_ref[q, :, width:], second_ref[q, :, width:]], 0)
        one_hot, _ = slots_of(meta, pair, lanes)
        rows = lax.dot_general(
            one_hot[:count], first_ref[q, :, :width], dims, preferred_element_type=f32
        ) + lax.dot_general(
            one_hot[count:], second_ref[q, :, :width], dims, preferred_element_type=f32
        )
        rows_ref[q * cap : (q + 1) * cap, :] = rows[:cap].astype(bf16)


def partial_kernel(cap, pair_ref, first_ref, second_ref, w_ref, out_ref, rows_ref):
    @pl.when(pl.program_id(0) == 0)
    def _():
        pick_rows(pair_ref, first_ref, second_ref, rows_ref, cap)

    out_ref[...] = jnp.dot(
        rows_ref[...], w_ref[...], preferred_element_type=f32
    ).astype(bf16)


def hidden_kernel(
    cap, pair_ref, first_ref, second_ref, wg_ref, wu_ref, rg_ref, ru_ref, out_ref, rows_ref
):
    @pl.when(pl.program_id(0) == 0)
    def _():
        pick_rows(pair_ref, first_ref, second_ref, rows_ref, cap)

    rows = rows_ref[...]
    gate = jnp.dot(rows, wg_ref[...], preferred_element_type=f32) + rg_ref[...].astype(f32)
    up = jnp.dot(rows, wu_ref[...], preferred_element_type=f32) + ru_ref[...].astype(f32)
    out_ref[...] = (silu(gate) * up).astype(bf16)


def down_kernel(
    cap,
    pair_ref,
    first_ref,
    second_ref,
    hid_ref,
    w_ref,
    near_ref,
    far_ref,
    hit_ref,
    gate_ref,
    rows_ref,
):
    chips, count, _ = near_ref.shape

    @pl.when(pl.program_id(0) == 0)
    def _():
        for q in range(chips):
            meta = jnp.concatenate([first_ref[q], second_ref[q]], 0)
            one_hot, gate = slots_of(meta, pair_ref[0].astype(f32), hit_ref.shape[2])
            hit_ref[q] = one_hot
            gate_ref[q] = jnp.broadcast_to(gate, gate_ref.shape[1:])
        rows_ref[...] = jnp.zeros_like(rows_ref)

    rows = jnp.dot(hid_ref[...], w_ref[...], preferred_element_type=f32).astype(bf16)
    for q in range(chips):
        rows_ref[q, :cap, :] = rows[q * cap : (q + 1) * cap]
        picked = jnp.dot(hit_ref[q], rows_ref[q], preferred_element_type=f32)
        gated = (picked * gate_ref[q, :, 0:1]).astype(bf16)
        near_ref[q] = gated[:count]
        far_ref[q] = gated[count:]


def params():
    return pltpu.CompilerParams(
        vmem_limit_bytes=vmem_bytes, dimension_semantics=("arbitrary",)
    )


def smem():
    return pl.BlockSpec(memory_space=pltpu.SMEM)


def whole(array):
    return pl.BlockSpec(array.shape, lambda j: (0,) * len(array.shape))


def cost(m, k, n):
    return pl.CostEstimate(flops=0, bytes_accessed=0, transcendentals=0)


def partial_sums(pair, tok, weights, cap):
    width, columns = weights.shape
    rows = tok[0].shape[0] * cap
    steps = 4
    return pl.pallas_call(
        functools.partial(partial_kernel, cap),
        grid=(steps,),
        in_specs=[
            smem(),
            whole(tok[0]),
            whole(tok[1]),
            pl.BlockSpec((width, columns // steps), lambda j: (0, j)),
        ],
        out_specs=pl.BlockSpec((rows, columns // steps), lambda j: (0, j)),
        out_shape=jax.ShapeDtypeStruct((rows, columns), bf16),
        scratch_shapes=[pltpu.VMEM((rows, width), bf16)],
        compiler_params=params(),
        cost_estimate=cost(rows, width, columns),
    )(pair, *tok, weights)


def hidden_rows(pair, tok, weights, received, cap):
    width, columns = weights.shape
    units = columns // 2
    rows = received.shape[0]
    steps = 4
    block = units // steps
    return pl.pallas_call(
        functools.partial(hidden_kernel, cap),
        grid=(steps,),
        in_specs=[
            smem(),
            whole(tok[0]),
            whole(tok[1]),
            pl.BlockSpec((width, block), lambda j: (0, j)),
            pl.BlockSpec((width, block), lambda j: (0, j + steps)),
            pl.BlockSpec((rows, block), lambda j: (0, j)),
            pl.BlockSpec((rows, block), lambda j: (0, j + steps)),
        ],
        out_specs=pl.BlockSpec((rows, block), lambda j: (0, j)),
        out_shape=jax.ShapeDtypeStruct((rows, units), bf16),
        scratch_shapes=[pltpu.VMEM((rows, width), bf16)],
        compiler_params=params(),
        cost_estimate=cost(rows, width, columns),
    )(pair, *tok, weights, weights, received, received)


def weighted_rows(pair, tok, hidden, weights, cap):
    units, width = weights.shape
    chips, count, _ = tok[0].shape
    lanes = -(-cap // 128) * 128
    steps = 2
    block = width // steps
    meta = pl.BlockSpec((chips, count, meta_lanes), lambda j: (0, 0, width // meta_lanes))
    return pl.pallas_call(
        functools.partial(down_kernel, cap),
        grid=(steps,),
        in_specs=[
            smem(),
            meta,
            meta,
            whole(hidden),
            pl.BlockSpec((units, block), lambda j: (0, j)),
        ],
        out_specs=[pl.BlockSpec((chips, count, block), lambda j: (0, 0, j))] * 2,
        out_shape=[jax.ShapeDtypeStruct((chips, count, width), bf16)] * 2,
        scratch_shapes=[
            pltpu.VMEM((chips, 2 * count, lanes), bf16),
            pltpu.VMEM((chips, 2 * count, 128), f32),
            pltpu.VMEM((chips, lanes, block), bf16),
        ],
        compiler_params=params(),
        cost_estimate=cost(chips * cap, units, width),
    )(pair, *tok, hidden, weights)


def assemble(masks, first_column, spots_ref, stack_refs, out_ref, sems):
    count, rows, _ = stack_refs[0].shape
    columns = out_ref.shape[1] // len({q for _, _, q in masks})
    copies = []
    for core, stack_ref in enumerate(stack_refs):
        for i, (upper, _, q) in enumerate(masks):
            shard = spots_ref[core * count + i]
            row = pl.multiple_of(shard * 2 * rows + upper * rows, rows)
            column = pl.multiple_of(spots_ref[2 * count + q] * columns, columns)
            copies.append(
                pltpu.make_async_copy(
                    stack_ref.at[i, :, pl.ds(first_column, columns)],
                    out_ref.at[pl.ds(row, rows), pl.ds(column, columns)],
                    sems.at[len(copies)],
                )
            )
    for copy in copies:
        copy.start()
    for copy in copies:
        copy.wait()


def shared_gate_kernel(
    masks, spots_ref, own_ref, other_ref, a_ref, b_ref, mine_ref, theirs_ref, w_ref, sems
):
    assemble(masks, 0, spots_ref, (a_ref, b_ref), w_ref, sems)
    width, columns = w_ref.shape
    step = 512

    @pl.loop(0, columns // step)
    def _(j):
        at = pl.ds(pl.multiple_of(j * step, step), step)
        w = w_ref[:, at]
        mine_ref[:, at] = jnp.dot(own_ref[:, :width], w, preferred_element_type=f32).astype(bf16)
        theirs_ref[:, at] = jnp.dot(other_ref[:, :width], w, preferred_element_type=f32)


def shared_partial(spots, masks, own, other, stacks, width, columns):
    rows = own.shape[0]
    vmem = pl.BlockSpec(memory_space=pltpu.VMEM)
    hbm = pl.BlockSpec(memory_space=pl.ANY)
    return pl.pallas_call(
        functools.partial(shared_gate_kernel, masks),
        in_specs=[smem(), vmem, vmem, hbm, hbm],
        out_specs=[vmem, vmem],
        out_shape=[
            jax.ShapeDtypeStruct((rows, columns), bf16),
            jax.ShapeDtypeStruct((rows, columns), f32),
        ],
        scratch_shapes=[
            pltpu.VMEM((width, columns), bf16),
            pltpu.SemaphoreType.DMA((2 * len(masks),)),
        ],
        compiler_params=pltpu.CompilerParams(vmem_limit_bytes=vmem_bytes),
        cost_estimate=cost(2 * rows, width, columns),
    )(spots, own, other, *stacks)


def shared_down_kernel(
    masks, first_column, spots_ref, hid_ref, a_ref, b_ref, out_ref, d_ref, sems
):
    assemble(masks, first_column, spots_ref, (a_ref, b_ref), d_ref, sems)
    step = 256

    @pl.loop(0, d_ref.shape[0] // step)
    def _(j):
        at = pl.ds(pl.multiple_of(j * step, step), step)
        out_ref[:, at] = lax.dot_general(
            hid_ref[...], d_ref[at, :], (((1,), (1,)), ((), ())), preferred_element_type=f32
        ).astype(bf16)


def shared_rows(spots, masks, hidden, stacks, first_column, width):
    rows, units = hidden.shape
    vmem = pl.BlockSpec(memory_space=pltpu.VMEM)
    hbm = pl.BlockSpec(memory_space=pl.ANY)
    return pl.pallas_call(
        functools.partial(shared_down_kernel, masks, first_column),
        in_specs=[smem(), vmem, hbm, hbm],
        out_specs=vmem,
        out_shape=jax.ShapeDtypeStruct((rows, width), bf16),
        scratch_shapes=[
            pltpu.VMEM((width, units), bf16),
            pltpu.SemaphoreType.DMA((2 * len(masks),)),
        ],
        compiler_params=pltpu.CompilerParams(vmem_limit_bytes=vmem_bytes),
        cost_estimate=cost(rows, units, width),
    )(spots, hidden, *stacks)


def in_order(masks, place, group_index, stacks):
    groups = len({q for _, _, q in masks})
    shards = len(masks) // groups
    spot = {}
    for core in (0, 1):
        for i, (upper, m, q) in enumerate(masks):
            spot[m | core, upper, q] = core * len(masks) + i
    table = [[[spot[m, u, q] for q in range(groups)] for u in (0, 1)] for m in range(shards)]
    table = jnp.array(table, jnp.int32)
    table = table[jnp.arange(shards, dtype=jnp.int32) ^ place]
    table = table[:, :, jnp.arange(groups, dtype=jnp.int32) ^ group_index]
    parts = jnp.concatenate(stacks)[table]
    parts = parts.transpose(0, 1, 3, 2, 4)
    return parts.reshape(shards, -1, groups, parts.shape[-1])


def local(
    tokens,
    expert_gate_up,
    expert_down,
    shared_gate_up,
    shared_down,
    host_expert,
    pair_picks,
    affinity,
):
    devices = lax.axis_size("expert")
    groups = lax.axis_size("groups")
    half = devices // 2
    dev_index = lax.axis_index("expert")
    group_index = lax.axis_index("groups")
    is_upper = dev_index >= half
    pair = jnp.reshape(dev_index % half, (1,)).astype(jnp.int32)
    tok_rows, full_width = tokens.shape
    width = full_width // 2
    units = expert_down.shape[0]
    pick_count = pair_picks.shape[1]
    capacity = 7 * tok_rows * pick_count // (4 * half)
    cap = -(-2 * capacity // 16) * 16
    chips = list(range(2, half, 2))
    near_chips = sorted([m for m in chips if m & (m - 1) == 0], reverse=True)
    far_chips = [m for m in chips if m & (m - 1)]

    pair_iota = jnp.arange(half, dtype=jnp.int32)
    expert_ids = jnp.sum(
        jnp.where(pair_picks[:, :, None] == pair_iota, host_expert[None, None, :], 0), 2
    )
    scores = jnp.sum(
        jnp.where(expert_ids[:, :, None] == pair_iota, affinity[:, None, :], 0.0), 2
    )
    gates = route_scale * scores / jnp.sum(scores, 1, keepdims=True)
    gates_high = lax.reduce_precision(gates, 8, 7)
    gates_low = gates - gates_high
    meta = jnp.concatenate(
        [
            pair_picks.astype(f32),
            jnp.stack([gates_high, gates_low], 2).reshape(tok_rows, 2 * pick_count),
            jnp.zeros((tok_rows, meta_lanes - 3 * pick_count), f32),
        ],
        1,
    ).astype(bf16)
    low, high = tokens[:, :width], tokens[:, width:]
    mine = jnp.concatenate([jnp.where(is_upper, high, low), meta], 1)
    theirs = jnp.concatenate([jnp.where(is_upper, low, high), meta], 1)

    def sums_of(tok):
        return partial_sums(pair, tok, expert_gate_up, cap)

    def hidden_of(tok, sums):
        return hidden_rows(pair, tok, expert_gate_up, sums, cap)

    def rows_of(tok, hidden):
        return weighted_rows(pair, tok, hidden, expert_down, cap)

    def summed(rows, other):
        return (rows.astype(f32) + other.astype(f32)).astype(bf16)

    def hops_of(blocks, masks):
        return [hop(block, m) for m, block in zip(masks, blocks)]

    def finished(shared, rows, other, parts):
        total = shared.astype(f32) + rows[0].astype(f32) + other.astype(f32)
        for part in parts:
            total = total + part.astype(f32)
        return total.astype(bf16)

    low_bit = near_chips[-1]
    group_bits = [1 << i for i in range(groups.bit_length() - 1)]
    gate_columns = 2 * units // groups
    down_rows = units // groups
    shard_rows = shared_gate_up.shape[0]
    upper_row = shard_rows // 2

    def share_of_weights():
        gate = lax.dynamic_slice_in_dim(shared_gate_up, group_index * gate_columns, gate_columns, 1)
        down = lax.dynamic_slice_in_dim(shared_down, group_index * down_rows, down_rows, 0)
        return jnp.concatenate([gate, down.T], 1)[None]

    def doubled(stack, bits, axis="expert"):
        for bit in bits:
            stack = jnp.concatenate([stack, hop(stack, bit, axis)])
        return stack

    def masks_of(upper, steps):
        masks = [(0, 0)]
        for m, q in steps:
            masks = masks + [(a ^ m, b ^ q) for a, b in masks]
        return [(upper, a, b) for a, b in masks]

    far_steps = [(m, 0) for m in near_chips[:-1]]
    group_steps = [(0, q) for q in group_bits]
    low_steps = [(low_bit, 0)]
    masks = masks_of(0, far_steps + group_steps + low_steps) + masks_of(
        1, far_steps + low_steps + group_steps
    )
    place = dev_index % half
    chip_masks = jnp.array([m for _, m, _ in masks], jnp.int32)
    spots = jnp.concatenate(
        [place ^ chip_masks, place ^ 1 ^ chip_masks, group_index ^ jnp.arange(groups)]
    ).astype(jnp.int32)
    by_kernel = upper_row % 16 == 0

    def shared_sums(stacks):
        if by_kernel:
            return shared_partial(spots, masks, mine, cross, stacks, width, 2 * units)
        gate = in_order(masks, place, group_index, stacks)[..., :gate_columns]
        gate = gate.reshape(width, 2 * units)
        own = jnp.dot(mine[:, :width], gate, preferred_element_type=f32).astype(bf16)
        return own, jnp.dot(cross[:, :width], gate, preferred_element_type=f32)

    def shared_down_of(hidden, stacks):
        if by_kernel:
            return shared_rows(spots, masks, hidden, stacks, gate_columns, width)
        down = in_order(masks, place, group_index, stacks)[..., gate_columns:]
        down = down.reshape(width, units)
        return lax.dot_general(
            hidden, down, (((1,), (1,)), ((), ())), preferred_element_type=f32
        ).astype(bf16)

    cross = hop(theirs, half)
    near = [hop(mine, m) for m in near_chips]
    own_tok = mine[None], hop(mine, 1)[None]
    own_sums = sums_of(own_tok)
    weights = share_of_weights()
    cross, near, own_tok, own_sums, weights = settle(cross, near, own_tok, own_sums, weights)

    own_in = hop(own_sums, half)
    got = dict(zip(near_chips, near))
    away_near = [hop(cross, m) for m in near_chips[:-1]]
    near_tok = jnp.stack(near)
    near_tok = near_tok, hop(near_tok, 1)
    first_far = [m for m in far_chips if m & low_bit]
    later_far = [m for m in far_chips if not m & low_bit]
    for m in sorted(later_far):
        got[m] = hop(got[m ^ (m & -m)], m & -m)
    both = hop(jnp.stack([cross] + [got[m ^ low_bit] for m in first_far]), low_bit)
    away_near.append(both[0])
    for i, m in enumerate(first_far):
        got[m] = both[1 + i]
    far = [got[m] for m in far_chips]
    near_sums = sums_of(near_tok)
    own_in, away_near, far, near_tok, near_sums = settle(
        own_in, away_near, far, near_tok, near_sums
    )

    near_in = hop(near_sums, half)
    got = dict(zip(near_chips, away_near))
    for m in sorted(far_chips, key=lambda m: bin(m).count("1")):
        got[m] = hop(got[m ^ (m & -m)], m & -m)
    away_far = [got[m] for m in far_chips]
    mixed = jnp.stack([cross] + away_near + far)
    others = hop(mixed, 1)
    cut = 1 + len(near_chips)
    away_own_tok = mixed[:1], others[:1]
    away_near_tok = mixed[1:cut], others[1:cut]
    far_tok = mixed[cut:], others[cut:]
    far_sums = sums_of(far_tok)
    away_own_hidden = hidden_of(away_own_tok, own_in)
    weights = doubled(weights, near_chips[:-1])
    (
        near_in, away_far, away_near_tok, away_own_tok, far_tok, far_sums, away_own_hidden, weights
    ) = settle(
        near_in, away_far, away_near_tok, away_own_tok, far_tok, far_sums, away_own_hidden, weights
    )

    far_in = hop(far_sums, half)
    own_hidden = hop(away_own_hidden, half)
    away_far_tok = jnp.stack(away_far)
    away_far_tok = away_far_tok, hop(away_far_tok, 1)
    away_near_hidden = hidden_of(away_near_tok, near_in)
    away_own_rows = rows_of(away_own_tok, away_own_hidden)
    away_near_rows = rows_of(away_near_tok, away_near_hidden)
    lower = doubled(weights[:, :upper_row], group_bits, "groups")
    upper = doubled(weights[:, upper_row:], [low_bit])
    (
        far_in, own_hidden, away_far_tok, away_near_hidden, away_own_rows, away_near_rows,
        lower, upper,
    ) = settle(
        far_in, own_hidden, away_far_tok, away_near_hidden, away_own_rows, away_near_rows,
        lower, upper,
    )

    near_hidden = hop(away_near_hidden, half)
    away_others = hop(jnp.concatenate([away_own_rows[1], away_near_rows[1]]), 1)
    away_far_hidden = hidden_of(away_far_tok, far_in)
    away_far_rows = rows_of(away_far_tok, away_far_hidden)
    own_rows = rows_of(own_tok, own_hidden)
    lower = doubled(lower, [low_bit])
    upper = doubled(upper, group_bits, "groups")
    weights = jnp.concatenate([lower, upper])
    near_hidden, away_others, away_far_hidden, away_far_rows, own_rows, weights = settle(
        near_hidden, away_others, away_far_hidden, away_far_rows, own_rows, weights
    )

    far_hidden = hop(away_far_hidden, half)
    stacks = weights, hop(weights, 1)
    shared_own, shared_other = shared_sums(stacks)
    parts = hops_of(summed(away_near_rows[0], away_others[1:]), near_chips)
    others = hop(jnp.concatenate([own_rows[1], away_far_rows[1]]), 1)
    near_rows = rows_of(near_tok, near_hidden)
    far_hidden, stacks, shared_own, shared_other, parts, others, near_rows = settle(
        far_hidden, stacks, shared_own, shared_other, parts, others, near_rows
    )

    shared_in = hop(shared_own, half)
    parts += hops_of(summed(away_far_rows[0], others[1:]), far_chips)
    near_others = hop(near_rows[1], 1)
    far_rows = rows_of(far_tok, far_hidden)
    shared_in, parts, near_others, far_rows = settle(shared_in, parts, near_others, far_rows)

    total = shared_other + shared_in.astype(f32)
    other_hidden = (silu(total[:, :units]) * total[:, units:]).astype(bf16)
    shared_hidden = hop(other_hidden, half)
    shared_out = shared_down_of(other_hidden, stacks)
    away_rows = finished(shared_out, away_own_rows[0], away_others[0], parts)
    parts = hops_of(summed(near_rows[0], near_others), near_chips)
    far_others = hop(far_rows[1], 1)
    shared_hidden, away_rows, parts, far_others = settle(
        shared_hidden, away_rows, parts, far_others
    )

    far_half = hop(away_rows, half)
    parts += hops_of(summed(far_rows[0], far_others), far_chips)
    shared_out = shared_down_of(shared_hidden, stacks)
    near_half = finished(shared_out, own_rows[0], others[0], parts)
    return ordered(is_upper, near_half, far_half, 1)


def solution(mesh):
    in_specs = (
        P(("groups", "expert"), None),
        P("expert", None),
        P(None, "expert"),
        P("expert", None),
        P(None, "expert"),
        P(),
        P(("groups", "expert"), None),
        P(("groups", "expert"), None),
    )
    out_specs = P(("groups", "expert"), None)
    return jax.shard_map(local, mesh=mesh, in_specs=in_specs, out_specs=out_specs, check_vma=False)
```

time: 340 us -> 275 us (0.81)
  waiting for transfers between devices: 173 us -> 137 us
  local copies, waits for them, and re-layouts: 33.7 us -> 7.84 us
  Pallas kernels: 74.7 us -> 69 us
  other arithmetic: 20 us -> 23.7 us
    ppermute x50 -> x35, waiting for transfers between devices: 173 us -> 137 us  [hop(): return lax.ppermute(block, axis, [(d, d ^ mask) for d in range(count)])]
    unnamed x81 -> x36, local copies, waits for them, and re-layouts: 11.9 us -> 3.06 us
    slice x13 -> x3, local copies, waits for them, and re-layouts: 9.63 us -> 1.35 us  [the longest x1 1.2 us: local(): upper = doubled(weights[:, upper_row:], [low_bit])]
    concatenate x6 -> x7, other arithmetic: 5.22 us -> 12.2 us  [the longest x1 5.46 us: local(): weights = jnp.concatenate([lower, upper])]
    convert_element_type x9 -> x4, other arithmetic: 9.91 us -> 3.52 us  [the longest x2 3.09 us: finished(): return total.astype(bf16)]
    ppermute x3 -> x0, local copies, waits for them, and re-layouts: 6.1 us -> none  [hop(): return lax.ppermute(block, axis, [(d, d ^ mask) for d in range(count)])]
    pallas_call x18 -> x15, Pallas kernels: 74.7 us -> 69 us  [the longest x3 17.4 us: partial_sums(): pl.pallas_call(functools.partial(partial_kernel, cap), grid=(steps,), in_...]
    concatenate x8 -> x0, local copies, waits for them, and re-layouts: 4.46 us -> none  [the longest x7 3.16 us: spread(): return {m: jnp.concatenate([b, hop(b, 1)], 0) for m, b in got.items()}]
  transfers between devices with their start and end apart: 50 -> 35, of which waited for: 16 -> 15; matrix products, arithmetic and copies ran while one was open for 13% -> 7% of each run, Pallas kernels for 22% -> 25%
where the time goes in v2:
time: 275 us; the launch traced here: 274 us
  waiting for transfers between devices  137 us (50%)
  Pallas kernels  69 us (25%)
  starting transfers between devices  36.1 us (13%)
  other arithmetic  23.7 us (9%)
  local copies, waits for them, and re-layouts  7.84 us (3%)
    ppermute x35, waiting for transfers between devices, hop(): return lax.ppermute(block, axis, [(d, d ^ mask) for d in range(count)])  137 us
    ppermute x35, starting transfers between devices, hop(): return lax.ppermute(block, axis, [(d, d ^ mask) for d in range(count)])  36.1 us
    pallas_call x3, Pallas kernels, partial_sums(): pl.pallas_call(functools.partial(partial_kernel, cap), grid=(steps,), in_...  17.4 us
    pallas_call x6, Pallas kernels, weighted_rows(): pl.pallas_call(functools.partial(down_kernel, cap), grid=(steps,), in_spe...  17.2 us
    pallas_call x3, Pallas kernels, hidden_rows(): pl.pallas_call(functools.partial(hidden_kernel, cap), grid=(steps,), in_s...  17.1 us
    pallas_call x2, Pallas kernels, shared_rows(): pl.pallas_call(functools.partial(shared_down_kernel, masks, first_column)...  10.3 us
    pallas_call x1, Pallas kernels, shared_partial(): pl.pallas_call(functools.partial(shared_gate_kernel, masks), in_specs=[sm...  6.96 us
  transfers between devices with their start and end apart: 35, of which 15 were waited for; matrix products, arithmetic and copies ran while one was open for 7% of the time, Pallas kernels for 25%

profile of v2, /device:TPU:0, one launch (start us, length us, event | category | flops | bytes accessed | tf_op | source)
XLA Modules:
  0.0 273.9 jit_solution(2471884821893133004)
XLA Ops:
  2.6 1.2 broadcast_select_fusion
  5.3 3.6 %collective-permute-start = (bf16[128,1920]{1,0:T(8,128)(2,1)}, bf16[128,1920]{1,0:T(8,128)(2,1)S(1)}, u32[]{:S(2)}, u32[]{:S(2)}) collective-permute-start(bf16[128,1920]{1,0:T(8,128)(2,1)} %concatenate.41), channel_id=1, source_target_pairs={{0,8},{1,9},{2,10},{3,11},{4,12},{5,13},{6,14},{7,15},{8,0},{9,1},... | collective-permute-start | bytes 1474568 | tf_op jit(solution)/shard_map/ppermute | solution.py:19
  8.9 1.5 collective-permute-start.2
  10.4 1.6 collective-permute-start.1
  13.1 5.5 %shard_map.91 = bf16[112,2048]{1,0:T(8,128)(2,1)S(1)} custom-call(s32[1]{0:T(128)} %bitcast.4.pair_ref, bf16[1,128,1920]{2,1,0:T(8,128)(2,1)S(1)} %bitcast.53, bf16[1,128,1920]{2,1,0:T(8,128)(2,1)S(1)} %bitcast.58, bf16[1792,2048]{1,0:T(8,128)(2,1)} %wu_ref.5), custom_call_target="tpu_custom_call" | custom-call | tf_op jit(solution)/shard_map/pallas_call | solution.py:154
  18.7 13.0 %collective-permute-done.other_ref = bf16[128,1920]{1,0:T(8,128)(2,1)S(1)} collective-permute-done((bf16[128,1920]{1,0:T(8,128)(2,1)}, bf16[128,1920]{1,0:T(8,128)(2,1)S(1)}, u32[]{:S(2)}, u32[]{:S(2)}) %collective-permute-start) | collective-permute-done | bytes 491552 | tf_op jit(solution)/shard_map/ppermute | solution.py:19
  31.7 1.3 collective-permute-done.1
  33.0 1.4 pad_maximum_fusion.7
  35.1 1.4 collective-permute-start.5
  36.5 2.2 collective-permute-start.4
  38.7 6.5 %shard_map.92 = bf16[224,2048]{1,0:T(8,128)(2,1)S(1)} custom-call(s32[1]{0:T(128)} %bitcast.4.pair_ref, bf16[2,128,1920]{2,1,0:T(8,128)(2,1)S(1)} %get-tuple-element.131.first_ref, bf16[2,128,1920]{2,1,0:T(8,128)(2,1)S(1)} %collective-permute-done.7.second_ref, bf16[1792,2048]{1,0:T(8,128)(2,1)} %wu_ref.5), custom_call_target="tpu_custom_call" | custom-call | tf_op jit(solution)/shard_map/pallas_call | solution.py:154
  45.3 13.3 %collective-permute-done.6 = bf16[2,128,1920]{2,1,0:T(8,128)(2,1)S(1)} collective-permute-done((bf16[2,128,1920]{2,1,0:T(8,128)(2,1)S(1)}, bf16[2,128,1920]{2,1,0:T(8,128)(2,1)S(1)}, u32[]{:S(2)}, u32[]{:S(2)}) %collective-permute-start.6) | collective-permute-done | bytes 983072 | tf_op jit(solution)/shard_map/ppermute | solution.py:19
  59.1 1.5 collective-permute-start.11
  60.6 1.9 collective-permute-start.8
  62.5 28.5 %collective-permute-done.11 = bf16[1,224,1536]{2,1,0:T(8,128)(2,1)S(1)} collective-permute-done((bf16[1,224,1536]{2,1,0:T(8,128)(2,1)S(1)}, bf16[1,224,1536]{2,1,0:T(8,128)(2,1)S(1)}, u32[]{:S(2)}, u32[]{:S(2)}) %collective-permute-start.11) | collective-permute-done | bytes 688160 | tf_op jit(solution)/shard_map/ppermute | solution.py:19
  92.1 5.4 %shard_map.93 = bf16[112,2048]{1,0:T(8,128)(2,1)S(1)} custom-call(s32[1]{0:T(128)} %bitcast.4.pair_ref, bf16[1,128,1920]{2,1,0:T(8,128)(2,1)S(1)} %bitcast.56, bf16[1,128,1920]{2,1,0:T(8,128)(2,1)S(1)} %get-tuple-element.144.second_ref, bf16[1792,2048]{1,0:T(8,128)(2,1)} %wu_ref.5), custom_call_target="tpu_custom_call" | custom-call | tf_op jit(solution)/shard_map/pallas_call | solution.py:154
  97.5 5.4 %shard_map.94.hid_ref = bf16[112,1024]{1,0:T(8,128)(2,1)S(1)} custom-call(s32[1]{0:T(128)} %bitcast.4.pair_ref, bf16[1,128,1920]{2,1,0:T(8,128)(2,1)S(1)} %bitcast.51, bf16[1,128,1920]{2,1,0:T(8,128)(2,1)S(1)} %get-tuple-element.102.second_ref, bf16[1792,2048]{1,0:T(8,128)(2,1)} %wu_ref.5, bf16[1792,2048]{1,0:T(8,128)(2,1)} %wu_ref.5, ...), custom_call_target="tpu_custom_call" | custom-call | tf_op jit(solution)/shard_map/pallas_call | solution.py:177
  105.9 1.5 collective-permute-start.15
  108.7 1.7 collective-permute-start.12
  110.4 6.3 %shard_map.95.hid_ref = bf16[224,1024]{1,0:T(8,128)(2,1)S(1)} custom-call(s32[1]{0:T(128)} %bitcast.4.pair_ref, bf16[2,128,1920]{2,1,0:T(8,128)(2,1)S(1)} %pad_maximum_fusion.8.first_ref, bf16[2,128,1920]{2,1,0:T(8,128)(2,1)S(1)} %slice.64.second_ref, bf16[1792,2048]{1,0:T(8,128)(2,1)} %wu_ref.5, bf16[1792,2048]{1,0:T(8,128)(2,1)} %wu_ref.5, ...), custom_call_target="tpu_custom_call" | custom-call | tf_op jit(solution)/shard_map/pallas_call | solution.py:177
  116.7 4.5 %shard_map.97 = (bf16[2,128,1792]{2,1,0:T(8,128)(2,1)S(1)}, bf16[2,128,1792]{2,1,0:T(8,128)(2,1)S(1)}) custom-call(s32[1]{0:T(128)} %bitcast.4.pair_ref, bf16[2,128,1920]{2,1,0:T(8,128)(2,1)S(1)} %pad_maximum_fusion.8.first_ref, bf16[2,128,1920]{2,1,0:T(8,128)(2,1)S(1)} %slice.64.second_ref, bf16[224,1024]{1,0:T(8,128)(2,1)S(1)} %shard_map.95.hid_ref, ...), custom_call_target="tpu_custom_call" | custom-call | tf_op jit(solution)/shard_map/pallas_call | solution.py:204
  121.2 2.1 shard_map.96
  123.4 1.6 pad_maximum_fusion.4
  125.0 2.5 pad_maximum_fusion.3
  127.5 1.9 collective-permute-done.13.hid_ref
  129.4 9.5 %collective-permute-done.12.rg_ref.ru_ref = bf16[112,2048]{1,0:T(8,128)(2,1)S(1)} collective-permute-done((bf16[112,2048]{1,0:T(8,128)(2,1)S(1)}, bf16[112,2048]{1,0:T(8,128)(2,1)S(1)}, u32[]{:S(2)}, u32[]{:S(2)}) %collective-permute-start.12) | collective-permute-done | bytes 458784 | tf_op jit(solution)/shard_map/ppermute | solution.py:19
  140.6 1.3 pad_maximum_fusion.5
  141.9 5.4 %shard_map.98.hid_ref = bf16[112,1024]{1,0:T(8,128)(2,1)S(1)} custom-call(s32[1]{0:T(128)} %bitcast.4.pair_ref, bf16[1,128,1920]{2,1,0:T(8,128)(2,1)S(1)} %bitcast.61, bf16[1,128,1920]{2,1,0:T(8,128)(2,1)S(1)} %collective-permute-done.14.second_ref, bf16[1792,2048]{1,0:T(8,128)(2,1)} %wu_ref.5, bf16[1792,2048]{1,0:T(8,128)(2,1)} %wu_ref.5, ...), custom_call_target="tpu_custom_call" | custom-call | tf_op jit(solution)/shard_map/pallas_call | solution.py:177
  147.3 2.1 shard_map.99
  150.2 2.1 shard_map.100
  152.3 18.8 %collective-permute-done.19 = bf16[4,112,1536]{2,1,0:T(8,128)(2,1)} collective-permute-done((bf16[4,112,1536]{2,1,0:T(8,128)(2,1)}, bf16[4,112,1536]{2,1,0:T(8,128)(2,1)}, u32[]{:S(2)}, u32[]{:S(2)}) %collective-permute-start.19) | collective-permute-done | bytes 1376288 | tf_op jit(solution)/shard_map/ppermute | solution.py:19
  172.0 5.5 %pad_maximum_fusion.a_ref = bf16[16,112,1536]{2,1,0:T(8,128)(2,1)} fusion(bf16[4,112,1536]{2,1,0:T(8,128)(2,1)} %collective-permute-done.20, bf16[4,112,1536]{2,1,0:T(8,128)(2,1)S(1)} %pad_maximum_fusion.4, bf16[4,112,1536]{2,1,0:T(8,128)(2,1)} %collective-permute-done.19, bf16[4,112,1536]{2,1,0:T(8,128)(2,1)} %pad_maximum_fusion.3), kind=kLoop, calls=%fused_computation | loop fusion | flops 8257536 | bytes 11010048 | tf_op jit(solution)/shard_map/concatenate | solution.py:525
  181.0 2.7 collective-permute-start.21
  185.9 4.3 %shard_map.102 = (bf16[2,128,1792]{2,1,0:T(8,128)(2,1)S(1)}, bf16[2,128,1792]{2,1,0:T(8,128)(2,1)S(1)}) custom-call(s32[1]{0:T(128)} %bitcast.4.pair_ref, bf16[2,128,1920]{2,1,0:T(8,128)(2,1)S(1)} %get-tuple-element.131.first_ref, bf16[2,128,1920]{2,1,0:T(8,128)(2,1)S(1)} %copy-done.5, bf16[224,1024]{1,0:T(8,128)(2,1)S(1)} %copy-done.9, ...), custom_call_target="tpu_custom_call" | custom-call | tf_op jit(solution)/shard_map/pallas_call | solution.py:204
  190.3 7.0 %shard_map.101 = (bf16[128,2048]{1,0:T(8,128)(2,1)S(1)}, f32[128,2048]{1,0:T(8,128)S(1)}) custom-call(s32[34]{0:T(128)S(1)} %pad_add_fusion.spots_ref, bf16[128,1920]{1,0:T(8,128)(2,1)S(1)} %concatenate.42.own_ref, bf16[128,1920]{1,0:T(8,128)(2,1)S(1)} %collective-permute-done.other_ref, bf16[16,112,1536]{2,1,0:T(8,128)(2,1)} %pad_maximum_fusion.a_ref, ...), custom_call_target="tpu_custom_call" | custom-call | tf_op jit(solution)/shard_map/pallas_call | solution.py:267
  200.8 2.0 collective-permute-start.27
  202.8 2.1 shard_map.103
  204.9 21.0 %collective-permute-done.27 = bf16[128,1792]{1,0:T(8,128)(2,1)S(1)} collective-permute-done((bf16[128,1792]{1,0:T(8,128)(2,1)S(1)}, bf16[128,1792]{1,0:T(8,128)(2,1)S(1)}, u32[]{:S(2)}, u32[]{:S(2)}) %collective-permute-start.27) | collective-permute-done | bytes 458784 | tf_op jit(solution)/shard_map/ppermute | solution.py:19
  227.6 2.5 collective-permute-start.30
  230.1 5.1 %shard_map.104 = bf16[128,1792]{1,0:T(8,128)(2,1)S(1)} custom-call(s32[34]{0:T(128)S(1)} %pad_add_fusion.spots_ref, bf16[128,1024]{1,0:T(8,128)(2,1)S(1)} %fusion.8.hid_ref, bf16[16,112,1536]{2,1,0:T(8,128)(2,1)} %pad_maximum_fusion.a_ref, bf16[16,112,1536]{2,1,0:T(8,128)(2,1)} %collective-permute-done.22.b_ref), custom_call_target="tpu_custom_call" | custom-call | tf_op jit(solution)/shard_map/pallas_call | solution.py:302
  235.3 1.7 fusion.7
  236.9 3.1 %collective-permute-done.29.hid_ref = bf16[128,1024]{1,0:T(8,128)(2,1)S(1)} collective-permute-done((bf16[128,1024]{1,0:T(8,128)(2,1)S(1)}, bf16[128,1024]{1,0:T(8,128)(2,1)S(1)}, u32[]{:S(2)}, u32[]{:S(2)}) %collective-permute-start.29) | collective-permute-done | bytes 262176 | tf_op jit(solution)/shard_map/ppermute | solution.py:19
  240.1 5.4 %collective-permute-done.30 = bf16[128,1792]{1,0:T(8,128)(2,1)S(1)} collective-permute-done((bf16[128,1792]{1,0:T(8,128)(2,1)S(1)}, bf16[128,1792]{1,0:T(8,128)(2,1)S(1)}, u32[]{:S(2)}, u32[]{:S(2)}) %collective-permute-start.30) | collective-permute-done | bytes 458784 | tf_op jit(solution)/shard_map/ppermute | solution.py:19
  245.7 5.1 %shard_map.105 = bf16[128,1792]{1,0:T(8,128)(2,1)S(1)} custom-call(s32[34]{0:T(128)S(1)} %pad_add_fusion.spots_ref, bf16[128,1024]{1,0:T(8,128)(2,1)S(1)} %collective-permute-done.29.hid_ref, bf16[16,112,1536]{2,1,0:T(8,128)(2,1)} %pad_maximum_fusion.a_ref, bf16[16,112,1536]{2,1,0:T(8,128)(2,1)} %collective-permute-done.22.b_ref), custom_call_target="tpu_custom_call" | custom-call | tf_op jit(solution)/shard_map/pallas_call | solution.py:302
  250.9 2.9 %collective-permute-start.33 = (bf16[128,1792]{1,0:T(8,128)(2,1)S(1)}, bf16[128,1792]{1,0:T(8,128)(2,1)S(1)}, u32[]{:S(2)}, u32[]{:S(2)}) collective-permute-start(bf16[128,1792]{1,0:T(8,128)(2,1)S(1)} %fusion.7), channel_id=1, source_target_pairs={{0,8},{1,9},{2,10},{3,11},{4,12},{5,13},{6,14},{7,15},{8,0},{9,1},... | collective-permute-start | bytes 1376264 | tf_op jit(solution)/shard_map/ppermute | solution.py:19
  253.8 7.8 %collective-permute-done.34 = bf16[128,1792]{1,0:T(8,128)(2,1)S(1)} collective-permute-done((bf16[128,1792]{1,0:T(8,128)(2,1)S(1)}, bf16[128,1792]{1,0:T(8,128)(2,1)S(1)}, u32[]{:S(2)}, u32[]{:S(2)}) %collective-permute-start.34) | collective-permute-done | bytes 458784 | tf_op jit(solution)/shard_map/ppermute | solution.py:19
  261.6 1.4 fusion.3
  263.0 9.7 %collective-permute-done.33 = bf16[128,1792]{1,0:T(8,128)(2,1)S(1)} collective-permute-done((bf16[128,1792]{1,0:T(8,128)(2,1)S(1)}, bf16[128,1792]{1,0:T(8,128)(2,1)S(1)}, u32[]{:S(2)}, u32[]{:S(2)}) %collective-permute-start.33) | collective-permute-done | bytes 458784 | tf_op jit(solution)/shard_map/ppermute | solution.py:19
  (115 shorter events, 27.3 us)
Async XLA Ops:
  0.0 13.0 %copy-start = (bf16[224,2048]{1,0:T(8,128)(2,1)S(1)}, bf16[224,2048]{1,0:T(8,128)(2,1)}, u32[]{:S(2)}) copy-start(bf16[224,2048]{1,0:T(8,128)(2,1)} %param.12) | copy-start | bytes 2752516
  3.9 9.2 %collective-permute-start.3 = (bf16[128,1920]{1,0:T(8,128)(2,1)S(1)}, bf16[128,1920]{1,0:T(8,128)(2,1)S(1)}, u32[]{:S(2)}, u32[]{:S(2)}) collective-permute-start(bf16[128,1920]{1,0:T(8,128)(2,1)S(1)} %concatenate.42.own_ref), channel_id=1, source_target_pairs={{0,1},{1,0},{2,3},{3,2},{4,5},{5,4},{6,7},{7,6},{8,9},{9,8},{10,11... | collective-permute-start | bytes 1474568 | tf_op jit(solution)/shard_map/ppermute | solution.py:19
  5.3 26.3 %collective-permute-start = (bf16[128,1920]{1,0:T(8,128)(2,1)}, bf16[128,1920]{1,0:T(8,128)(2,1)S(1)}, u32[]{:S(2)}, u32[]{:S(2)}) collective-permute-start(bf16[128,1920]{1,0:T(8,128)(2,1)} %concatenate.41), channel_id=1, source_target_pairs={{0,8},{1,9},{2,10},{3,11},{4,12},{5,13},{6,14},{7,15},{8,0},{9,1},... | collective-permute-start | bytes 1474568 | tf_op jit(solution)/shard_map/ppermute | solution.py:19
  8.9 22.7 %collective-permute-start.2 = (bf16[128,1920]{1,0:T(8,128)(2,1)S(1)}, bf16[128,1920]{1,0:T(8,128)(2,1)S(1)}, u32[]{:S(2)}, u32[]{:S(2)}) collective-permute-start(bf16[128,1920]{1,0:T(8,128)(2,1)S(1)} %concatenate.42.own_ref), channel_id=1, source_target_pairs={{0,2},{1,3},{2,0},{3,1},{4,6},{5,7},{6,4},{7,5},{8,10},{9,11},{10,... | collective-permute-start | bytes 1474568 | tf_op jit(solution)/shard_map/ppermute | solution.py:19
  10.4 22.5 %collective-permute-start.1 = (bf16[128,1920]{1,0:T(8,128)(2,1)S(1)}, bf16[128,1920]{1,0:T(8,128)(2,1)}, u32[]{:S(2)}, u32[]{:S(2)}) collective-permute-start(bf16[128,1920]{1,0:T(8,128)(2,1)S(1)} %concatenate.42.own_ref), channel_id=1, source_target_pairs={{0,4},{1,5},{2,6},{3,7},{4,0},{5,1},{6,2},{7,3},{8,12},{9,13},{10,... | collective-permute-start | bytes 1474568 | tf_op jit(solution)/shard_map/ppermute | solution.py:19
  13.1 5.6 %copy-start.6 = (bf16[128,1920]{1,0:T(8,128)(2,1)}, bf16[128,1920]{1,0:T(8,128)(2,1)S(1)}, u32[]{:S(2)}) copy-start(bf16[128,1920]{1,0:T(8,128)(2,1)S(1)} %collective-permute-done.3) | copy-start | bytes 1474564
  34.4 4.4 %collective-permute-start.7 = (bf16[2,128,1920]{2,1,0:T(8,128)(2,1)S(1)}, bf16[2,128,1920]{2,1,0:T(8,128)(2,1)S(1)}, u32[]{:S(2)}, u32[]{:S(2)}) collective-permute-start(bf16[2,128,1920]{2,1,0:T(8,128)(2,1)S(1)} %get-tuple-element.131.first_ref), channel_id=1, source_target_pairs={{0,1},{1,0},{2,3},{3,2},{4,5},{5,4},{6,7},{7,6},{8,9},{9,8},{10,11... | collective-permute-start | bytes 2949128 | tf_op jit(solution)/shard_map/ppermute | solution.py:19
  34.4 24.2 %collective-permute-start.6 = (bf16[2,128,1920]{2,1,0:T(8,128)(2,1)S(1)}, bf16[2,128,1920]{2,1,0:T(8,128)(2,1)S(1)}, u32[]{:S(2)}, u32[]{:S(2)}) collective-permute-start(bf16[2,128,1920]{2,1,0:T(8,128)(2,1)S(1)} %get-tuple-element.180), channel_id=1, source_target_pairs={{0,2},{1,3},{2,0},{3,1},{4,6},{5,7},{6,4},{7,5},{8,10},{9,11},{10,... | collective-permute-start | bytes 2949128 | tf_op jit(solution)/shard_map/ppermute | solution.py:19
  35.1 23.6 %collective-permute-start.5 = (bf16[128,1920]{1,0:T(8,128)(2,1)S(1)}, bf16[128,1920]{1,0:T(8,128)(2,1)S(1)}, u32[]{:S(2)}, u32[]{:S(2)}) collective-permute-start(bf16[128,1920]{1,0:T(8,128)(2,1)S(1)} %collective-permute-done.other_ref), channel_id=1, source_target_pairs={{0,4},{1,5},{2,6},{3,7},{4,0},{5,1},{6,2},{7,3},{8,12},{9,13},{10,... | collective-permute-start | bytes 1474568 | tf_op jit(solution)/shard_map/ppermute | solution.py:19
  36.5 22.2 %collective-permute-start.4 = (bf16[112,2048]{1,0:T(8,128)(2,1)S(1)}, bf16[112,2048]{1,0:T(8,128)(2,1)S(1)}, u32[]{:S(2)}, u32[]{:S(2)}) collective-permute-start(bf16[112,2048]{1,0:T(8,128)(2,1)S(1)} %shard_map.91), channel_id=1, source_target_pairs={{0,8},{1,9},{2,10},{3,11},{4,12},{5,13},{6,14},{7,15},{8,0},{9,1},... | collective-permute-start | bytes 1376264 | tf_op jit(solution)/shard_map/ppermute | solution.py:19
  38.7 6.5 %copy-start.4 = (bf16[2,128,1920]{2,1,0:T(8,128)(2,1)}, bf16[2,128,1920]{2,1,0:T(8,128)(2,1)S(1)}, u32[]{:S(2)}) copy-start(bf16[2,128,1920]{2,1,0:T(8,128)(2,1)S(1)} %collective-permute-done.7.second_ref) | copy-start | bytes 2949124
  59.0 33.0 %collective-permute-start.10 = (bf16[4,128,1920]{2,1,0:T(8,128)(2,1)S(1)}, bf16[4,128,1920]{2,1,0:T(8,128)(2,1)S(1)}, u32[]{:S(2)}, u32[]{:S(2)}) collective-permute-start(bf16[4,128,1920]{2,1,0:T(8,128)(2,1)S(1)} %pad_maximum_fusion.1), channel_id=1, source_target_pairs={{0,1},{1,0},{2,3},{3,2},{4,5},{5,4},{6,7},{7,6},{8,9},{9,8},{10,11... | collective-permute-start | bytes 5898248 | tf_op jit(solution)/shard_map/ppermute | solution.py:19
  59.1 31.9 %collective-permute-start.11 = (bf16[1,224,1536]{2,1,0:T(8,128)(2,1)S(1)}, bf16[1,224,1536]{2,1,0:T(8,128)(2,1)S(1)}, u32[]{:S(2)}, u32[]{:S(2)}) collective-permute-start(bf16[1,224,1536]{2,1,0:T(8,128)(2,1)S(1)} %maximum_bitcast_fusion), channel_id=1, source_target_pairs={{0,4},{1,5},{2,6},{3,7},{4,0},{5,1},{6,2},{7,3},{8,12},{9,13},{10,... | collective-permute-start | bytes 2064392 | tf_op jit(solution)/shard_map/ppermute | solution.py:19
  60.6 43.4 %collective-permute-start.8 = (bf16[224,2048]{1,0:T(8,128)(2,1)S(1)}, bf16[224,2048]{1,0:T(8,128)(2,1)S(1)}, u32[]{:S(2)}, u32[]{:S(2)}) collective-permute-start(bf16[224,2048]{1,0:T(8,128)(2,1)S(1)} %shard_map.92), channel_id=1, source_target_pairs={{0,8},{1,9},{2,10},{3,11},{4,12},{5,13},{6,14},{7,15},{8,0},{9,1},... | collective-permute-start | bytes 2752520 | tf_op jit(solution)/shard_map/ppermute | solution.py:19
  91.2 12.9 %collective-permute-start.9 = (bf16[128,1920]{1,0:T(8,128)(2,1)S(1)}, bf16[128,1920]{1,0:T(8,128)(2,1)S(1)}, u32[]{:S(2)}, u32[]{:S(2)}) collective-permute-start(bf16[128,1920]{1,0:T(8,128)(2,1)S(1)} %collective-permute-done.5), channel_id=1, source_target_pairs={{0,2},{1,3},{2,0},{3,1},{4,6},{5,7},{6,4},{7,5},{8,10},{9,11},{10,... | collective-permute-start | bytes 1474568 | tf_op jit(solution)/shard_map/ppermute | solution.py:19
  105.2 18.1 %collective-permute-start.16 = (bf16[2,112,1536]{2,1,0:T(8,128)(2,1)}, bf16[2,112,1536]{2,1,0:T(8,128)(2,1)}, u32[]{:S(2)}, u32[]{:S(2)}) collective-permute-start(bf16[2,112,1536]{2,1,0:T(8,128)(2,1)} %get-tuple-element.169), channel_id=1, source_target_pairs={{0,2},{1,3},{2,0},{3,1},{4,6},{5,7},{6,4},{7,5},{8,10},{9,11},{10,... | collective-permute-start | bytes 2064392 | tf_op jit(solution)/shard_map/ppermute | solution.py:19
  105.9 19.1 %collective-permute-start.15 = (bf16[2,112,1536]{2,1,0:T(8,128)(2,1)}, bf16[2,112,1536]{2,1,0:T(8,128)(2,1)}, u32[]{:S(2)}, u32[]{:S(2)}) collective-permute-start(bf16[2,112,1536]{2,1,0:T(8,128)(2,1)} %get-tuple-element.170), channel_id=1, source_target_pairs={{0,16},{16,0},{1,17},{17,1},{2,18},{18,2},{3,19},{19,3},{4,20},{20... | collective-permute-start | bytes 2064392 | tf_op jit(solution)/shard_map/ppermute | solution.py:19
  107.5 21.9 %collective-permute-start.13 = (bf16[112,1024]{1,0:T(8,128)(2,1)S(1)}, bf16[112,1024]{1,0:T(8,128)(2,1)S(1)}, u32[]{:S(2)}, u32[]{:S(2)}) collective-permute-start(bf16[112,1024]{1,0:T(8,128)(2,1)S(1)} %shard_map.94.hid_ref), channel_id=1, source_target_pairs={{0,8},{1,9},{2,10},{3,11},{4,12},{5,13},{6,14},{7,15},{8,0},{9,1},... | collective-permute-start | bytes 688136 | tf_op jit(solution)/shard_map/ppermute | solution.py:19
  108.7 30.2 %collective-permute-start.12 = (bf16[112,2048]{1,0:T(8,128)(2,1)S(1)}, bf16[112,2048]{1,0:T(8,128)(2,1)S(1)}, u32[]{:S(2)}, u32[]{:S(2)}) collective-permute-start(bf16[112,2048]{1,0:T(8,128)(2,1)S(1)} %shard_map.93), channel_id=1, source_target_pairs={{0,8},{1,9},{2,10},{3,11},{4,12},{5,13},{6,14},{7,15},{8,0},{9,1},... | collective-permute-start | bytes 1376264 | tf_op jit(solution)/shard_map/ppermute | solution.py:19
  110.4 28.5 %collective-permute-start.14 = (bf16[1,128,1920]{2,1,0:T(8,128)(2,1)S(1)}, bf16[1,128,1920]{2,1,0:T(8,128)(2,1)S(1)}, u32[]{:S(2)}, u32[]{:S(2)}) collective-permute-start(bf16[1,128,1920]{2,1,0:T(8,128)(2,1)S(1)} %bitcast.60), channel_id=1, source_target_pairs={{0,1},{1,0},{2,3},{3,2},{4,5},{5,4},{6,7},{7,6},{8,9},{9,8},{10,11... | collective-permute-start | bytes 1474568 | tf_op jit(solution)/shard_map/ppermute | solution.py:19
  116.7 4.5 %copy-start.2 = (bf16[1024,1792]{1,0:T(8,128)(2,1)S(1)}, bf16[1024,1792]{1,0:T(8,128)(2,1)}, u32[]{:S(2)}) copy-start(bf16[1024,1792]{1,0:T(8,128)(2,1)} %w_ref.17) | copy-start | bytes 11010052
  123.3 4.1 %copy-start.10 = (bf16[1,128,1792]{2,1,0:T(8,128)(2,1)}, bf16[1,128,1792]{2,1,0:T(8,128)(2,1)S(1)}, u32[]{:S(2)}) copy-start(bf16[1,128,1792]{2,1,0:T(8,128)(2,1)S(1)} %get-tuple-element.151) | copy-start | bytes 1376260
  138.9 32.2 %collective-permute-start.19 = (bf16[4,112,1536]{2,1,0:T(8,128)(2,1)}, bf16[4,112,1536]{2,1,0:T(8,128)(2,1)}, u32[]{:S(2)}, u32[]{:S(2)}) collective-permute-start(bf16[4,112,1536]{2,1,0:T(8,128)(2,1)} %pad_maximum_fusion.3), channel_id=1, source_target_pairs={{0,2},{1,3},{2,0},{3,1},{4,6},{5,7},{6,4},{7,5},{8,10},{9,11},{10,... | collective-permute-start | bytes 4128776 | tf_op jit(solution)/shard_map/ppermute | solution.py:19
  140.1 31.9 %collective-permute-start.20 = (bf16[4,112,1536]{2,1,0:T(8,128)(2,1)S(1)}, bf16[4,112,1536]{2,1,0:T(8,128)(2,1)}, u32[]{:S(2)}, u32[]{:S(2)}) collective-permute-start(bf16[4,112,1536]{2,1,0:T(8,128)(2,1)S(1)} %pad_maximum_fusion.4), channel_id=1, source_target_pairs={{0,16},{16,0},{1,17},{17,1},{2,18},{18,2},{3,19},{19,3},{4,20},{20... | collective-permute-start | bytes 4128776 | tf_op jit(solution)/shard_map/ppermute | solution.py:19
  141.9 35.6 %collective-permute-start.18 = (bf16[3,128,1792]{2,1,0:T(8,128)(2,1)}, bf16[3,128,1792]{2,1,0:T(8,128)(2,1)S(1)}, u32[]{:S(2)}, u32[]{:S(2)}) collective-permute-start(bf16[3,128,1792]{2,1,0:T(8,128)(2,1)} %pad_maximum_fusion.5), channel_id=1, source_target_pairs={{0,1},{1,0},{2,3},{3,2},{4,5},{5,4},{6,7},{7,6},{8,9},{9,8},{10,11... | collective-permute-start | bytes 4128776 | tf_op jit(solution)/shard_map/ppermute | solution.py:19
  147.3 2.9 %copy-start.7 = (bf16[128,1920]{1,0:T(8,128)(2,1)S(1)}, bf16[128,1920]{1,0:T(8,128)(2,1)}, u32[]{:S(2)}) copy-start(bf16[128,1920]{1,0:T(8,128)(2,1)} %copy-done.6) | copy-start | bytes 1474564
  150.2 27.3 %collective-permute-start.17 = (bf16[224,1024]{1,0:T(8,128)(2,1)S(1)}, bf16[224,1024]{1,0:T(8,128)(2,1)S(1)}, u32[]{:S(2)}, u32[]{:S(2)}) collective-permute-start(bf16[224,1024]{1,0:T(8,128)(2,1)S(1)} %shard_map.95.hid_ref), channel_id=1, source_target_pairs={{0,8},{1,9},{2,10},{3,11},{4,12},{5,13},{6,14},{7,15},{8,0},{9,1},... | collective-permute-start | bytes 1376264 | tf_op jit(solution)/shard_map/ppermute | solution.py:19
  152.3 25.2 %copy-start.12 = (bf16[1,128,1792]{2,1,0:T(8,128)(2,1)}, bf16[1,128,1792]{2,1,0:T(8,128)(2,1)S(1)}, u32[]{:S(2)}) copy-start(bf16[1,128,1792]{2,1,0:T(8,128)(2,1)S(1)} %get-tuple-element.160) | copy-start | bytes 1376260
  177.5 12.8 %collective-permute-start.22 = (bf16[16,112,1536]{2,1,0:T(8,128)(2,1)}, bf16[16,112,1536]{2,1,0:T(8,128)(2,1)}, u32[]{:S(2)}, u32[]{:S(2)}) collective-permute-start(bf16[16,112,1536]{2,1,0:T(8,128)(2,1)} %pad_maximum_fusion.a_ref), channel_id=1, source_target_pairs={{0,1},{1,0},{2,3},{3,2},{4,5},{5,4},{6,7},{7,6},{8,9},{9,8},{10,11... | collective-permute-start | bytes 16515080 | tf_op jit(solution)/shard_map/ppermute | solution.py:19
  178.7 4.9 %copy-start.17 = (s32[16]{0:T(128)S(1)}, s32[16]{0:T(128)}, u32[]{:S(2)}) copy-start(s32[16]{0:T(128)} %constant.44.clone) | copy-start | bytes 196
  178.7 19.8 %collective-permute-start.25 = (bf16[2,128,1792]{2,1,0:T(8,128)(2,1)}, bf16[2,128,1792]{2,1,0:T(8,128)(2,1)}, u32[]{:S(2)}, u32[]{:S(2)}) collective-permute-start(bf16[2,128,1792]{2,1,0:T(8,128)(2,1)} %pad_maximum_fusion.9), channel_id=1, source_target_pairs={{0,1},{1,0},{2,3},{3,2},{4,5},{5,4},{6,7},{7,6},{8,9},{9,8},{10,11... | collective-permute-start | bytes 2752520 | tf_op jit(solution)/shard_map/ppermute | solution.py:19
  180.3 16.9 %collective-permute-start.24 = (bf16[128,1792]{1,0:T(8,128)(2,1)}, bf16[128,1792]{1,0:T(8,128)(2,1)}, u32[]{:S(2)}, u32[]{:S(2)}) collective-permute-start(bf16[128,1792]{1,0:T(8,128)(2,1)} %get-tuple-element.175), channel_id=1, source_target_pairs={{0,2},{1,3},{2,0},{3,1},{4,6},{5,7},{6,4},{7,5},{8,10},{9,11},{10,... | collective-permute-start | bytes 1376264 | tf_op jit(solution)/shard_map/ppermute | solution.py:19
  181.0 17.5 %collective-permute-start.23 = (bf16[128,1792]{1,0:T(8,128)(2,1)}, bf16[128,1792]{1,0:T(8,128)(2,1)}, u32[]{:S(2)}, u32[]{:S(2)}) collective-permute-start(bf16[128,1792]{1,0:T(8,128)(2,1)} %get-tuple-element.176), channel_id=1, source_target_pairs={{0,4},{1,5},{2,6},{3,7},{4,0},{5,1},{6,2},{7,3},{8,12},{9,13},{10,... | collective-permute-start | bytes 1376264 | tf_op jit(solution)/shard_map/ppermute | solution.py:19
  181.0 16.3 %collective-permute-start.21 = (bf16[112,1024]{1,0:T(8,128)(2,1)S(1)}, bf16[112,1024]{1,0:T(8,128)(2,1)S(1)}, u32[]{:S(2)}, u32[]{:S(2)}) collective-permute-start(bf16[112,1024]{1,0:T(8,128)(2,1)S(1)} %shard_map.98.hid_ref), channel_id=1, source_target_pairs={{0,8},{1,9},{2,10},{3,11},{4,12},{5,13},{6,14},{7,15},{8,0},{9,1},... | collective-permute-start | bytes 688136 | tf_op jit(solution)/shard_map/ppermute | solution.py:19
  190.3 9.4 %copy-start.15 = (bf16[1,128,1792]{2,1,0:T(8,128)(2,1)S(1)}, bf16[1,128,1792]{2,1,0:T(8,128)(2,1)}, u32[]{:S(2)}) copy-start(bf16[1,128,1792]{2,1,0:T(8,128)(2,1)} %copy-done.14) | copy-start | bytes 1376260
  190.3 12.5 %copy-start.3 = (bf16[1024,1792]{1,0:T(8,128)(2,1)S(1)}, bf16[1024,1792]{1,0:T(8,128)(2,1)}, u32[]{:S(2)}) copy-start(bf16[1024,1792]{1,0:T(8,128)(2,1)} %w_ref.17) | copy-start | bytes 11010052
  198.5 27.4 %collective-permute-start.26 = (bf16[128,2048]{1,0:T(8,128)(2,1)S(1)}, bf16[128,2048]{1,0:T(8,128)(2,1)S(1)}, u32[]{:S(2)}, u32[]{:S(2)}) collective-permute-start(bf16[128,2048]{1,0:T(8,128)(2,1)S(1)} %get-tuple-element.137), channel_id=1, source_target_pairs={{0,8},{1,9},{2,10},{3,11},{4,12},{5,13},{6,14},{7,15},{8,0},{9,1},... | collective-permute-start | bytes 1572872 | tf_op jit(solution)/shard_map/ppermute | solution.py:19
  199.6 26.2 %collective-permute-start.28 = (bf16[2,128,1792]{2,1,0:T(8,128)(2,1)S(1)}, bf16[2,128,1792]{2,1,0:T(8,128)(2,1)S(1)}, u32[]{:S(2)}, u32[]{:S(2)}) collective-permute-start(bf16[2,128,1792]{2,1,0:T(8,128)(2,1)S(1)} %get-tuple-element.142), channel_id=1, source_target_pairs={{0,1},{1,0},{2,3},{3,2},{4,5},{5,4},{6,7},{7,6},{8,9},{9,8},{10,11... | collective-permute-start | bytes 2752520 | tf_op jit(solution)/shard_map/ppermute | solution.py:19
  200.8 25.0 %collective-permute-start.27 = (bf16[128,1792]{1,0:T(8,128)(2,1)S(1)}, bf16[128,1792]{1,0:T(8,128)(2,1)S(1)}, u32[]{:S(2)}, u32[]{:S(2)}) collective-permute-start(bf16[128,1792]{1,0:T(8,128)(2,1)S(1)} %fusion.9), channel_id=1, source_target_pairs={{0,6},{1,7},{2,4},{3,5},{4,2},{5,3},{6,0},{7,1},{8,14},{9,15},{10,... | collective-permute-start | bytes 1376264 | tf_op jit(solution)/shard_map/ppermute | solution.py:19
  226.4 13.7 %collective-permute-start.29 = (bf16[128,1024]{1,0:T(8,128)(2,1)S(1)}, bf16[128,1024]{1,0:T(8,128)(2,1)S(1)}, u32[]{:S(2)}, u32[]{:S(2)}) collective-permute-start(bf16[128,1024]{1,0:T(8,128)(2,1)S(1)} %fusion.8.hid_ref), channel_id=1, source_target_pairs={{0,8},{1,9},{2,10},{3,11},{4,12},{5,13},{6,14},{7,15},{8,0},{9,1},... | collective-permute-start | bytes 786440 | tf_op jit(solution)/shard_map/ppermute | solution.py:19
  226.5 13.6 %collective-permute-start.31 = (bf16[128,1792]{1,0:T(8,128)(2,1)S(1)}, bf16[128,1792]{1,0:T(8,128)(2,1)S(1)}, u32[]{:S(2)}, u32[]{:S(2)}) collective-permute-start(bf16[128,1792]{1,0:T(8,128)(2,1)S(1)} %get-tuple-element.173), channel_id=1, source_target_pairs={{0,2},{1,3},{2,0},{3,1},{4,6},{5,7},{6,4},{7,5},{8,10},{9,11},{10,... | collective-permute-start | bytes 1376264 | tf_op jit(solution)/shard_map/ppermute | solution.py:19
  227.6 7.6 %copy-start.11 = (bf16[1,128,1792]{2,1,0:T(8,128)(2,1)S(1)}, bf16[1,128,1792]{2,1,0:T(8,128)(2,1)}, u32[]{:S(2)}) copy-start(bf16[1,128,1792]{2,1,0:T(8,128)(2,1)} %copy-done.10) | copy-start | bytes 1376260
  227.6 17.9 %collective-permute-start.30 = (bf16[128,1792]{1,0:T(8,128)(2,1)S(1)}, bf16[128,1792]{1,0:T(8,128)(2,1)S(1)}, u32[]{:S(2)}, u32[]{:S(2)}) collective-permute-start(bf16[128,1792]{1,0:T(8,128)(2,1)S(1)} %get-tuple-element.174), channel_id=1, source_target_pairs={{0,4},{1,5},{2,6},{3,7},{4,0},{5,1},{6,2},{7,3},{8,12},{9,13},{10,... | collective-permute-start | bytes 1376264 | tf_op jit(solution)/shard_map/ppermute | solution.py:19
  230.1 15.4 %collective-permute-start.32 = (bf16[1,128,1792]{2,1,0:T(8,128)(2,1)S(1)}, bf16[1,128,1792]{2,1,0:T(8,128)(2,1)S(1)}, u32[]{:S(2)}, u32[]{:S(2)}) collective-permute-start(bf16[1,128,1792]{2,1,0:T(8,128)(2,1)S(1)} %get-tuple-element.157), channel_id=1, source_target_pairs={{0,1},{1,0},{2,3},{3,2},{4,5},{5,4},{6,7},{7,6},{8,9},{9,8},{10,11... | collective-permute-start | bytes 1376264 | tf_op jit(solution)/shard_map/ppermute | solution.py:19
  245.6 16.0 %copy-start.13 = (bf16[1,128,1792]{2,1,0:T(8,128)(2,1)S(1)}, bf16[1,128,1792]{2,1,0:T(8,128)(2,1)}, u32[]{:S(2)}) copy-start(bf16[1,128,1792]{2,1,0:T(8,128)(2,1)} %copy-done.12) | copy-start | bytes 1376260
  245.6 15.9 %collective-permute-start.34 = (bf16[128,1792]{1,0:T(8,128)(2,1)S(1)}, bf16[128,1792]{1,0:T(8,128)(2,1)S(1)}, u32[]{:S(2)}, u32[]{:S(2)}) collective-permute-start(bf16[128,1792]{1,0:T(8,128)(2,1)S(1)} %fusion.10), channel_id=1, source_target_pairs={{0,6},{1,7},{2,4},{3,5},{4,2},{5,3},{6,0},{7,1},{8,14},{9,15},{10,... | collective-permute-start | bytes 1376264 | tf_op jit(solution)/shard_map/ppermute | solution.py:19
  245.7 28.2 %copy-start.1 = (bf16[224,2048]{1,0:T(8,128)(2,1)S(1)}, bf16[224,2048]{1,0:T(8,128)(2,1)}, u32[]{:S(2)}) copy-start(bf16[224,2048]{1,0:T(8,128)(2,1)} %param.12) | copy-start | bytes 2752516
  250.9 21.8 %collective-permute-start.33 = (bf16[128,1792]{1,0:T(8,128)(2,1)S(1)}, bf16[128,1792]{1,0:T(8,128)(2,1)S(1)}, u32[]{:S(2)}, u32[]{:S(2)}) collective-permute-start(bf16[128,1792]{1,0:T(8,128)(2,1)S(1)} %fusion.7), channel_id=1, source_target_pairs={{0,8},{1,9},{2,10},{3,11},{4,12},{5,13},{6,14},{7,15},{8,0},{9,1},... | collective-permute-start | bytes 1376264 | tf_op jit(solution)/shard_map/ppermute | solution.py:19
  (5 other events, 6.6 us)

commit v3 on v2

--- a/solution.py
+++ b/solution.py
@@ -224,31 +224,32 @@
 
 
 def assemble(masks, first_column, spots_ref, stack_refs, out_ref, sems):
-    count, rows, _ = stack_refs[0].shape
+    count = len(masks)
     columns = out_ref.shape[1] // len({q for _, _, q in masks})
+    shard_rows = out_ref.shape[0] // len({m for _, m, _ in masks}) // 2
+    places = [(ref, i) for ref in stack_refs for i in range(ref.shape[0])]
     copies = []
-    for core, stack_ref in enumerate(stack_refs):
-        for i, (upper, _, q) in enumerate(masks):
-            shard = spots_ref[core * count + i]
-            row = pl.multiple_of(shard * 2 * rows + upper * rows, rows)
-            column = pl.multiple_of(spots_ref[2 * count + q] * columns, columns)
-            copies.append(
-                pltpu.make_async_copy(
-                    stack_ref.at[i, :, pl.ds(first_column, columns)],
-                    out_ref.at[pl.ds(row, rows), pl.ds(column, columns)],
-                    sems.at[len(copies)],
-                )
+    for at, (stack_ref, i) in enumerate(places):
+        upper, _, q = masks[at % count]
+        rows = stack_ref.shape[1]
+        row = pl.multiple_of(spots_ref[at] * shard_rows + upper * rows, rows)
+        column = pl.multiple_of(spots_ref[2 * count + q] * columns, columns)
+        copies.append(
+            pltpu.make_async_copy(
+                stack_ref.at[i, :, pl.ds(first_column, columns)],
+                out_ref.at[pl.ds(row, rows), pl.ds(column, columns)],
+                sems.at[at],
             )
+        )
     for copy in copies:
         copy.start()
     for copy in copies:
         copy.wait()
 
 
-def shared_gate_kernel(
-    masks, spots_ref, own_ref, other_ref, a_ref, b_ref, mine_ref, theirs_ref, w_ref, sems
-):
-    assemble(masks, 0, spots_ref, (a_ref, b_ref), w_ref, sems)
+def shared_gate_kernel(masks, spots_ref, own_ref, other_ref, *refs):
+    stack_refs, (mine_ref, theirs_ref, w_ref, sems) = refs[:-4], refs[-4:]
+    assemble(masks, 0, spots_ref, stack_refs, w_ref, sems)
     width, columns = w_ref.shape
     step = 512
 
@@ -266,7 +267,7 @@
     hbm = pl.BlockSpec(memory_space=pl.ANY)
     return pl.pallas_call(
         functools.partial(shared_gate_kernel, masks),
-        in_specs=[smem(), vmem, vmem, hbm, hbm],
+        in_specs=[smem(), vmem, vmem] + [hbm] * len(stacks),
         out_specs=[vmem, vmem],
         out_shape=[
             jax.ShapeDtypeStruct((rows, columns), bf16),
@@ -281,10 +282,9 @@
     )(spots, own, other, *stacks)
 
 
-def shared_down_kernel(
-    masks, first_column, spots_ref, hid_ref, a_ref, b_ref, out_ref, d_ref, sems
-):
-    assemble(masks, first_column, spots_ref, (a_ref, b_ref), d_ref, sems)
+def shared_down_kernel(masks, first_column, spots_ref, hid_ref, *refs):
+    stack_refs, (out_ref, d_ref, sems) = refs[:-3], refs[-3:]
+    assemble(masks, first_column, spots_ref, stack_refs, d_ref, sems)
     step = 256
 
     @pl.loop(0, d_ref.shape[0] // step)
@@ -301,7 +301,7 @@
     hbm = pl.BlockSpec(memory_space=pl.ANY)
     return pl.pallas_call(
         functools.partial(shared_down_kernel, masks, first_column),
-        in_specs=[smem(), vmem, hbm, hbm],
+        in_specs=[smem(), vmem] + [hbm] * len(stacks),
         out_specs=vmem,
         out_shape=jax.ShapeDtypeStruct((rows, width), bf16),
         scratch_shapes=[
@@ -315,18 +315,31 @@
 
 def in_order(masks, place, group_index, stacks):
     groups = len({q for _, _, q in masks})
-    shards = len(masks) // groups
+    shards = 2 * len({m for _, m, _ in masks})
+    rows = min(stack.shape[1] for stack in stacks)
+    pieces = [
+        (stack[i : i + 1, at : at + rows], i_mask, stack.shape[1] > rows and at > 0)
+        for stack, i, i_mask in numbered(masks, stacks)
+        for at in range(0, stack.shape[1], rows)
+    ]
     spot = {}
-    for core in (0, 1):
-        for i, (upper, m, q) in enumerate(masks):
-            spot[m | core, upper, q] = core * len(masks) + i
+    for number, (_, (core, upper, m, q), second) in enumerate(pieces):
+        spot[m | core, 1 if second else upper, q] = number
     table = [[[spot[m, u, q] for q in range(groups)] for u in (0, 1)] for m in range(shards)]
     table = jnp.array(table, jnp.int32)
     table = table[jnp.arange(shards, dtype=jnp.int32) ^ place]
     table = table[:, :, jnp.arange(groups, dtype=jnp.int32) ^ group_index]
-    parts = jnp.concatenate(stacks)[table]
+    parts = jnp.concatenate([piece for piece, _, _ in pieces])[table]
     parts = parts.transpose(0, 1, 3, 2, 4)
     return parts.reshape(shards, -1, groups, parts.shape[-1])
+
+
+def numbered(masks, stacks):
+    places = [(stack, i) for stack in stacks for i in range(stack.shape[0])]
+    count = len(masks)
+    return [
+        (stack, i, (at // count,) + masks[at % count]) for at, (stack, i) in enumerate(places)
+    ]
 
 
 def local(
@@ -399,7 +412,7 @@
             total = total + part.astype(f32)
         return total.astype(bf16)
 
-    low_bit = near_chips[-1]
+    low_bit, later_bits = near_chips[-1], near_chips[:-1]
     group_bits = [1 << i for i in range(groups.bit_length() - 1)]
     gate_columns = 2 * units // groups
     down_rows = units // groups
@@ -422,12 +435,11 @@
             masks = masks + [(a ^ m, b ^ q) for a, b in masks]
         return [(upper, a, b) for a, b in masks]
 
-    far_steps = [(m, 0) for m in near_chips[:-1]]
-    group_steps = [(0, q) for q in group_bits]
-    low_steps = [(low_bit, 0)]
-    masks = masks_of(0, far_steps + group_steps + low_steps) + masks_of(
-        1, far_steps + low_steps + group_steps
-    )
+    start_masks = masks_of(0, [(m, 0) for m in later_bits])
+    all_groups = masks_of(0, [(m, 0) for m in later_bits] + [(0, q) for q in group_bits])
+    other_groups = all_groups[len(start_masks) :]
+    masks = start_masks + other_groups + [(0, m ^ low_bit, q) for _, m, q in start_masks]
+    masks += [(upper, m ^ low_bit, q) for upper in (0, 1) for _, m, q in other_groups]
     place = dev_index % half
     chip_masks = jnp.array([m for _, m, _ in masks], jnp.int32)
     spots = jnp.concatenate(
@@ -491,7 +503,7 @@
     far_tok = mixed[cut:], others[cut:]
     far_sums = sums_of(far_tok)
     away_own_hidden = hidden_of(away_own_tok, own_in)
-    weights = doubled(weights, near_chips[:-1])
+    weights = doubled(weights, later_bits)
     (
         near_in, away_far, away_near_tok, away_own_tok, far_tok, far_sums, away_own_hidden, weights
     ) = settle(
@@ -505,31 +517,39 @@
     away_near_hidden = hidden_of(away_near_tok, near_in)
     away_own_rows = rows_of(away_own_tok, away_own_hidden)
     away_near_rows = rows_of(away_near_tok, away_near_hidden)
-    lower = doubled(weights[:, :upper_row], group_bits, "groups")
-    upper = doubled(weights[:, upper_row:], [low_bit])
+    by_group = doubled(weights, group_bits, "groups")[weights.shape[0] :]
+    by_chip = hop(weights, low_bit)
     (
         far_in, own_hidden, away_far_tok, away_near_hidden, away_own_rows, away_near_rows,
-        lower, upper,
+        by_group, by_chip,
     ) = settle(
         far_in, own_hidden, away_far_tok, away_near_hidden, away_own_rows, away_near_rows,
-        lower, upper,
+        by_group, by_chip,
     )
 
     near_hidden = hop(away_near_hidden, half)
     away_others = hop(jnp.concatenate([away_own_rows[1], away_near_rows[1]]), 1)
+    lower = hop(by_group[:, :upper_row], low_bit)
+    upper = doubled(by_chip[:, upper_row:], group_bits, "groups")[by_chip.shape[0] :]
+    first = jnp.concatenate([weights, by_group, by_chip])
+    first_other = hop(first, 1)
+    far_in, own_hidden, away_others = settle(far_in, own_hidden, away_others)
     away_far_hidden = hidden_of(away_far_tok, far_in)
     away_far_rows = rows_of(away_far_tok, away_far_hidden)
     own_rows = rows_of(own_tok, own_hidden)
-    lower = doubled(lower, [low_bit])
-    upper = doubled(upper, group_bits, "groups")
-    weights = jnp.concatenate([lower, upper])
-    near_hidden, away_others, away_far_hidden, away_far_rows, own_rows, weights = settle(
-        near_hidden, away_others, away_far_hidden, away_far_rows, own_rows, weights
+    (
+        near_hidden, away_others, away_far_hidden, away_far_rows, own_rows, first, first_other,
+        lower, upper,
+    ) = settle(
+        near_hidden, away_others, away_far_hidden, away_far_rows, own_rows, first, first_other,
+        lower, upper,
     )
 
     far_hidden = hop(away_far_hidden, half)
-    stacks = weights, hop(weights, 1)
+    second = jnp.concatenate([lower, upper])
+    stacks = first, second, first_other, hop(second, 1)
     shared_own, shared_other = shared_sums(stacks)
+    near_hidden, shared_own = settle(near_hidden, shared_own)
     parts = hops_of(summed(away_near_rows[0], away_others[1:]), near_chips)
     others = hop(jnp.concatenate([own_rows[1], away_far_rows[1]]), 1)
     near_rows = rows_of(near_tok, near_hidden)
@@ -550,11 +570,8 @@
     away_rows = finished(shared_out, away_own_rows[0], away_others[0], parts)
     parts = hops_of(summed(near_rows[0], near_others), near_chips)
     far_others = hop(far_rows[1], 1)
-    shared_hidden, away_rows, parts, far_others = settle(
-        shared_hidden, away_rows, parts, far_others
-    )
-
     far_half = hop(away_rows, half)
+    shared_hidden, parts[-1] = settle(shared_hidden, parts[-1])
     parts += hops_of(summed(far_rows[0], far_others), far_chips)
     shared_out = shared_down_of(shared_hidden, stacks)
     near_half = finished(shared_out, own_rows[0], others[0], parts)

time: 275 us -> 263 us (0.956)
  other arithmetic: 23.7 us -> 12.7 us
  waiting for transfers between devices: 137 us -> 130 us
  local copies, waits for them, and re-layouts: 7.84 us -> 13.2 us
    ppermute x35 -> x36, waiting for transfers between devices: 137 us -> 130 us  [hop(): return lax.ppermute(block, axis, [(d, d ^ mask) for d in range(count)])]
    concatenate x1 -> x0, other arithmetic: 5.46 us -> none  [local(): weights = jnp.concatenate([lower, upper])]
    concatenate x3 -> x1, other arithmetic: 4.24 us -> 0.13 us  [doubled(): stack = jnp.concatenate([stack, hop(stack, bit, axis)])]
    ppermute x35 -> x36, starting transfers between devices: 36.1 us -> 36.8 us  [hop(): return lax.ppermute(block, axis, [(d, d ^ mask) for d in range(count)])]
  transfers between devices with their start and end apart: 35 -> 36, of which waited for: 15 -> 14; matrix products, arithmetic and copies ran while one was open for 7% -> 5% of each run, Pallas kernels for 25% -> 26%
where the time goes in v3:
time: 263 us; the launch traced here: 262 us
  waiting for transfers between devices  130 us (49%)
  Pallas kernels  68.6 us (26%)
  starting transfers between devices  36.8 us (14%)
  local copies, waits for them, and re-layouts  13.2 us (5%)
  other arithmetic  12.7 us (5%)
    ppermute x36, waiting for transfers between devices, hop(): return lax.ppermute(block, axis, [(d, d ^ mask) for d in range(count)])  130 us
    ppermute x36, starting transfers between devices, hop(): return lax.ppermute(block, axis, [(d, d ^ mask) for d in range(count)])  36.8 us
    pallas_call x3, Pallas kernels, hidden_rows(): pl.pallas_call(functools.partial(hidden_kernel, cap), grid=(steps,), in_s...  17.6 us
    pallas_call x3, Pallas kernels, partial_sums(): pl.pallas_call(functools.partial(partial_kernel, cap), grid=(steps,), in_...  17.4 us
    pallas_call x6, Pallas kernels, weighted_rows(): pl.pallas_call(functools.partial(down_kernel, cap), grid=(steps,), in_spe...  17.4 us
    pallas_call x2, Pallas kernels, shared_rows(): pl.pallas_call(functools.partial(shared_down_kernel, masks, first_column)...  9.86 us
    pallas_call x1, Pallas kernels, shared_partial(): pl.pallas_call(functools.partial(shared_gate_kernel, masks), in_specs=[sm...  6.35 us
  transfers between devices with their start and end apart: 36, of which 14 were waited for; matrix products, arithmetic and copies ran while one was open for 5% of the time, Pallas kernels for 26%

profile of v3, /device:TPU:0, one launch (start us, length us, event | category | flops | bytes accessed | tf_op | source)
XLA Modules:
  0.0 262.4 jit_solution(16769982747423481014)
XLA Ops:
  4.6 3.7 %collective-permute-start = (bf16[128,1920]{1,0:T(8,128)(2,1)S(1)}, bf16[128,1920]{1,0:T(8,128)(2,1)S(1)}, u32[]{:S(2)}, u32[]{:S(2)}) collective-permute-start(bf16[128,1920]{1,0:T(8,128)(2,1)S(1)} %concatenate.39), channel_id=1, source_target_pairs={{0,8},{1,9},{2,10},{3,11},{4,12},{5,13},{6,14},{7,15},{8,0},{9,1},... | collective-permute-start | bytes 1474568 | tf_op jit(solution)/shard_map/ppermute | solution.py:19
  8.2 1.5 collective-permute-start.2
  9.7 1.6 collective-permute-start.1
  12.4 5.4 %shard_map.91 = bf16[112,2048]{1,0:T(8,128)(2,1)S(1)} custom-call(s32[1]{0:T(128)} %bitcast.4.pair_ref, bf16[1,128,1920]{2,1,0:T(8,128)(2,1)S(1)} %bitcast.53, bf16[1,128,1920]{2,1,0:T(8,128)(2,1)S(1)} %bitcast.58, bf16[1792,2048]{1,0:T(8,128)(2,1)} %wu_ref.5), custom_call_target="tpu_custom_call" | custom-call | tf_op jit(solution)/shard_map/pallas_call | solution.py:154
  17.8 13.0 %collective-permute-done.other_ref = bf16[128,1920]{1,0:T(8,128)(2,1)S(1)} collective-permute-done((bf16[128,1920]{1,0:T(8,128)(2,1)S(1)}, bf16[128,1920]{1,0:T(8,128)(2,1)S(1)}, u32[]{:S(2)}, u32[]{:S(2)}) %collective-permute-start) | collective-permute-done | bytes 491552 | tf_op jit(solution)/shard_map/ppermute | solution.py:19
  30.7 1.4 collective-permute-done.1
  32.2 1.2 pad_maximum_fusion.4
  35.3 2.3 collective-permute-start.4
  37.7 6.5 %shard_map.92 = bf16[224,2048]{1,0:T(8,128)(2,1)S(1)} custom-call(s32[1]{0:T(128)} %bitcast.4.pair_ref, bf16[2,128,1920]{2,1,0:T(8,128)(2,1)S(1)} %get-tuple-element.146.first_ref, bf16[2,128,1920]{2,1,0:T(8,128)(2,1)S(1)} %collective-permute-done.7.second_ref, bf16[1792,2048]{1,0:T(8,128)(2,1)} %wu_ref.5), custom_call_target="tpu_custom_call" | custom-call | tf_op jit(solution)/shard_map/pallas_call | solution.py:154
  44.2 13.4 %collective-permute-done.6 = bf16[2,128,1920]{2,1,0:T(8,128)(2,1)S(1)} collective-permute-done((bf16[2,128,1920]{2,1,0:T(8,128)(2,1)S(1)}, bf16[2,128,1920]{2,1,0:T(8,128)(2,1)S(1)}, u32[]{:S(2)}, u32[]{:S(2)}) %collective-permute-start.6) | collective-permute-done | bytes 983072 | tf_op jit(solution)/shard_map/ppermute | solution.py:19
  58.1 1.3 collective-permute-start.11
  59.5 2.0 collective-permute-start.8
  61.5 28.6 %collective-permute-done.11 = bf16[1,224,1536]{2,1,0:T(8,128)(2,1)S(1)} collective-permute-done((bf16[1,224,1536]{2,1,0:T(8,128)(2,1)S(1)}, bf16[1,224,1536]{2,1,0:T(8,128)(2,1)S(1)}, u32[]{:S(2)}, u32[]{:S(2)}) %collective-permute-start.11) | collective-permute-done | bytes 688160 | tf_op jit(solution)/shard_map/ppermute | solution.py:19
  91.2 5.5 %shard_map.93 = bf16[112,2048]{1,0:T(8,128)(2,1)S(1)} custom-call(s32[1]{0:T(128)} %bitcast.4.pair_ref, bf16[1,128,1920]{2,1,0:T(8,128)(2,1)S(1)} %bitcast.56, bf16[1,128,1920]{2,1,0:T(8,128)(2,1)S(1)} %get-tuple-element.159.second_ref, bf16[1792,2048]{1,0:T(8,128)(2,1)} %wu_ref.5), custom_call_target="tpu_custom_call" | custom-call | tf_op jit(solution)/shard_map/pallas_call | solution.py:154
  96.8 5.4 %shard_map.94.hid_ref = bf16[112,1024]{1,0:T(8,128)(2,1)S(1)} custom-call(s32[1]{0:T(128)} %bitcast.4.pair_ref, bf16[1,128,1920]{2,1,0:T(8,128)(2,1)S(1)} %bitcast.51, bf16[1,128,1920]{2,1,0:T(8,128)(2,1)S(1)} %get-tuple-element.109.second_ref, bf16[1792,2048]{1,0:T(8,128)(2,1)} %wu_ref.5, bf16[1792,2048]{1,0:T(8,128)(2,1)} %wu_ref.5, ...), custom_call_target="tpu_custom_call" | custom-call | tf_op jit(solution)/shard_map/pallas_call | solution.py:177
  103.8 1.5 collective-permute-start.15
  106.5 1.7 collective-permute-start.13
  108.2 6.3 %shard_map.95.hid_ref = bf16[224,1024]{1,0:T(8,128)(2,1)S(1)} custom-call(s32[1]{0:T(128)} %bitcast.4.pair_ref, bf16[2,128,1920]{2,1,0:T(8,128)(2,1)S(1)} %pad_maximum_fusion.5.first_ref, bf16[2,128,1920]{2,1,0:T(8,128)(2,1)S(1)} %slice.64.second_ref, bf16[1792,2048]{1,0:T(8,128)(2,1)} %wu_ref.5, bf16[1792,2048]{1,0:T(8,128)(2,1)} %wu_ref.5, ...), custom_call_target="tpu_custom_call" | custom-call | tf_op jit(solution)/shard_map/pallas_call | solution.py:177
  114.6 4.5 %shard_map.97 = (bf16[2,128,1792]{2,1,0:T(8,128)(2,1)S(1)}, bf16[2,128,1792]{2,1,0:T(8,128)(2,1)S(1)}) custom-call(s32[1]{0:T(128)} %bitcast.4.pair_ref, bf16[2,128,1920]{2,1,0:T(8,128)(2,1)S(1)} %pad_maximum_fusion.5.first_ref, bf16[2,128,1920]{2,1,0:T(8,128)(2,1)S(1)} %slice.64.second_ref, bf16[224,1024]{1,0:T(8,128)(2,1)S(1)} %shard_map.95.hid_ref, ...), custom_call_target="tpu_custom_call" | custom-call | tf_op jit(solution)/shard_map/pallas_call | solution.py:204
  119.1 2.1 shard_map.96
  121.2 1.3 constant_dynamic-update-slice_fusion.2
  122.5 16.3 %collective-permute-done.13.hid_ref = bf16[112,1024]{1,0:T(8,128)(2,1)S(1)} collective-permute-done((bf16[112,1024]{1,0:T(8,128)(2,1)S(1)}, bf16[112,1024]{1,0:T(8,128)(2,1)S(1)}, u32[]{:S(2)}, u32[]{:S(2)}) %collective-permute-start.13) | collective-permute-done | bytes 229408 | tf_op jit(solution)/shard_map/ppermute | solution.py:19
  138.8 2.5 constant_dynamic-update-slice_fusion.1
  141.3 2.6 constant_dynamic-update-slice_fusion.refs_0_
  145.8 2.0 slice.55
  148.3 1.3 collective-permute-start.20
  149.5 3.1 %collective-permute-done.18 = bf16[3,128,1792]{2,1,0:T(8,128)(2,1)S(1)} collective-permute-done((bf16[3,128,1792]{2,1,0:T(8,128)(2,1)S(1)}, bf16[3,128,1792]{2,1,0:T(8,128)(2,1)S(1)}, u32[]{:S(2)}, u32[]{:S(2)}) %collective-permute-start.18) | collective-permute-done | bytes 1376288 | tf_op jit(solution)/shard_map/ppermute | solution.py:19
  152.6 5.9 %shard_map.98.hid_ref = bf16[112,1024]{1,0:T(8,128)(2,1)S(1)} custom-call(s32[1]{0:T(128)} %bitcast.4.pair_ref, bf16[1,128,1920]{2,1,0:T(8,128)(2,1)S(1)} %bitcast.61, bf16[1,128,1920]{2,1,0:T(8,128)(2,1)S(1)} %collective-permute-done.14.second_ref, bf16[1792,2048]{1,0:T(8,128)(2,1)} %wu_ref.5, bf16[1792,2048]{1,0:T(8,128)(2,1)} %wu_ref.5, ...), custom_call_target="tpu_custom_call" | custom-call | tf_op jit(solution)/shard_map/pallas_call | solution.py:177
  158.5 2.1 shard_map.99
  161.4 2.1 shard_map.100
  163.5 7.8 %collective-permute-done.17.hid_ref = bf16[224,1024]{1,0:T(8,128)(2,1)S(1)} collective-permute-done((bf16[224,1024]{1,0:T(8,128)(2,1)S(1)}, bf16[224,1024]{1,0:T(8,128)(2,1)S(1)}, u32[]{:S(2)}, u32[]{:S(2)}) %collective-permute-start.17) | collective-permute-done | bytes 458784 | tf_op jit(solution)/shard_map/ppermute | solution.py:19
  175.5 2.2 collective-permute-start.22
  177.7 6.4 %shard_map.101 = (bf16[128,2048]{1,0:T(8,128)(2,1)S(1)}, f32[128,2048]{1,0:T(8,128)S(1)}) custom-call(s32[22]{0:T(128)S(1)} %pad_add_fusion.spots_ref, bf16[128,1920]{1,0:T(8,128)(2,1)S(1)} %concatenate.40.own_ref, bf16[128,1920]{1,0:T(8,128)(2,1)S(1)} %collective-permute-done.other_ref, bf16[6,224,1536]{2,1,0:T(8,128)(2,1)} %constant_dynamic-update-slice_fusion.refs_0_, ...), custom_call_target="tpu_custom_call" | custom-call | tf_op jit(solution)/shard_map/pallas_call | solution.py:268
  184.2 4.5 %shard_map.102 = (bf16[2,128,1792]{2,1,0:T(8,128)(2,1)S(1)}, bf16[2,128,1792]{2,1,0:T(8,128)(2,1)S(1)}) custom-call(s32[1]{0:T(128)} %bitcast.4.pair_ref, bf16[2,128,1920]{2,1,0:T(8,128)(2,1)S(1)} %copy-done.5, bf16[2,128,1920]{2,1,0:T(8,128)(2,1)S(1)} %copy-done.9, bf16[224,1024]{1,0:T(8,128)(2,1)S(1)} %copy-done.11, bf16[1024,1792]{1,0:T(8,128)(2,1)} %w_ref.17), custom_call_target="tpu_custom_call" | custom-call | tf_op jit(solution)/shard_map/pallas_call | solution.py:204
  188.7 1.9 collective-permute-done.22.hid_ref
  190.6 2.3 collective-permute-done.24
  195.2 1.8 collective-permute-start.28
  197.0 2.1 shard_map.103
  199.1 21.0 %collective-permute-done.28 = bf16[128,1792]{1,0:T(8,128)(2,1)S(1)} collective-permute-done((bf16[128,1792]{1,0:T(8,128)(2,1)S(1)}, bf16[128,1792]{1,0:T(8,128)(2,1)S(1)}, u32[]{:S(2)}, u32[]{:S(2)}) %collective-permute-start.28) | collective-permute-done | bytes 458784 | tf_op jit(solution)/shard_map/ppermute | solution.py:19
  220.8 2.3 collective-permute-start.33
  224.0 4.9 %shard_map.104 = bf16[128,1792]{1,0:T(8,128)(2,1)S(1)} custom-call(s32[22]{0:T(128)S(1)} %pad_add_fusion.spots_ref, bf16[128,1024]{1,0:T(8,128)(2,1)S(1)} %fusion.8.hid_ref, bf16[6,224,1536]{2,1,0:T(8,128)(2,1)} %constant_dynamic-update-slice_fusion.refs_0_, bf16[4,112,1536]{2,1,0:T(8,128)(2,1)S(1)} %constant_dynamic-update-slice_fusion.3.refs_1_, ...), custom_call_target="tpu_custom_call" | custom-call | tf_op jit(solution)/shard_map/pallas_call | solution.py:302
  229.8 1.7 fusion.7
  231.5 2.6 collective-permute-start.30
  234.1 1.6 collective-permute-done.32
  235.8 4.9 %shard_map.105 = bf16[128,1792]{1,0:T(8,128)(2,1)S(1)} custom-call(s32[22]{0:T(128)S(1)} %pad_add_fusion.spots_ref, bf16[128,1024]{1,0:T(8,128)(2,1)S(1)} %collective-permute-done.31.hid_ref, bf16[6,224,1536]{2,1,0:T(8,128)(2,1)} %constant_dynamic-update-slice_fusion.refs_0_, bf16[4,112,1536]{2,1,0:T(8,128)(2,1)S(1)} %constant_dynamic-update-slice_fusion.3.refs_1_, ...), custom_call_target="tpu_custom_call" | custom-call | tf_op jit(solution)/shard_map/pallas_call | solution.py:302
  240.7 9.1 %collective-permute-done.33 = bf16[128,1792]{1,0:T(8,128)(2,1)S(1)} collective-permute-done((bf16[128,1792]{1,0:T(8,128)(2,1)S(1)}, bf16[128,1792]{1,0:T(8,128)(2,1)S(1)}, u32[]{:S(2)}, u32[]{:S(2)}) %collective-permute-start.33) | collective-permute-done | bytes 458784 | tf_op jit(solution)/shard_map/ppermute | solution.py:19
  249.8 10.0 %collective-permute-done.35 = bf16[128,1792]{1,0:T(8,128)(2,1)S(1)} collective-permute-done((bf16[128,1792]{1,0:T(8,128)(2,1)S(1)}, bf16[128,1792]{1,0:T(8,128)(2,1)S(1)}, u32[]{:S(2)}, u32[]{:S(2)}) %collective-permute-start.35) | collective-permute-done | bytes 458784 | tf_op jit(solution)/shard_map/ppermute | solution.py:19
  259.9 1.4 fusion.3
  (124 shorter events, 25.2 us)
Async XLA Ops:
  0.0 12.3 %copy-start = (bf16[224,2048]{1,0:T(8,128)(2,1)S(1)}, bf16[224,2048]{1,0:T(8,128)(2,1)}, u32[]{:S(2)}) copy-start(bf16[224,2048]{1,0:T(8,128)(2,1)} %param.12) | copy-start | bytes 2752516
  3.9 8.5 %collective-permute-start.3 = (bf16[128,1920]{1,0:T(8,128)(2,1)S(1)}, bf16[128,1920]{1,0:T(8,128)(2,1)S(1)}, u32[]{:S(2)}, u32[]{:S(2)}) collective-permute-start(bf16[128,1920]{1,0:T(8,128)(2,1)S(1)} %concatenate.40.own_ref), channel_id=1, source_target_pairs={{0,1},{1,0},{2,3},{3,2},{4,5},{5,4},{6,7},{7,6},{8,9},{9,8},{10,11... | collective-permute-start | bytes 1474568 | tf_op jit(solution)/shard_map/ppermute | solution.py:19
  4.6 26.2 %collective-permute-start = (bf16[128,1920]{1,0:T(8,128)(2,1)S(1)}, bf16[128,1920]{1,0:T(8,128)(2,1)S(1)}, u32[]{:S(2)}, u32[]{:S(2)}) collective-permute-start(bf16[128,1920]{1,0:T(8,128)(2,1)S(1)} %concatenate.39), channel_id=1, source_target_pairs={{0,8},{1,9},{2,10},{3,11},{4,12},{5,13},{6,14},{7,15},{8,0},{9,1},... | collective-permute-start | bytes 1474568 | tf_op jit(solution)/shard_map/ppermute | solution.py:19
  8.2 22.5 %collective-permute-start.2 = (bf16[128,1920]{1,0:T(8,128)(2,1)S(1)}, bf16[128,1920]{1,0:T(8,128)(2,1)}, u32[]{:S(2)}, u32[]{:S(2)}) collective-permute-start(bf16[128,1920]{1,0:T(8,128)(2,1)S(1)} %concatenate.40.own_ref), channel_id=1, source_target_pairs={{0,2},{1,3},{2,0},{3,1},{4,6},{5,7},{6,4},{7,5},{8,10},{9,11},{10,... | collective-permute-start | bytes 1474568 | tf_op jit(solution)/shard_map/ppermute | solution.py:19
  9.7 22.4 %collective-permute-start.1 = (bf16[128,1920]{1,0:T(8,128)(2,1)S(1)}, bf16[128,1920]{1,0:T(8,128)(2,1)S(1)}, u32[]{:S(2)}, u32[]{:S(2)}) collective-permute-start(bf16[128,1920]{1,0:T(8,128)(2,1)S(1)} %concatenate.40.own_ref), channel_id=1, source_target_pairs={{0,4},{1,5},{2,6},{3,7},{4,0},{5,1},{6,2},{7,3},{8,12},{9,13},{10,... | collective-permute-start | bytes 1474568 | tf_op jit(solution)/shard_map/ppermute | solution.py:19
  33.4 10.8 %copy-start.4 = (bf16[2,128,1920]{2,1,0:T(8,128)(2,1)}, bf16[2,128,1920]{2,1,0:T(8,128)(2,1)S(1)}, u32[]{:S(2)}) copy-start(bf16[2,128,1920]{2,1,0:T(8,128)(2,1)S(1)} %get-tuple-element.146.first_ref) | copy-start | bytes 2949124
  33.4 4.2 %collective-permute-start.7 = (bf16[2,128,1920]{2,1,0:T(8,128)(2,1)S(1)}, bf16[2,128,1920]{2,1,0:T(8,128)(2,1)S(1)}, u32[]{:S(2)}, u32[]{:S(2)}) collective-permute-start(bf16[2,128,1920]{2,1,0:T(8,128)(2,1)S(1)} %get-tuple-element.146.first_ref), channel_id=1, source_target_pairs={{0,1},{1,0},{2,3},{3,2},{4,5},{5,4},{6,7},{7,6},{8,9},{9,8},{10,11... | collective-permute-start | bytes 2949128 | tf_op jit(solution)/shard_map/ppermute | solution.py:19
  33.5 24.2 %collective-permute-start.6 = (bf16[2,128,1920]{2,1,0:T(8,128)(2,1)S(1)}, bf16[2,128,1920]{2,1,0:T(8,128)(2,1)S(1)}, u32[]{:S(2)}, u32[]{:S(2)}) collective-permute-start(bf16[2,128,1920]{2,1,0:T(8,128)(2,1)S(1)} %get-tuple-element.192), channel_id=1, source_target_pairs={{0,2},{1,3},{2,0},{3,1},{4,6},{5,7},{6,4},{7,5},{8,10},{9,11},{10,... | collective-permute-start | bytes 2949128 | tf_op jit(solution)/shard_map/ppermute | solution.py:19
  34.1 23.6 %collective-permute-start.5 = (bf16[128,1920]{1,0:T(8,128)(2,1)S(1)}, bf16[128,1920]{1,0:T(8,128)(2,1)S(1)}, u32[]{:S(2)}, u32[]{:S(2)}) collective-permute-start(bf16[128,1920]{1,0:T(8,128)(2,1)S(1)} %collective-permute-done.other_ref), channel_id=1, source_target_pairs={{0,4},{1,5},{2,6},{3,7},{4,0},{5,1},{6,2},{7,3},{8,12},{9,13},{10,... | collective-permute-start | bytes 1474568 | tf_op jit(solution)/shard_map/ppermute | solution.py:19
  35.3 22.4 %collective-permute-start.4 = (bf16[112,2048]{1,0:T(8,128)(2,1)S(1)}, bf16[112,2048]{1,0:T(8,128)(2,1)S(1)}, u32[]{:S(2)}, u32[]{:S(2)}) collective-permute-start(bf16[112,2048]{1,0:T(8,128)(2,1)S(1)} %shard_map.91), channel_id=1, source_target_pairs={{0,8},{1,9},{2,10},{3,11},{4,12},{5,13},{6,14},{7,15},{8,0},{9,1},... | collective-permute-start | bytes 1376264 | tf_op jit(solution)/shard_map/ppermute | solution.py:19
  37.7 6.6 %copy-start.8 = (bf16[2,128,1920]{2,1,0:T(8,128)(2,1)}, bf16[2,128,1920]{2,1,0:T(8,128)(2,1)S(1)}, u32[]{:S(2)}) copy-start(bf16[2,128,1920]{2,1,0:T(8,128)(2,1)S(1)} %collective-permute-done.7.second_ref) | copy-start | bytes 2949124
  58.1 33.0 %collective-permute-start.10 = (bf16[4,128,1920]{2,1,0:T(8,128)(2,1)S(1)}, bf16[4,128,1920]{2,1,0:T(8,128)(2,1)S(1)}, u32[]{:S(2)}, u32[]{:S(2)}) collective-permute-start(bf16[4,128,1920]{2,1,0:T(8,128)(2,1)S(1)} %pad_maximum_fusion), channel_id=1, source_target_pairs={{0,1},{1,0},{2,3},{3,2},{4,5},{5,4},{6,7},{7,6},{8,9},{9,8},{10,11... | collective-permute-start | bytes 5898248 | tf_op jit(solution)/shard_map/ppermute | solution.py:19
  58.1 31.9 %collective-permute-start.11 = (bf16[1,224,1536]{2,1,0:T(8,128)(2,1)S(1)}, bf16[1,224,1536]{2,1,0:T(8,128)(2,1)S(1)}, u32[]{:S(2)}, u32[]{:S(2)}) collective-permute-start(bf16[1,224,1536]{2,1,0:T(8,128)(2,1)S(1)} %maximum_bitcast_fusion), channel_id=1, source_target_pairs={{0,4},{1,5},{2,6},{3,7},{4,0},{5,1},{6,2},{7,3},{8,12},{9,13},{10,... | collective-permute-start | bytes 2064392 | tf_op jit(solution)/shard_map/ppermute | solution.py:19
  59.5 43.5 %collective-permute-start.8 = (bf16[224,2048]{1,0:T(8,128)(2,1)S(1)}, bf16[224,2048]{1,0:T(8,128)(2,1)S(1)}, u32[]{:S(2)}, u32[]{:S(2)}) collective-permute-start(bf16[224,2048]{1,0:T(8,128)(2,1)S(1)} %shard_map.92), channel_id=1, source_target_pairs={{0,8},{1,9},{2,10},{3,11},{4,12},{5,13},{6,14},{7,15},{8,0},{9,1},... | collective-permute-start | bytes 2752520 | tf_op jit(solution)/shard_map/ppermute | solution.py:19
  90.2 12.9 %collective-permute-start.9 = (bf16[128,1920]{1,0:T(8,128)(2,1)S(1)}, bf16[128,1920]{1,0:T(8,128)(2,1)S(1)}, u32[]{:S(2)}, u32[]{:S(2)}) collective-permute-start(bf16[128,1920]{1,0:T(8,128)(2,1)S(1)} %collective-permute-done.5), channel_id=1, source_target_pairs={{0,2},{1,3},{2,0},{3,1},{4,6},{5,7},{6,4},{7,5},{8,10},{9,11},{10,... | collective-permute-start | bytes 1474568 | tf_op jit(solution)/shard_map/ppermute | solution.py:19
  103.0 35.8 %collective-permute-start.16 = (bf16[2,224,1536]{2,1,0:T(8,128)(2,1)S(1)}, bf16[2,224,1536]{2,1,0:T(8,128)(2,1)}, u32[]{:S(2)}, u32[]{:S(2)}) collective-permute-start(bf16[2,224,1536]{2,1,0:T(8,128)(2,1)S(1)} %pad_maximum_fusion.1), channel_id=1, source_target_pairs={{0,2},{1,3},{2,0},{3,1},{4,6},{5,7},{6,4},{7,5},{8,10},{9,11},{10,... | collective-permute-start | bytes 4128776 | tf_op jit(solution)/shard_map/ppermute | solution.py:19
  103.8 35.1 %collective-permute-start.15 = (bf16[2,224,1536]{2,1,0:T(8,128)(2,1)S(1)}, bf16[2,224,1536]{2,1,0:T(8,128)(2,1)}, u32[]{:S(2)}, u32[]{:S(2)}) collective-permute-start(bf16[2,224,1536]{2,1,0:T(8,128)(2,1)S(1)} %pad_maximum_fusion.1), channel_id=1, source_target_pairs={{0,16},{16,0},{1,17},{17,1},{2,18},{18,2},{3,19},{19,3},{4,20},{20... | collective-permute-start | bytes 4128776 | tf_op jit(solution)/shard_map/ppermute | solution.py:19
  105.3 33.5 %collective-permute-start.14 = (bf16[1,128,1920]{2,1,0:T(8,128)(2,1)S(1)}, bf16[1,128,1920]{2,1,0:T(8,128)(2,1)S(1)}, u32[]{:S(2)}, u32[]{:S(2)}) collective-permute-start(bf16[1,128,1920]{2,1,0:T(8,128)(2,1)S(1)} %bitcast.60), channel_id=1, source_target_pairs={{0,1},{1,0},{2,3},{3,2},{4,5},{5,4},{6,7},{7,6},{8,9},{9,8},{10,11... | collective-permute-start | bytes 1474568 | tf_op jit(solution)/shard_map/ppermute | solution.py:19
  105.3 33.5 %collective-permute-start.12 = (bf16[112,2048]{1,0:T(8,128)(2,1)S(1)}, bf16[112,2048]{1,0:T(8,128)(2,1)S(1)}, u32[]{:S(2)}, u32[]{:S(2)}) collective-permute-start(bf16[112,2048]{1,0:T(8,128)(2,1)S(1)} %shard_map.93), channel_id=1, source_target_pairs={{0,8},{1,9},{2,10},{3,11},{4,12},{5,13},{6,14},{7,15},{8,0},{9,1},... | collective-permute-start | bytes 1376264 | tf_op jit(solution)/shard_map/ppermute | solution.py:19
  106.5 32.3 %collective-permute-start.13 = (bf16[112,1024]{1,0:T(8,128)(2,1)S(1)}, bf16[112,1024]{1,0:T(8,128)(2,1)S(1)}, u32[]{:S(2)}, u32[]{:S(2)}) collective-permute-start(bf16[112,1024]{1,0:T(8,128)(2,1)S(1)} %shard_map.94.hid_ref), channel_id=1, source_target_pairs={{0,8},{1,9},{2,10},{3,11},{4,12},{5,13},{6,14},{7,15},{8,0},{9,1},... | collective-permute-start | bytes 688136 | tf_op jit(solution)/shard_map/ppermute | solution.py:19
  121.2 20.1 %copy-start.12 = (bf16[1,128,1792]{2,1,0:T(8,128)(2,1)}, bf16[1,128,1792]{2,1,0:T(8,128)(2,1)S(1)}, u32[]{:S(2)}) copy-start(bf16[1,128,1792]{2,1,0:T(8,128)(2,1)S(1)} %get-tuple-element.168) | copy-start | bytes 1376260
  143.9 27.4 %collective-permute-start.19 = (bf16[6,224,1536]{2,1,0:T(8,128)(2,1)}, bf16[6,224,1536]{2,1,0:T(8,128)(2,1)}, u32[]{:S(2)}, u32[]{:S(2)}) collective-permute-start(bf16[6,224,1536]{2,1,0:T(8,128)(2,1)} %constant_dynamic-update-slice_fusion.refs_0_), channel_id=1, source_target_pairs={{0,1},{1,0},{2,3},{3,2},{4,5},{5,4},{6,7},{7,6},{8,9},{9,8},{10,11... | collective-permute-start | bytes 12386312 | tf_op jit(solution)/shard_map/ppermute | solution.py:19
  144.1 8.5 %collective-permute-start.18 = (bf16[3,128,1792]{2,1,0:T(8,128)(2,1)S(1)}, bf16[3,128,1792]{2,1,0:T(8,128)(2,1)S(1)}, u32[]{:S(2)}, u32[]{:S(2)}) collective-permute-start(bf16[3,128,1792]{2,1,0:T(8,128)(2,1)S(1)} %pad_maximum_fusion.2), channel_id=1, source_target_pairs={{0,1},{1,0},{2,3},{3,2},{4,5},{5,4},{6,7},{7,6},{8,9},{9,8},{10,11... | collective-permute-start | bytes 4128776 | tf_op jit(solution)/shard_map/ppermute | solution.py:19
  147.8 23.5 %collective-permute-start.21 = (bf16[2,112,1536]{2,1,0:T(8,128)(2,1)}, bf16[2,112,1536]{2,1,0:T(8,128)(2,1)S(1)}, u32[]{:S(2)}, u32[]{:S(2)}) collective-permute-start(bf16[2,112,1536]{2,1,0:T(8,128)(2,1)} %slice.55), channel_id=1, source_target_pairs={{0,16},{16,0},{1,17},{17,1},{2,18},{18,2},{3,19},{19,3},{4,20},{20... | collective-permute-start | bytes 2064392 | tf_op jit(solution)/shard_map/ppermute | solution.py:19
  148.3 23.0 %collective-permute-start.20 = (bf16[2,112,1536]{2,1,0:T(8,128)(2,1)S(1)}, bf16[2,112,1536]{2,1,0:T(8,128)(2,1)S(1)}, u32[]{:S(2)}, u32[]{:S(2)}) collective-permute-start(bf16[2,112,1536]{2,1,0:T(8,128)(2,1)S(1)} %slice.54), channel_id=1, source_target_pairs={{0,2},{1,3},{2,0},{3,1},{4,6},{5,7},{6,4},{7,5},{8,10},{9,11},{10,... | collective-permute-start | bytes 2064392 | tf_op jit(solution)/shard_map/ppermute | solution.py:19
  149.5 21.8 %collective-permute-start.17 = (bf16[224,1024]{1,0:T(8,128)(2,1)S(1)}, bf16[224,1024]{1,0:T(8,128)(2,1)S(1)}, u32[]{:S(2)}, u32[]{:S(2)}) collective-permute-start(bf16[224,1024]{1,0:T(8,128)(2,1)S(1)} %shard_map.95.hid_ref), channel_id=1, source_target_pairs={{0,8},{1,9},{2,10},{3,11},{4,12},{5,13},{6,14},{7,15},{8,0},{9,1},... | collective-permute-start | bytes 1376264 | tf_op jit(solution)/shard_map/ppermute | solution.py:19
  152.6 20.5 %copy-start.18 = (bf16[3,128,1792]{2,1,0:T(8,128)(2,1)}, bf16[3,128,1792]{2,1,0:T(8,128)(2,1)S(1)}, u32[]{:S(2)}) copy-start(bf16[3,128,1792]{2,1,0:T(8,128)(2,1)S(1)} %collective-permute-done.18) | copy-start | bytes 4128772
  163.5 9.0 %copy-start.14 = (bf16[1,128,1792]{2,1,0:T(8,128)(2,1)}, bf16[1,128,1792]{2,1,0:T(8,128)(2,1)S(1)}, u32[]{:S(2)}) copy-start(bf16[1,128,1792]{2,1,0:T(8,128)(2,1)S(1)} %get-tuple-element.175) | copy-start | bytes 1376260
  172.4 20.5 %collective-permute-start.26 = (bf16[2,128,1792]{2,1,0:T(8,128)(2,1)}, bf16[2,128,1792]{2,1,0:T(8,128)(2,1)}, u32[]{:S(2)}, u32[]{:S(2)}) collective-permute-start(bf16[2,128,1792]{2,1,0:T(8,128)(2,1)} %pad_maximum_fusion.6), channel_id=1, source_target_pairs={{0,1},{1,0},{2,3},{3,2},{4,5},{5,4},{6,7},{7,6},{8,9},{9,8},{10,11... | collective-permute-start | bytes 2752520 | tf_op jit(solution)/shard_map/ppermute | solution.py:19
  172.5 5.2 %collective-permute-start.23 = (bf16[4,112,1536]{2,1,0:T(8,128)(2,1)S(1)}, bf16[4,112,1536]{2,1,0:T(8,128)(2,1)}, u32[]{:S(2)}, u32[]{:S(2)}) collective-permute-start(bf16[4,112,1536]{2,1,0:T(8,128)(2,1)S(1)} %constant_dynamic-update-slice_fusion.3.refs_1_), channel_id=1, source_target_pairs={{0,1},{1,0},{2,3},{3,2},{4,5},{5,4},{6,7},{7,6},{8,9},{9,8},{10,11... | collective-permute-start | bytes 4128776 | tf_op jit(solution)/shard_map/ppermute | solution.py:19
  174.3 16.3 %collective-permute-start.25 = (bf16[128,1792]{1,0:T(8,128)(2,1)}, bf16[128,1792]{1,0:T(8,128)(2,1)}, u32[]{:S(2)}, u32[]{:S(2)}) collective-permute-start(bf16[128,1792]{1,0:T(8,128)(2,1)} %get-tuple-element.187), channel_id=1, source_target_pairs={{0,2},{1,3},{2,0},{3,1},{4,6},{5,7},{6,4},{7,5},{8,10},{9,11},{10,... | collective-permute-start | bytes 1376264 | tf_op jit(solution)/shard_map/ppermute | solution.py:19
  175.5 17.4 %collective-permute-start.24 = (bf16[128,1792]{1,0:T(8,128)(2,1)}, bf16[128,1792]{1,0:T(8,128)(2,1)}, u32[]{:S(2)}, u32[]{:S(2)}) collective-permute-start(bf16[128,1792]{1,0:T(8,128)(2,1)} %get-tuple-element.188), channel_id=1, source_target_pairs={{0,4},{1,5},{2,6},{3,7},{4,0},{5,1},{6,2},{7,3},{8,12},{9,13},{10,... | collective-permute-start | bytes 1376264 | tf_op jit(solution)/shard_map/ppermute | solution.py:19
  175.5 15.1 %collective-permute-start.22 = (bf16[112,1024]{1,0:T(8,128)(2,1)S(1)}, bf16[112,1024]{1,0:T(8,128)(2,1)S(1)}, u32[]{:S(2)}, u32[]{:S(2)}) collective-permute-start(bf16[112,1024]{1,0:T(8,128)(2,1)S(1)} %shard_map.98.hid_ref), channel_id=1, source_target_pairs={{0,8},{1,9},{2,10},{3,11},{4,12},{5,13},{6,14},{7,15},{8,0},{9,1},... | collective-permute-start | bytes 688136 | tf_op jit(solution)/shard_map/ppermute | solution.py:19
  184.1 9.9 %copy-start.17 = (bf16[1,128,1792]{2,1,0:T(8,128)(2,1)S(1)}, bf16[1,128,1792]{2,1,0:T(8,128)(2,1)}, u32[]{:S(2)}) copy-start(bf16[1,128,1792]{2,1,0:T(8,128)(2,1)} %copy-done.16) | copy-start | bytes 1376260
  184.1 12.8 %copy-start.3 = (bf16[1024,1792]{1,0:T(8,128)(2,1)S(1)}, bf16[1024,1792]{1,0:T(8,128)(2,1)}, u32[]{:S(2)}) copy-start(bf16[1024,1792]{1,0:T(8,128)(2,1)} %w_ref.17) | copy-start | bytes 11010052
  184.2 12.8 %copy-start.7 = (bf16[1,128,1920]{2,1,0:T(8,128)(2,1)S(1)}, bf16[1,128,1920]{2,1,0:T(8,128)(2,1)}, u32[]{:S(2)}) copy-start(bf16[1,128,1920]{2,1,0:T(8,128)(2,1)} %copy-done.6) | copy-start | bytes 1474564
  192.9 27.2 %collective-permute-start.27 = (bf16[128,2048]{1,0:T(8,128)(2,1)S(1)}, bf16[128,2048]{1,0:T(8,128)(2,1)S(1)}, u32[]{:S(2)}, u32[]{:S(2)}) collective-permute-start(bf16[128,2048]{1,0:T(8,128)(2,1)S(1)} %get-tuple-element.152), channel_id=1, source_target_pairs={{0,8},{1,9},{2,10},{3,11},{4,12},{5,13},{6,14},{7,15},{8,0},{9,1},... | collective-permute-start | bytes 1572872 | tf_op jit(solution)/shard_map/ppermute | solution.py:19
  194.0 26.1 %collective-permute-start.29 = (bf16[2,128,1792]{2,1,0:T(8,128)(2,1)S(1)}, bf16[2,128,1792]{2,1,0:T(8,128)(2,1)S(1)}, u32[]{:S(2)}, u32[]{:S(2)}) collective-permute-start(bf16[2,128,1792]{2,1,0:T(8,128)(2,1)S(1)} %get-tuple-element.157), channel_id=1, source_target_pairs={{0,1},{1,0},{2,3},{3,2},{4,5},{5,4},{6,7},{7,6},{8,9},{9,8},{10,11... | collective-permute-start | bytes 2752520 | tf_op jit(solution)/shard_map/ppermute | solution.py:19
  195.2 24.9 %collective-permute-start.28 = (bf16[128,1792]{1,0:T(8,128)(2,1)S(1)}, bf16[128,1792]{1,0:T(8,128)(2,1)S(1)}, u32[]{:S(2)}, u32[]{:S(2)}) collective-permute-start(bf16[128,1792]{1,0:T(8,128)(2,1)S(1)} %fusion.9), channel_id=1, source_target_pairs={{0,6},{1,7},{2,4},{3,5},{4,2},{5,3},{6,0},{7,1},{8,14},{9,15},{10,... | collective-permute-start | bytes 1376264 | tf_op jit(solution)/shard_map/ppermute | solution.py:19
  220.4 13.8 %collective-permute-start.31 = (bf16[128,1024]{1,0:T(8,128)(2,1)S(1)}, bf16[128,1024]{1,0:T(8,128)(2,1)S(1)}, u32[]{:S(2)}, u32[]{:S(2)}) collective-permute-start(bf16[128,1024]{1,0:T(8,128)(2,1)S(1)} %fusion.8.hid_ref), channel_id=1, source_target_pairs={{0,8},{1,9},{2,10},{3,11},{4,12},{5,13},{6,14},{7,15},{8,0},{9,1},... | collective-permute-start | bytes 786440 | tf_op jit(solution)/shard_map/ppermute | solution.py:19
  220.5 8.5 %collective-permute-start.34 = (bf16[1,128,1792]{2,1,0:T(8,128)(2,1)S(1)}, bf16[1,128,1792]{2,1,0:T(8,128)(2,1)S(1)}, u32[]{:S(2)}, u32[]{:S(2)}) collective-permute-start(bf16[1,128,1792]{2,1,0:T(8,128)(2,1)S(1)} %get-tuple-element.178), channel_id=1, source_target_pairs={{0,1},{1,0},{2,3},{3,2},{4,5},{5,4},{6,7},{7,6},{8,9},{9,8},{10,11... | collective-permute-start | bytes 1376264 | tf_op jit(solution)/shard_map/ppermute | solution.py:19
  220.8 29.0 %collective-permute-start.33 = (bf16[128,1792]{1,0:T(8,128)(2,1)S(1)}, bf16[128,1792]{1,0:T(8,128)(2,1)S(1)}, u32[]{:S(2)}, u32[]{:S(2)}) collective-permute-start(bf16[128,1792]{1,0:T(8,128)(2,1)S(1)} %get-tuple-element.185), channel_id=1, source_target_pairs={{0,4},{1,5},{2,6},{3,7},{4,0},{5,1},{6,2},{7,3},{8,12},{9,13},{10,... | collective-permute-start | bytes 1376264 | tf_op jit(solution)/shard_map/ppermute | solution.py:19
  223.1 6.7 %copy-start.13 = (bf16[1,128,1792]{2,1,0:T(8,128)(2,1)S(1)}, bf16[1,128,1792]{2,1,0:T(8,128)(2,1)}, u32[]{:S(2)}) copy-start(bf16[1,128,1792]{2,1,0:T(8,128)(2,1)} %copy-done.12) | copy-start | bytes 1376260
  223.1 12.7 %collective-permute-start.32 = (bf16[128,1792]{1,0:T(8,128)(2,1)S(1)}, bf16[128,1792]{1,0:T(8,128)(2,1)S(1)}, u32[]{:S(2)}, u32[]{:S(2)}) collective-permute-start(bf16[128,1792]{1,0:T(8,128)(2,1)S(1)} %get-tuple-element.186), channel_id=1, source_target_pairs={{0,2},{1,3},{2,0},{3,1},{4,6},{5,7},{6,4},{7,5},{8,10},{9,11},{10,... | collective-permute-start | bytes 1376264 | tf_op jit(solution)/shard_map/ppermute | solution.py:19
  229.1 30.7 %collective-permute-start.35 = (bf16[128,1792]{1,0:T(8,128)(2,1)S(1)}, bf16[128,1792]{1,0:T(8,128)(2,1)S(1)}, u32[]{:S(2)}, u32[]{:S(2)}) collective-permute-start(bf16[128,1792]{1,0:T(8,128)(2,1)S(1)} %fusion.10), channel_id=1, source_target_pairs={{0,6},{1,7},{2,4},{3,5},{4,2},{5,3},{6,0},{7,1},{8,14},{9,15},{10,... | collective-permute-start | bytes 1376264 | tf_op jit(solution)/shard_map/ppermute | solution.py:19
  231.5 28.4 %copy-start.15 = (bf16[1,128,1792]{2,1,0:T(8,128)(2,1)S(1)}, bf16[1,128,1792]{2,1,0:T(8,128)(2,1)}, u32[]{:S(2)}) copy-start(bf16[1,128,1792]{2,1,0:T(8,128)(2,1)} %copy-done.14) | copy-start | bytes 1376260
  231.5 29.7 %collective-permute-start.30 = (bf16[128,1792]{1,0:T(8,128)(2,1)S(1)}, bf16[128,1792]{1,0:T(8,128)(2,1)S(1)}, u32[]{:S(2)}, u32[]{:S(2)}) collective-permute-start(bf16[128,1792]{1,0:T(8,128)(2,1)S(1)} %fusion.7), channel_id=1, source_target_pairs={{0,8},{1,9},{2,10},{3,11},{4,12},{5,13},{6,14},{7,15},{8,0},{9,1},... | collective-permute-start | bytes 1376264 | tf_op jit(solution)/shard_map/ppermute | solution.py:19
  235.8 26.6 %copy-start.1 = (bf16[224,2048]{1,0:T(8,128)(2,1)S(1)}, bf16[224,2048]{1,0:T(8,128)(2,1)}, u32[]{:S(2)}) copy-start(bf16[224,2048]{1,0:T(8,128)(2,1)} %param.12) | copy-start | bytes 2752516
  (8 other events, 36.4 us)

commit v4 on v3

--- a/solution.py
+++ b/solution.py
@@ -17,6 +17,12 @@
 def hop(block, mask, axis="expert"):
     count = lax.axis_size(axis)
     return lax.ppermute(block, axis, [(d, d ^ mask) for d in range(count)])
+
+
+def settle_round(late, *values):
+    last, rest = values[:late], lax.optimization_barrier(values[late:])
+    last, rest = lax.optimization_barrier((last, rest))
+    return last + rest
 
 
 def settle(*values):
@@ -519,19 +525,21 @@
     away_near_rows = rows_of(away_near_tok, away_near_hidden)
     by_group = doubled(weights, group_bits, "groups")[weights.shape[0] :]
     by_chip = hop(weights, low_bit)
+    first = jnp.concatenate([weights, by_group, by_chip])
+    lower, upper = by_group[:, :upper_row], by_chip[:, upper_row:]
     (
         far_in, own_hidden, away_far_tok, away_near_hidden, away_own_rows, away_near_rows,
-        by_group, by_chip,
-    ) = settle(
-        far_in, own_hidden, away_far_tok, away_near_hidden, away_own_rows, away_near_rows,
-        by_group, by_chip,
+        first, lower, upper,
+    ) = settle_round(
+        2, far_in, own_hidden, away_far_tok, away_near_hidden, away_own_rows, away_near_rows,
+        first, lower, upper,
     )
 
     near_hidden = hop(away_near_hidden, half)
     away_others = hop(jnp.concatenate([away_own_rows[1], away_near_rows[1]]), 1)
-    lower = hop(by_group[:, :upper_row], low_bit)
-    upper = doubled(by_chip[:, upper_row:], group_bits, "groups")[by_chip.shape[0] :]
-    first = jnp.concatenate([weights, by_group, by_chip])
+    chip_count = upper.shape[0]
+    lower = hop(lower, low_bit)
+    upper = doubled(upper, group_bits, "groups")[chip_count:]
     first_other = hop(first, 1)
     far_in, own_hidden, away_others = settle(far_in, own_hidden, away_others)
     away_far_hidden = hidden_of(away_far_tok, far_in)

time: 263 us -> 259 us (0.985)
  local copies, waits for them, and re-layouts: 13.2 us -> 6.87 us
  other arithmetic: 12.7 us -> 16.2 us
  waiting for transfers between devices: 130 us -> 127 us
    unnamed x43 -> x41, local copies, waits for them, and re-layouts: 4.67 us -> 0.91 us
    concatenate x0 -> x1, other arithmetic: none -> 3.49 us  [local(): first = jnp.concatenate([weights, by_group, by_chip])]
    ppermute x36, waiting for transfers between devices: 130 us -> 127 us  [hop(): return lax.ppermute(block, axis, [(d, d ^ mask) for d in range(count)])]
  transfers between devices with their start and end apart: 36 -> 36, of which waited for: 14 -> 14; matrix products, arithmetic and copies ran while one was open for 5% -> 6% of each run, Pallas kernels for 26% -> 27%
where the time goes in v4:
time: 259 us; the launch traced here: 258 us
  waiting for transfers between devices  127 us (49%)
  Pallas kernels  68.6 us (26%)
  starting transfers between devices  38.6 us (15%)
  other arithmetic  16.2 us (6%)
  local copies, waits for them, and re-layouts  6.87 us (3%)
    ppermute x36, waiting for transfers between devices, hop(): return lax.ppermute(block, axis, [(d, d ^ mask) for d in range(count)])  127 us
    ppermute x36, starting transfers between devices, hop(): return lax.ppermute(block, axis, [(d, d ^ mask) for d in range(count)])  38.6 us
    pallas_call x3, Pallas kernels, hidden_rows(): pl.pallas_call(functools.partial(hidden_kernel, cap), grid=(steps,), in_s...  17.6 us
    pallas_call x3, Pallas kernels, partial_sums(): pl.pallas_call(functools.partial(partial_kernel, cap), grid=(steps,), in_...  17.4 us
    pallas_call x6, Pallas kernels, weighted_rows(): pl.pallas_call(functools.partial(down_kernel, cap), grid=(steps,), in_spe...  17.4 us
    pallas_call x2, Pallas kernels, shared_rows(): pl.pallas_call(functools.partial(shared_down_kernel, masks, first_column)...  9.84 us
    pallas_call x1, Pallas kernels, shared_partial(): pl.pallas_call(functools.partial(shared_gate_kernel, masks), in_specs=[sm...  6.35 us
  transfers between devices with their start and end apart: 36, of which 14 were waited for; matrix products, arithmetic and copies ran while one was open for 6% of the time, Pallas kernels for 27%

profile of v4, /device:TPU:0, one launch (start us, length us, event | category | flops | bytes accessed | tf_op | source)
XLA Modules:
  0.0 257.9 jit_solution(16381572455682909274)
XLA Ops:
  2.6 1.2 broadcast_select_fusion
  4.6 3.7 %collective-permute-start = (bf16[128,1920]{1,0:T(8,128)(2,1)S(1)}, bf16[128,1920]{1,0:T(8,128)(2,1)S(1)}, u32[]{:S(2)}, u32[]{:S(2)}) collective-permute-start(bf16[128,1920]{1,0:T(8,128)(2,1)S(1)} %concatenate.39), channel_id=1, source_target_pairs={{0,8},{1,9},{2,10},{3,11},{4,12},{5,13},{6,14},{7,15},{8,0},{9,1},... | collective-permute-start | bytes 1474568 | tf_op jit(solution)/shard_map/ppermute | solution.py:19
  8.2 1.5 collective-permute-start.2
  9.7 1.6 collective-permute-start.1
  12.4 5.4 %shard_map.91 = bf16[112,2048]{1,0:T(8,128)(2,1)S(1)} custom-call(s32[1]{0:T(128)} %bitcast.4.pair_ref, bf16[1,128,1920]{2,1,0:T(8,128)(2,1)S(1)} %bitcast.53, bf16[1,128,1920]{2,1,0:T(8,128)(2,1)S(1)} %bitcast.58, bf16[1792,2048]{1,0:T(8,128)(2,1)} %wu_ref.5), custom_call_target="tpu_custom_call" | custom-call | tf_op jit(solution)/shard_map/pallas_call | solution.py:160
  17.8 13.0 %collective-permute-done.other_ref = bf16[128,1920]{1,0:T(8,128)(2,1)S(1)} collective-permute-done((bf16[128,1920]{1,0:T(8,128)(2,1)S(1)}, bf16[128,1920]{1,0:T(8,128)(2,1)S(1)}, u32[]{:S(2)}, u32[]{:S(2)}) %collective-permute-start) | collective-permute-done | bytes 491552 | tf_op jit(solution)/shard_map/ppermute | solution.py:19
  30.7 1.4 collective-permute-done.1
  32.2 1.2 pad_maximum_fusion.5
  35.3 2.3 collective-permute-start.4
  37.7 6.5 %shard_map.92 = bf16[224,2048]{1,0:T(8,128)(2,1)S(1)} custom-call(s32[1]{0:T(128)} %bitcast.4.pair_ref, bf16[2,128,1920]{2,1,0:T(8,128)(2,1)S(1)} %get-tuple-element.168.first_ref, bf16[2,128,1920]{2,1,0:T(8,128)(2,1)S(1)} %collective-permute-done.7.second_ref, bf16[1792,2048]{1,0:T(8,128)(2,1)} %wu_ref.5), custom_call_target="tpu_custom_call" | custom-call | tf_op jit(solution)/shard_map/pallas_call | solution.py:160
  44.2 13.4 %collective-permute-done.6 = bf16[2,128,1920]{2,1,0:T(8,128)(2,1)S(1)} collective-permute-done((bf16[2,128,1920]{2,1,0:T(8,128)(2,1)S(1)}, bf16[2,128,1920]{2,1,0:T(8,128)(2,1)S(1)}, u32[]{:S(2)}, u32[]{:S(2)}) %collective-permute-start.6) | collective-permute-done | bytes 983072 | tf_op jit(solution)/shard_map/ppermute | solution.py:19
  58.1 1.3 collective-permute-start.11
  59.5 2.0 collective-permute-start.8
  61.5 28.6 %collective-permute-done.11 = bf16[1,224,1536]{2,1,0:T(8,128)(2,1)S(1)} collective-permute-done((bf16[1,224,1536]{2,1,0:T(8,128)(2,1)S(1)}, bf16[1,224,1536]{2,1,0:T(8,128)(2,1)S(1)}, u32[]{:S(2)}, u32[]{:S(2)}) %collective-permute-start.11) | collective-permute-done | bytes 688160 | tf_op jit(solution)/shard_map/ppermute | solution.py:19
  91.2 5.5 %shard_map.93 = bf16[112,2048]{1,0:T(8,128)(2,1)S(1)} custom-call(s32[1]{0:T(128)} %bitcast.4.pair_ref, bf16[1,128,1920]{2,1,0:T(8,128)(2,1)S(1)} %bitcast.56, bf16[1,128,1920]{2,1,0:T(8,128)(2,1)S(1)} %get-tuple-element.181.second_ref, bf16[1792,2048]{1,0:T(8,128)(2,1)} %wu_ref.5), custom_call_target="tpu_custom_call" | custom-call | tf_op jit(solution)/shard_map/pallas_call | solution.py:160
  96.8 5.4 %shard_map.94.hid_ref = bf16[112,1024]{1,0:T(8,128)(2,1)S(1)} custom-call(s32[1]{0:T(128)} %bitcast.4.pair_ref, bf16[1,128,1920]{2,1,0:T(8,128)(2,1)S(1)} %bitcast.51, bf16[1,128,1920]{2,1,0:T(8,128)(2,1)S(1)} %get-tuple-element.120.second_ref, bf16[1792,2048]{1,0:T(8,128)(2,1)} %wu_ref.5, bf16[1792,2048]{1,0:T(8,128)(2,1)} %wu_ref.5, ...), custom_call_target="tpu_custom_call" | custom-call | tf_op jit(solution)/shard_map/pallas_call | solution.py:183
  103.8 1.5 collective-permute-start.15
  105.3 1.2 collective-permute-start.12
  106.5 1.7 collective-permute-start.13
  108.2 6.3 %shard_map.95.hid_ref = bf16[224,1024]{1,0:T(8,128)(2,1)S(1)} custom-call(s32[1]{0:T(128)} %bitcast.4.pair_ref, bf16[2,128,1920]{2,1,0:T(8,128)(2,1)S(1)} %pad_maximum_fusion.6.first_ref, bf16[2,128,1920]{2,1,0:T(8,128)(2,1)S(1)} %slice.64.second_ref, bf16[1792,2048]{1,0:T(8,128)(2,1)} %wu_ref.5, bf16[1792,2048]{1,0:T(8,128)(2,1)} %wu_ref.5, ...), custom_call_target="tpu_custom_call" | custom-call | tf_op jit(solution)/shard_map/pallas_call | solution.py:183
  114.6 4.5 %shard_map.97 = (bf16[2,128,1792]{2,1,0:T(8,128)(2,1)S(1)}, bf16[2,128,1792]{2,1,0:T(8,128)(2,1)S(1)}) custom-call(s32[1]{0:T(128)} %bitcast.4.pair_ref, bf16[2,128,1920]{2,1,0:T(8,128)(2,1)S(1)} %pad_maximum_fusion.6.first_ref, bf16[2,128,1920]{2,1,0:T(8,128)(2,1)S(1)} %slice.64.second_ref, bf16[224,1024]{1,0:T(8,128)(2,1)S(1)} %shard_map.95.hid_ref, ...), custom_call_target="tpu_custom_call" | custom-call | tf_op jit(solution)/shard_map/pallas_call | solution.py:210
  119.1 2.1 shard_map.96
  121.2 12.8 %collective-permute-done.16 = bf16[2,224,1536]{2,1,0:T(8,128)(2,1)} collective-permute-done((bf16[2,224,1536]{2,1,0:T(8,128)(2,1)S(1)}, bf16[2,224,1536]{2,1,0:T(8,128)(2,1)}, u32[]{:S(2)}, u32[]{:S(2)}) %collective-permute-start.16) | collective-permute-done | bytes 1376288 | tf_op jit(solution)/shard_map/ppermute | solution.py:19
  135.2 2.0 slice.67
  137.2 3.5 %pad_maximum_fusion.refs_0_ = bf16[6,224,1536]{2,1,0:T(8,128)(2,1)} fusion(bf16[2,224,1536]{2,1,0:T(8,128)(2,1)} %collective-permute-done.16, bf16[2,224,1536]{2,1,0:T(8,128)(2,1)} %collective-permute-done.15, bf16[2,224,1536]{2,1,0:T(8,128)(2,1)S(1)} %pad_maximum_fusion.2), kind=kLoop, calls=%fused_computation | loop fusion | flops 4128768 | bytes 8257536 | tf_op jit(solution)/shard_map/concatenate | solution.py:528
  142.6 1.5 collective-permute-start.21
  144.9 4.5 %collective-permute-done.18 = bf16[3,128,1792]{2,1,0:T(8,128)(2,1)S(1)} collective-permute-done((bf16[3,128,1792]{2,1,0:T(8,128)(2,1)S(1)}, bf16[3,128,1792]{2,1,0:T(8,128)(2,1)S(1)}, u32[]{:S(2)}, u32[]{:S(2)}) %collective-permute-start.18) | collective-permute-done | bytes 1376288 | tf_op jit(solution)/shard_map/ppermute | solution.py:19
  149.4 5.9 %shard_map.98.hid_ref = bf16[112,1024]{1,0:T(8,128)(2,1)S(1)} custom-call(s32[1]{0:T(128)} %bitcast.4.pair_ref, bf16[1,128,1920]{2,1,0:T(8,128)(2,1)S(1)} %bitcast.61, bf16[1,128,1920]{2,1,0:T(8,128)(2,1)S(1)} %collective-permute-done.14.second_ref, bf16[1792,2048]{1,0:T(8,128)(2,1)} %wu_ref.5, bf16[1792,2048]{1,0:T(8,128)(2,1)} %wu_ref.5, ...), custom_call_target="tpu_custom_call" | custom-call | tf_op jit(solution)/shard_map/pallas_call | solution.py:183
  155.3 2.1 shard_map.99
  158.2 2.1 shard_map.100
  160.3 6.5 %collective-permute-done.17.hid_ref = bf16[224,1024]{1,0:T(8,128)(2,1)S(1)} collective-permute-done((bf16[224,1024]{1,0:T(8,128)(2,1)S(1)}, bf16[224,1024]{1,0:T(8,128)(2,1)S(1)}, u32[]{:S(2)}, u32[]{:S(2)}) %collective-permute-start.17) | collective-permute-done | bytes 458784 | tf_op jit(solution)/shard_map/ppermute | solution.py:19
  170.7 2.6 %collective-permute-start.22 = (bf16[112,1024]{1,0:T(8,128)(2,1)S(1)}, bf16[112,1024]{1,0:T(8,128)(2,1)S(1)}, u32[]{:S(2)}, u32[]{:S(2)}) collective-permute-start(bf16[112,1024]{1,0:T(8,128)(2,1)S(1)} %shard_map.98.hid_ref), channel_id=1, source_target_pairs={{0,8},{1,9},{2,10},{3,11},{4,12},{5,13},{6,14},{7,15},{8,0},{9,1},... | collective-permute-start | bytes 688136 | tf_op jit(solution)/shard_map/ppermute | solution.py:19
  173.4 6.3 %shard_map.101 = (bf16[128,2048]{1,0:T(8,128)(2,1)S(1)}, f32[128,2048]{1,0:T(8,128)S(1)}) custom-call(s32[22]{0:T(128)S(1)} %pad_add_fusion.spots_ref, bf16[128,1920]{1,0:T(8,128)(2,1)S(1)} %concatenate.40.own_ref, bf16[128,1920]{1,0:T(8,128)(2,1)S(1)} %collective-permute-done.other_ref, bf16[6,224,1536]{2,1,0:T(8,128)(2,1)} %pad_maximum_fusion.refs_0_, ...), custom_call_target="tpu_custom_call" | custom-call | tf_op jit(solution)/shard_map/pallas_call | solution.py:274
  179.8 4.5 %shard_map.102 = (bf16[2,128,1792]{2,1,0:T(8,128)(2,1)S(1)}, bf16[2,128,1792]{2,1,0:T(8,128)(2,1)S(1)}) custom-call(s32[1]{0:T(128)} %bitcast.4.pair_ref, bf16[2,128,1920]{2,1,0:T(8,128)(2,1)S(1)} %copy-done.5, bf16[2,128,1920]{2,1,0:T(8,128)(2,1)S(1)} %copy-done.9, bf16[224,1024]{1,0:T(8,128)(2,1)S(1)} %copy-done.11, bf16[1024,1792]{1,0:T(8,128)(2,1)} %w_ref.17), custom_call_target="tpu_custom_call" | custom-call | tf_op jit(solution)/shard_map/pallas_call | solution.py:210
  184.3 1.5 collective-permute-done.22.hid_ref
  185.8 2.3 collective-permute-done.24
  190.4 1.8 collective-permute-start.28
  192.2 2.1 shard_map.103
  194.3 21.1 %collective-permute-done.28 = bf16[128,1792]{1,0:T(8,128)(2,1)S(1)} collective-permute-done((bf16[128,1792]{1,0:T(8,128)(2,1)S(1)}, bf16[128,1792]{1,0:T(8,128)(2,1)S(1)}, u32[]{:S(2)}, u32[]{:S(2)}) %collective-permute-start.28) | collective-permute-done | bytes 458784 | tf_op jit(solution)/shard_map/ppermute | solution.py:19
  216.2 2.3 collective-permute-start.33
  219.6 4.9 %shard_map.104 = bf16[128,1792]{1,0:T(8,128)(2,1)S(1)} custom-call(s32[22]{0:T(128)S(1)} %pad_add_fusion.spots_ref, bf16[128,1024]{1,0:T(8,128)(2,1)S(1)} %fusion.8.hid_ref, bf16[6,224,1536]{2,1,0:T(8,128)(2,1)} %pad_maximum_fusion.refs_0_, bf16[4,112,1536]{2,1,0:T(8,128)(2,1)S(1)} %constant_dynamic-update-slice_fusion.refs_1_, ...), custom_call_target="tpu_custom_call" | custom-call | tf_op jit(solution)/shard_map/pallas_call | solution.py:308
  225.2 1.7 fusion.7
  226.9 2.6 %collective-permute-start.30 = (bf16[128,1792]{1,0:T(8,128)(2,1)S(1)}, bf16[128,1792]{1,0:T(8,128)(2,1)S(1)}, u32[]{:S(2)}, u32[]{:S(2)}) collective-permute-start(bf16[128,1792]{1,0:T(8,128)(2,1)S(1)} %fusion.7), channel_id=1, source_target_pairs={{0,8},{1,9},{2,10},{3,11},{4,12},{5,13},{6,14},{7,15},{8,0},{9,1},... | collective-permute-start | bytes 1376264 | tf_op jit(solution)/shard_map/ppermute | solution.py:19
  229.5 1.7 collective-permute-done.32
  231.1 4.9 %shard_map.105 = bf16[128,1792]{1,0:T(8,128)(2,1)S(1)} custom-call(s32[22]{0:T(128)S(1)} %pad_add_fusion.spots_ref, bf16[128,1024]{1,0:T(8,128)(2,1)S(1)} %collective-permute-done.31.hid_ref, bf16[6,224,1536]{2,1,0:T(8,128)(2,1)} %pad_maximum_fusion.refs_0_, bf16[4,112,1536]{2,1,0:T(8,128)(2,1)S(1)} %constant_dynamic-update-slice_fusion.refs_1_, ...), custom_call_target="tpu_custom_call" | custom-call | tf_op jit(solution)/shard_map/pallas_call | solution.py:308
  236.1 9.1 %collective-permute-done.33 = bf16[128,1792]{1,0:T(8,128)(2,1)S(1)} collective-permute-done((bf16[128,1792]{1,0:T(8,128)(2,1)S(1)}, bf16[128,1792]{1,0:T(8,128)(2,1)S(1)}, u32[]{:S(2)}, u32[]{:S(2)}) %collective-permute-start.33) | collective-permute-done | bytes 458784 | tf_op jit(solution)/shard_map/ppermute | solution.py:19
  245.2 10.2 %collective-permute-done.35 = bf16[128,1792]{1,0:T(8,128)(2,1)S(1)} collective-permute-done((bf16[128,1792]{1,0:T(8,128)(2,1)S(1)}, bf16[128,1792]{1,0:T(8,128)(2,1)S(1)}, u32[]{:S(2)}, u32[]{:S(2)}) %collective-permute-start.35) | collective-permute-done | bytes 458784 | tf_op jit(solution)/shard_map/ppermute | solution.py:19
  255.4 1.4 fusion.3
  (122 shorter events, 23.9 us)
Async XLA Ops:
  0.0 12.3 %copy-start = (bf16[224,2048]{1,0:T(8,128)(2,1)S(1)}, bf16[224,2048]{1,0:T(8,128)(2,1)}, u32[]{:S(2)}) copy-start(bf16[224,2048]{1,0:T(8,128)(2,1)} %param.12) | copy-start | bytes 2752516
  3.9 8.5 %collective-permute-start.3 = (bf16[128,1920]{1,0:T(8,128)(2,1)S(1)}, bf16[128,1920]{1,0:T(8,128)(2,1)S(1)}, u32[]{:S(2)}, u32[]{:S(2)}) collective-permute-start(bf16[128,1920]{1,0:T(8,128)(2,1)S(1)} %concatenate.40.own_ref), channel_id=1, source_target_pairs={{0,1},{1,0},{2,3},{3,2},{4,5},{5,4},{6,7},{7,6},{8,9},{9,8},{10,11... | collective-permute-start | bytes 1474568 | tf_op jit(solution)/shard_map/ppermute | solution.py:19
  4.6 26.2 %collective-permute-start = (bf16[128,1920]{1,0:T(8,128)(2,1)S(1)}, bf16[128,1920]{1,0:T(8,128)(2,1)S(1)}, u32[]{:S(2)}, u32[]{:S(2)}) collective-permute-start(bf16[128,1920]{1,0:T(8,128)(2,1)S(1)} %concatenate.39), channel_id=1, source_target_pairs={{0,8},{1,9},{2,10},{3,11},{4,12},{5,13},{6,14},{7,15},{8,0},{9,1},... | collective-permute-start | bytes 1474568 | tf_op jit(solution)/shard_map/ppermute | solution.py:19
  8.2 22.5 %collective-permute-start.2 = (bf16[128,1920]{1,0:T(8,128)(2,1)S(1)}, bf16[128,1920]{1,0:T(8,128)(2,1)}, u32[]{:S(2)}, u32[]{:S(2)}) collective-permute-start(bf16[128,1920]{1,0:T(8,128)(2,1)S(1)} %concatenate.40.own_ref), channel_id=1, source_target_pairs={{0,2},{1,3},{2,0},{3,1},{4,6},{5,7},{6,4},{7,5},{8,10},{9,11},{10,... | collective-permute-start | bytes 1474568 | tf_op jit(solution)/shard_map/ppermute | solution.py:19
  9.7 22.4 %collective-permute-start.1 = (bf16[128,1920]{1,0:T(8,128)(2,1)S(1)}, bf16[128,1920]{1,0:T(8,128)(2,1)S(1)}, u32[]{:S(2)}, u32[]{:S(2)}) collective-permute-start(bf16[128,1920]{1,0:T(8,128)(2,1)S(1)} %concatenate.40.own_ref), channel_id=1, source_target_pairs={{0,4},{1,5},{2,6},{3,7},{4,0},{5,1},{6,2},{7,3},{8,12},{9,13},{10,... | collective-permute-start | bytes 1474568 | tf_op jit(solution)/shard_map/ppermute | solution.py:19
  33.4 10.8 %copy-start.4 = (bf16[2,128,1920]{2,1,0:T(8,128)(2,1)}, bf16[2,128,1920]{2,1,0:T(8,128)(2,1)S(1)}, u32[]{:S(2)}) copy-start(bf16[2,128,1920]{2,1,0:T(8,128)(2,1)S(1)} %get-tuple-element.168.first_ref) | copy-start | bytes 2949124
  33.4 4.2 %collective-permute-start.7 = (bf16[2,128,1920]{2,1,0:T(8,128)(2,1)S(1)}, bf16[2,128,1920]{2,1,0:T(8,128)(2,1)S(1)}, u32[]{:S(2)}, u32[]{:S(2)}) collective-permute-start(bf16[2,128,1920]{2,1,0:T(8,128)(2,1)S(1)} %get-tuple-element.168.first_ref), channel_id=1, source_target_pairs={{0,1},{1,0},{2,3},{3,2},{4,5},{5,4},{6,7},{7,6},{8,9},{9,8},{10,11... | collective-permute-start | bytes 2949128 | tf_op jit(solution)/shard_map/ppermute | solution.py:19
  33.5 24.2 %collective-permute-start.6 = (bf16[2,128,1920]{2,1,0:T(8,128)(2,1)S(1)}, bf16[2,128,1920]{2,1,0:T(8,128)(2,1)S(1)}, u32[]{:S(2)}, u32[]{:S(2)}) collective-permute-start(bf16[2,128,1920]{2,1,0:T(8,128)(2,1)S(1)} %get-tuple-element.214), channel_id=1, source_target_pairs={{0,2},{1,3},{2,0},{3,1},{4,6},{5,7},{6,4},{7,5},{8,10},{9,11},{10,... | collective-permute-start | bytes 2949128 | tf_op jit(solution)/shard_map/ppermute | solution.py:19
  34.1 23.6 %collective-permute-start.5 = (bf16[128,1920]{1,0:T(8,128)(2,1)S(1)}, bf16[128,1920]{1,0:T(8,128)(2,1)S(1)}, u32[]{:S(2)}, u32[]{:S(2)}) collective-permute-start(bf16[128,1920]{1,0:T(8,128)(2,1)S(1)} %collective-permute-done.other_ref), channel_id=1, source_target_pairs={{0,4},{1,5},{2,6},{3,7},{4,0},{5,1},{6,2},{7,3},{8,12},{9,13},{10,... | collective-permute-start | bytes 1474568 | tf_op jit(solution)/shard_map/ppermute | solution.py:19
  35.3 22.4 %collective-permute-start.4 = (bf16[112,2048]{1,0:T(8,128)(2,1)S(1)}, bf16[112,2048]{1,0:T(8,128)(2,1)S(1)}, u32[]{:S(2)}, u32[]{:S(2)}) collective-permute-start(bf16[112,2048]{1,0:T(8,128)(2,1)S(1)} %shard_map.91), channel_id=1, source_target_pairs={{0,8},{1,9},{2,10},{3,11},{4,12},{5,13},{6,14},{7,15},{8,0},{9,1},... | collective-permute-start | bytes 1376264 | tf_op jit(solution)/shard_map/ppermute | solution.py:19
  37.7 6.6 %copy-start.8 = (bf16[2,128,1920]{2,1,0:T(8,128)(2,1)}, bf16[2,128,1920]{2,1,0:T(8,128)(2,1)S(1)}, u32[]{:S(2)}) copy-start(bf16[2,128,1920]{2,1,0:T(8,128)(2,1)S(1)} %collective-permute-done.7.second_ref) | copy-start | bytes 2949124
  58.1 33.0 %collective-permute-start.10 = (bf16[4,128,1920]{2,1,0:T(8,128)(2,1)S(1)}, bf16[4,128,1920]{2,1,0:T(8,128)(2,1)S(1)}, u32[]{:S(2)}, u32[]{:S(2)}) collective-permute-start(bf16[4,128,1920]{2,1,0:T(8,128)(2,1)S(1)} %pad_maximum_fusion.1), channel_id=1, source_target_pairs={{0,1},{1,0},{2,3},{3,2},{4,5},{5,4},{6,7},{7,6},{8,9},{9,8},{10,11... | collective-permute-start | bytes 5898248 | tf_op jit(solution)/shard_map/ppermute | solution.py:19
  58.1 31.9 %collective-permute-start.11 = (bf16[1,224,1536]{2,1,0:T(8,128)(2,1)S(1)}, bf16[1,224,1536]{2,1,0:T(8,128)(2,1)S(1)}, u32[]{:S(2)}, u32[]{:S(2)}) collective-permute-start(bf16[1,224,1536]{2,1,0:T(8,128)(2,1)S(1)} %maximum_bitcast_fusion), channel_id=1, source_target_pairs={{0,4},{1,5},{2,6},{3,7},{4,0},{5,1},{6,2},{7,3},{8,12},{9,13},{10,... | collective-permute-start | bytes 2064392 | tf_op jit(solution)/shard_map/ppermute | solution.py:19
  59.5 43.5 %collective-permute-start.8 = (bf16[224,2048]{1,0:T(8,128)(2,1)S(1)}, bf16[224,2048]{1,0:T(8,128)(2,1)S(1)}, u32[]{:S(2)}, u32[]{:S(2)}) collective-permute-start(bf16[224,2048]{1,0:T(8,128)(2,1)S(1)} %shard_map.92), channel_id=1, source_target_pairs={{0,8},{1,9},{2,10},{3,11},{4,12},{5,13},{6,14},{7,15},{8,0},{9,1},... | collective-permute-start | bytes 2752520 | tf_op jit(solution)/shard_map/ppermute | solution.py:19
  90.2 12.9 %collective-permute-start.9 = (bf16[128,1920]{1,0:T(8,128)(2,1)S(1)}, bf16[128,1920]{1,0:T(8,128)(2,1)S(1)}, u32[]{:S(2)}, u32[]{:S(2)}) collective-permute-start(bf16[128,1920]{1,0:T(8,128)(2,1)S(1)} %collective-permute-done.5), channel_id=1, source_target_pairs={{0,2},{1,3},{2,0},{3,1},{4,6},{5,7},{6,4},{7,5},{8,10},{9,11},{10,... | collective-permute-start | bytes 1474568 | tf_op jit(solution)/shard_map/ppermute | solution.py:19
  103.0 31.0 %collective-permute-start.16 = (bf16[2,224,1536]{2,1,0:T(8,128)(2,1)S(1)}, bf16[2,224,1536]{2,1,0:T(8,128)(2,1)}, u32[]{:S(2)}, u32[]{:S(2)}) collective-permute-start(bf16[2,224,1536]{2,1,0:T(8,128)(2,1)S(1)} %pad_maximum_fusion.2), channel_id=1, source_target_pairs={{0,2},{1,3},{2,0},{3,1},{4,6},{5,7},{6,4},{7,5},{8,10},{9,11},{10,... | collective-permute-start | bytes 4128776 | tf_op jit(solution)/shard_map/ppermute | solution.py:19
  103.8 31.4 %collective-permute-start.15 = (bf16[2,224,1536]{2,1,0:T(8,128)(2,1)S(1)}, bf16[2,224,1536]{2,1,0:T(8,128)(2,1)}, u32[]{:S(2)}, u32[]{:S(2)}) collective-permute-start(bf16[2,224,1536]{2,1,0:T(8,128)(2,1)S(1)} %pad_maximum_fusion.2), channel_id=1, source_target_pairs={{0,16},{16,0},{1,17},{17,1},{2,18},{18,2},{3,19},{19,3},{4,20},{20... | collective-permute-start | bytes 4128776 | tf_op jit(solution)/shard_map/ppermute | solution.py:19
  105.3 35.4 %collective-permute-start.14 = (bf16[1,128,1920]{2,1,0:T(8,128)(2,1)S(1)}, bf16[1,128,1920]{2,1,0:T(8,128)(2,1)S(1)}, u32[]{:S(2)}, u32[]{:S(2)}) collective-permute-start(bf16[1,128,1920]{2,1,0:T(8,128)(2,1)S(1)} %bitcast.60), channel_id=1, source_target_pairs={{0,1},{1,0},{2,3},{3,2},{4,5},{5,4},{6,7},{7,6},{8,9},{9,8},{10,11... | collective-permute-start | bytes 1474568 | tf_op jit(solution)/shard_map/ppermute | solution.py:19
  105.3 35.4 %collective-permute-start.12 = (bf16[112,2048]{1,0:T(8,128)(2,1)S(1)}, bf16[112,2048]{1,0:T(8,128)(2,1)S(1)}, u32[]{:S(2)}, u32[]{:S(2)}) collective-permute-start(bf16[112,2048]{1,0:T(8,128)(2,1)S(1)} %shard_map.93), channel_id=1, source_target_pairs={{0,8},{1,9},{2,10},{3,11},{4,12},{5,13},{6,14},{7,15},{8,0},{9,1},... | collective-permute-start | bytes 1376264 | tf_op jit(solution)/shard_map/ppermute | solution.py:19
  106.5 34.2 %collective-permute-start.13 = (bf16[112,1024]{1,0:T(8,128)(2,1)S(1)}, bf16[112,1024]{1,0:T(8,128)(2,1)S(1)}, u32[]{:S(2)}, u32[]{:S(2)}) collective-permute-start(bf16[112,1024]{1,0:T(8,128)(2,1)S(1)} %shard_map.94.hid_ref), channel_id=1, source_target_pairs={{0,8},{1,9},{2,10},{3,11},{4,12},{5,13},{6,14},{7,15},{8,0},{9,1},... | collective-permute-start | bytes 688136 | tf_op jit(solution)/shard_map/ppermute | solution.py:19
  121.2 19.5 %copy-start.12 = (bf16[1,128,1792]{2,1,0:T(8,128)(2,1)}, bf16[1,128,1792]{2,1,0:T(8,128)(2,1)S(1)}, u32[]{:S(2)}) copy-start(bf16[1,128,1792]{2,1,0:T(8,128)(2,1)S(1)} %get-tuple-element.190) | copy-start | bytes 1376260
  140.7 26.1 %collective-permute-start.19 = (bf16[6,224,1536]{2,1,0:T(8,128)(2,1)}, bf16[6,224,1536]{2,1,0:T(8,128)(2,1)}, u32[]{:S(2)}, u32[]{:S(2)}) collective-permute-start(bf16[6,224,1536]{2,1,0:T(8,128)(2,1)} %pad_maximum_fusion.refs_0_), channel_id=1, source_target_pairs={{0,1},{1,0},{2,3},{3,2},{4,5},{5,4},{6,7},{7,6},{8,9},{9,8},{10,11... | collective-permute-start | bytes 12386312 | tf_op jit(solution)/shard_map/ppermute | solution.py:19
  140.9 8.5 %collective-permute-start.18 = (bf16[3,128,1792]{2,1,0:T(8,128)(2,1)S(1)}, bf16[3,128,1792]{2,1,0:T(8,128)(2,1)S(1)}, u32[]{:S(2)}, u32[]{:S(2)}) collective-permute-start(bf16[3,128,1792]{2,1,0:T(8,128)(2,1)S(1)} %pad_maximum_fusion.3), channel_id=1, source_target_pairs={{0,1},{1,0},{2,3},{3,2},{4,5},{5,4},{6,7},{7,6},{8,9},{9,8},{10,11... | collective-permute-start | bytes 4128776 | tf_op jit(solution)/shard_map/ppermute | solution.py:19
  141.5 25.3 %collective-permute-start.20 = (bf16[2,112,1536]{2,1,0:T(8,128)(2,1)}, bf16[2,112,1536]{2,1,0:T(8,128)(2,1)S(1)}, u32[]{:S(2)}, u32[]{:S(2)}) collective-permute-start(bf16[2,112,1536]{2,1,0:T(8,128)(2,1)} %slice.67), channel_id=1, source_target_pairs={{0,2},{1,3},{2,0},{3,1},{4,6},{5,7},{6,4},{7,5},{8,10},{9,11},{10,... | collective-permute-start | bytes 2064392 | tf_op jit(solution)/shard_map/ppermute | solution.py:19
  142.6 24.2 %collective-permute-start.21 = (bf16[2,112,1536]{2,1,0:T(8,128)(2,1)S(1)}, bf16[2,112,1536]{2,1,0:T(8,128)(2,1)S(1)}, u32[]{:S(2)}, u32[]{:S(2)}) collective-permute-start(bf16[2,112,1536]{2,1,0:T(8,128)(2,1)S(1)} %slice.68), channel_id=1, source_target_pairs={{0,16},{16,0},{1,17},{17,1},{2,18},{18,2},{3,19},{19,3},{4,20},{20... | collective-permute-start | bytes 2064392 | tf_op jit(solution)/shard_map/ppermute | solution.py:19
  144.1 22.7 %collective-permute-start.17 = (bf16[224,1024]{1,0:T(8,128)(2,1)S(1)}, bf16[224,1024]{1,0:T(8,128)(2,1)S(1)}, u32[]{:S(2)}, u32[]{:S(2)}) collective-permute-start(bf16[224,1024]{1,0:T(8,128)(2,1)S(1)} %shard_map.95.hid_ref), channel_id=1, source_target_pairs={{0,8},{1,9},{2,10},{3,11},{4,12},{5,13},{6,14},{7,15},{8,0},{9,1},... | collective-permute-start | bytes 1376264 | tf_op jit(solution)/shard_map/ppermute | solution.py:19
  149.4 19.2 %copy-start.18 = (bf16[3,128,1792]{2,1,0:T(8,128)(2,1)}, bf16[3,128,1792]{2,1,0:T(8,128)(2,1)S(1)}, u32[]{:S(2)}) copy-start(bf16[3,128,1792]{2,1,0:T(8,128)(2,1)S(1)} %collective-permute-done.18) | copy-start | bytes 4128772
  160.3 7.7 %copy-start.14 = (bf16[1,128,1792]{2,1,0:T(8,128)(2,1)}, bf16[1,128,1792]{2,1,0:T(8,128)(2,1)S(1)}, u32[]{:S(2)}) copy-start(bf16[1,128,1792]{2,1,0:T(8,128)(2,1)S(1)} %get-tuple-element.197) | copy-start | bytes 1376260
  167.9 20.2 %collective-permute-start.26 = (bf16[2,128,1792]{2,1,0:T(8,128)(2,1)}, bf16[2,128,1792]{2,1,0:T(8,128)(2,1)}, u32[]{:S(2)}, u32[]{:S(2)}) collective-permute-start(bf16[2,128,1792]{2,1,0:T(8,128)(2,1)} %pad_maximum_fusion.7), channel_id=1, source_target_pairs={{0,1},{1,0},{2,3},{3,2},{4,5},{5,4},{6,7},{7,6},{8,9},{9,8},{10,11... | collective-permute-start | bytes 2752520 | tf_op jit(solution)/shard_map/ppermute | solution.py:19
  168.0 5.3 %collective-permute-start.23 = (bf16[4,112,1536]{2,1,0:T(8,128)(2,1)S(1)}, bf16[4,112,1536]{2,1,0:T(8,128)(2,1)}, u32[]{:S(2)}, u32[]{:S(2)}) collective-permute-start(bf16[4,112,1536]{2,1,0:T(8,128)(2,1)S(1)} %constant_dynamic-update-slice_fusion.refs_1_), channel_id=1, source_target_pairs={{0,1},{1,0},{2,3},{3,2},{4,5},{5,4},{6,7},{7,6},{8,9},{9,8},{10,11... | collective-permute-start | bytes 4128776 | tf_op jit(solution)/shard_map/ppermute | solution.py:19
  169.8 16.0 %collective-permute-start.25 = (bf16[128,1792]{1,0:T(8,128)(2,1)}, bf16[128,1792]{1,0:T(8,128)(2,1)}, u32[]{:S(2)}, u32[]{:S(2)}) collective-permute-start(bf16[128,1792]{1,0:T(8,128)(2,1)} %get-tuple-element.209), channel_id=1, source_target_pairs={{0,2},{1,3},{2,0},{3,1},{4,6},{5,7},{6,4},{7,5},{8,10},{9,11},{10,... | collective-permute-start | bytes 1376264 | tf_op jit(solution)/shard_map/ppermute | solution.py:19
  170.7 17.4 %collective-permute-start.24 = (bf16[128,1792]{1,0:T(8,128)(2,1)}, bf16[128,1792]{1,0:T(8,128)(2,1)}, u32[]{:S(2)}, u32[]{:S(2)}) collective-permute-start(bf16[128,1792]{1,0:T(8,128)(2,1)} %get-tuple-element.210), channel_id=1, source_target_pairs={{0,4},{1,5},{2,6},{3,7},{4,0},{5,1},{6,2},{7,3},{8,12},{9,13},{10,... | collective-permute-start | bytes 1376264 | tf_op jit(solution)/shard_map/ppermute | solution.py:19
  170.7 15.1 %collective-permute-start.22 = (bf16[112,1024]{1,0:T(8,128)(2,1)S(1)}, bf16[112,1024]{1,0:T(8,128)(2,1)S(1)}, u32[]{:S(2)}, u32[]{:S(2)}) collective-permute-start(bf16[112,1024]{1,0:T(8,128)(2,1)S(1)} %shard_map.98.hid_ref), channel_id=1, source_target_pairs={{0,8},{1,9},{2,10},{3,11},{4,12},{5,13},{6,14},{7,15},{8,0},{9,1},... | collective-permute-start | bytes 688136 | tf_op jit(solution)/shard_map/ppermute | solution.py:19
  179.7 9.5 %copy-start.17 = (bf16[1,128,1792]{2,1,0:T(8,128)(2,1)S(1)}, bf16[1,128,1792]{2,1,0:T(8,128)(2,1)}, u32[]{:S(2)}) copy-start(bf16[1,128,1792]{2,1,0:T(8,128)(2,1)} %copy-done.16) | copy-start | bytes 1376260
  179.7 12.4 %copy-start.3 = (bf16[1024,1792]{1,0:T(8,128)(2,1)S(1)}, bf16[1024,1792]{1,0:T(8,128)(2,1)}, u32[]{:S(2)}) copy-start(bf16[1024,1792]{1,0:T(8,128)(2,1)} %w_ref.17) | copy-start | bytes 11010052
  179.8 12.4 %copy-start.7 = (bf16[1,128,1920]{2,1,0:T(8,128)(2,1)S(1)}, bf16[1,128,1920]{2,1,0:T(8,128)(2,1)}, u32[]{:S(2)}) copy-start(bf16[1,128,1920]{2,1,0:T(8,128)(2,1)} %copy-done.6) | copy-start | bytes 1474564
  188.1 27.4 %collective-permute-start.27 = (bf16[128,2048]{1,0:T(8,128)(2,1)S(1)}, bf16[128,2048]{1,0:T(8,128)(2,1)S(1)}, u32[]{:S(2)}, u32[]{:S(2)}) collective-permute-start(bf16[128,2048]{1,0:T(8,128)(2,1)S(1)} %get-tuple-element.174), channel_id=1, source_target_pairs={{0,8},{1,9},{2,10},{3,11},{4,12},{5,13},{6,14},{7,15},{8,0},{9,1},... | collective-permute-start | bytes 1572872 | tf_op jit(solution)/shard_map/ppermute | solution.py:19
  189.2 26.2 %collective-permute-start.29 = (bf16[2,128,1792]{2,1,0:T(8,128)(2,1)S(1)}, bf16[2,128,1792]{2,1,0:T(8,128)(2,1)S(1)}, u32[]{:S(2)}, u32[]{:S(2)}) collective-permute-start(bf16[2,128,1792]{2,1,0:T(8,128)(2,1)S(1)} %get-tuple-element.179), channel_id=1, source_target_pairs={{0,1},{1,0},{2,3},{3,2},{4,5},{5,4},{6,7},{7,6},{8,9},{9,8},{10,11... | collective-permute-start | bytes 2752520 | tf_op jit(solution)/shard_map/ppermute | solution.py:19
  190.4 25.0 %collective-permute-start.28 = (bf16[128,1792]{1,0:T(8,128)(2,1)S(1)}, bf16[128,1792]{1,0:T(8,128)(2,1)S(1)}, u32[]{:S(2)}, u32[]{:S(2)}) collective-permute-start(bf16[128,1792]{1,0:T(8,128)(2,1)S(1)} %fusion.9), channel_id=1, source_target_pairs={{0,6},{1,7},{2,4},{3,5},{4,2},{5,3},{6,0},{7,1},{8,14},{9,15},{10,... | collective-permute-start | bytes 1376264 | tf_op jit(solution)/shard_map/ppermute | solution.py:19
  215.7 13.8 %collective-permute-start.31 = (bf16[128,1024]{1,0:T(8,128)(2,1)S(1)}, bf16[128,1024]{1,0:T(8,128)(2,1)S(1)}, u32[]{:S(2)}, u32[]{:S(2)}) collective-permute-start(bf16[128,1024]{1,0:T(8,128)(2,1)S(1)} %fusion.8.hid_ref), channel_id=1, source_target_pairs={{0,8},{1,9},{2,10},{3,11},{4,12},{5,13},{6,14},{7,15},{8,0},{9,1},... | collective-permute-start | bytes 786440 | tf_op jit(solution)/shard_map/ppermute | solution.py:19
  215.8 8.7 %collective-permute-start.34 = (bf16[1,128,1792]{2,1,0:T(8,128)(2,1)S(1)}, bf16[1,128,1792]{2,1,0:T(8,128)(2,1)S(1)}, u32[]{:S(2)}, u32[]{:S(2)}) collective-permute-start(bf16[1,128,1792]{2,1,0:T(8,128)(2,1)S(1)} %get-tuple-element.200), channel_id=1, source_target_pairs={{0,1},{1,0},{2,3},{3,2},{4,5},{5,4},{6,7},{7,6},{8,9},{9,8},{10,11... | collective-permute-start | bytes 1376264 | tf_op jit(solution)/shard_map/ppermute | solution.py:19
  216.2 29.0 %collective-permute-start.33 = (bf16[128,1792]{1,0:T(8,128)(2,1)S(1)}, bf16[128,1792]{1,0:T(8,128)(2,1)S(1)}, u32[]{:S(2)}, u32[]{:S(2)}) collective-permute-start(bf16[128,1792]{1,0:T(8,128)(2,1)S(1)} %get-tuple-element.207), channel_id=1, source_target_pairs={{0,4},{1,5},{2,6},{3,7},{4,0},{5,1},{6,2},{7,3},{8,12},{9,13},{10,... | collective-permute-start | bytes 1376264 | tf_op jit(solution)/shard_map/ppermute | solution.py:19
  218.5 6.7 %copy-start.13 = (bf16[1,128,1792]{2,1,0:T(8,128)(2,1)S(1)}, bf16[1,128,1792]{2,1,0:T(8,128)(2,1)}, u32[]{:S(2)}) copy-start(bf16[1,128,1792]{2,1,0:T(8,128)(2,1)} %copy-done.12) | copy-start | bytes 1376260
  218.5 12.7 %collective-permute-start.32 = (bf16[128,1792]{1,0:T(8,128)(2,1)S(1)}, bf16[128,1792]{1,0:T(8,128)(2,1)S(1)}, u32[]{:S(2)}, u32[]{:S(2)}) collective-permute-start(bf16[128,1792]{1,0:T(8,128)(2,1)S(1)} %get-tuple-element.208), channel_id=1, source_target_pairs={{0,2},{1,3},{2,0},{3,1},{4,6},{5,7},{6,4},{7,5},{8,10},{9,11},{10,... | collective-permute-start | bytes 1376264 | tf_op jit(solution)/shard_map/ppermute | solution.py:19
  224.6 30.8 %collective-permute-start.35 = (bf16[128,1792]{1,0:T(8,128)(2,1)S(1)}, bf16[128,1792]{1,0:T(8,128)(2,1)S(1)}, u32[]{:S(2)}, u32[]{:S(2)}) collective-permute-start(bf16[128,1792]{1,0:T(8,128)(2,1)S(1)} %fusion.10), channel_id=1, source_target_pairs={{0,6},{1,7},{2,4},{3,5},{4,2},{5,3},{6,0},{7,1},{8,14},{9,15},{10,... | collective-permute-start | bytes 1376264 | tf_op jit(solution)/shard_map/ppermute | solution.py:19
  226.8 28.6 %copy-start.15 = (bf16[1,128,1792]{2,1,0:T(8,128)(2,1)S(1)}, bf16[1,128,1792]{2,1,0:T(8,128)(2,1)}, u32[]{:S(2)}) copy-start(bf16[1,128,1792]{2,1,0:T(8,128)(2,1)} %copy-done.14) | copy-start | bytes 1376260
  226.9 29.9 %collective-permute-start.30 = (bf16[128,1792]{1,0:T(8,128)(2,1)S(1)}, bf16[128,1792]{1,0:T(8,128)(2,1)S(1)}, u32[]{:S(2)}, u32[]{:S(2)}) collective-permute-start(bf16[128,1792]{1,0:T(8,128)(2,1)S(1)} %fusion.7), channel_id=1, source_target_pairs={{0,8},{1,9},{2,10},{3,11},{4,12},{5,13},{6,14},{7,15},{8,0},{9,1},... | collective-permute-start | bytes 1376264 | tf_op jit(solution)/shard_map/ppermute | solution.py:19
  231.1 26.8 %copy-start.1 = (bf16[224,2048]{1,0:T(8,128)(2,1)S(1)}, bf16[224,2048]{1,0:T(8,128)(2,1)}, u32[]{:S(2)}) copy-start(bf16[224,2048]{1,0:T(8,128)(2,1)} %param.12) | copy-start | bytes 2752516
  (8 other events, 36.4 us)

commit v5 on v4

--- a/solution.py
+++ b/solution.py
@@ -545,12 +545,14 @@
     away_far_hidden = hidden_of(away_far_tok, far_in)
     away_far_rows = rows_of(away_far_tok, away_far_hidden)
     own_rows = rows_of(own_tok, own_hidden)
+    blocks = list(summed(away_near_rows[0], away_others[1:]))
+    others = jnp.concatenate([own_rows[1], away_far_rows[1]])
     (
-        near_hidden, away_others, away_far_hidden, away_far_rows, own_rows, first, first_other,
-        lower, upper,
-    ) = settle(
-        near_hidden, away_others, away_far_hidden, away_far_rows, own_rows, first, first_other,
-        lower, upper,
+        near_hidden, blocks, others, away_others, away_far_hidden, away_far_rows, own_rows, first,
+        first_other, lower, upper,
+    ) = settle_round(
+        1, near_hidden, blocks, others, away_others, away_far_hidden, away_far_rows, own_rows,
+        first, first_other, lower, upper,
     )
 
     far_hidden = hop(away_far_hidden, half)
@@ -558,15 +560,16 @@
     stacks = first, second, first_other, hop(second, 1)
     shared_own, shared_other = shared_sums(stacks)
     near_hidden, shared_own = settle(near_hidden, shared_own)
-    parts = hops_of(summed(away_near_rows[0], away_others[1:]), near_chips)
-    others = hop(jnp.concatenate([own_rows[1], away_far_rows[1]]), 1)
+    parts = hops_of(blocks, near_chips)
+    others = hop(others, 1)
     near_rows = rows_of(near_tok, near_hidden)
-    far_hidden, stacks, shared_own, shared_other, parts, others, near_rows = settle(
-        far_hidden, stacks, shared_own, shared_other, parts, others, near_rows
+    blocks = list(summed(away_far_rows[0], others[1:]))
+    far_hidden, parts, stacks, shared_own, shared_other, others, near_rows, blocks = settle_round(
+        2, far_hidden, parts, stacks, shared_own, shared_other, others, near_rows, blocks
     )
 
     shared_in = hop(shared_own, half)
-    parts += hops_of(summed(away_far_rows[0], others[1:]), far_chips)
+    parts += hops_of(blocks, far_chips)
     near_others = hop(near_rows[1], 1)
     far_rows = rows_of(far_tok, far_hidden)
     shared_in, parts, near_others, far_rows = settle(shared_in, parts, near_others, far_rows)

time: 259 us -> 253 us (0.977)
  waiting for transfers between devices: 127 us -> 121 us
    ppermute x36, waiting for transfers between devices: 127 us -> 121 us  [hop(): return lax.ppermute(block, axis, [(d, d ^ mask) for d in range(count)])]
  transfers between devices with their start and end apart: 36 -> 36, of which waited for: 14 -> 15; matrix products, arithmetic and copies ran while one was open for 6% -> 6% of each run, Pallas kernels for 27% -> 27%
where the time goes in v5:
time: 253 us; the launch traced here: 252 us
  waiting for transfers between devices  121 us (48%)
  Pallas kernels  68.6 us (27%)
  starting transfers between devices  37.8 us (15%)
  other arithmetic  16.9 us (7%)
  local copies, waits for them, and re-layouts  6.7 us (3%)
    ppermute x36, waiting for transfers between devices, hop(): return lax.ppermute(block, axis, [(d, d ^ mask) for d in range(count)])  121 us
    ppermute x36, starting transfers between devices, hop(): return lax.ppermute(block, axis, [(d, d ^ mask) for d in range(count)])  37.8 us
    pallas_call x3, Pallas kernels, hidden_rows(): pl.pallas_call(functools.partial(hidden_kernel, cap), grid=(steps,), in_s...  17.6 us
    pallas_call x3, Pallas kernels, partial_sums(): pl.pallas_call(functools.partial(partial_kernel, cap), grid=(steps,), in_...  17.4 us
    pallas_call x6, Pallas kernels, weighted_rows(): pl.pallas_call(functools.partial(down_kernel, cap), grid=(steps,), in_spe...  17.4 us
    pallas_call x2, Pallas kernels, shared_rows(): pl.pallas_call(functools.partial(shared_down_kernel, masks, first_column)...  9.86 us
    pallas_call x1, Pallas kernels, shared_partial(): pl.pallas_call(functools.partial(shared_gate_kernel, masks), in_specs=[sm...  6.36 us
  transfers between devices with their start and end apart: 36, of which 15 were waited for; matrix products, arithmetic and copies ran while one was open for 6% of the time, Pallas kernels for 27%

profile of v5, /device:TPU:0, one launch (start us, length us, event | category | flops | bytes accessed | tf_op | source)
XLA Modules:
  0.0 251.9 jit_solution(2661586405286744415)
XLA Ops:
  2.6 1.2 broadcast_select_fusion
  4.6 3.7 %collective-permute-start = (bf16[128,1920]{1,0:T(8,128)(2,1)S(1)}, bf16[128,1920]{1,0:T(8,128)(2,1)S(1)}, u32[]{:S(2)}, u32[]{:S(2)}) collective-permute-start(bf16[128,1920]{1,0:T(8,128)(2,1)S(1)} %concatenate.39), channel_id=1, source_target_pairs={{0,8},{1,9},{2,10},{3,11},{4,12},{5,13},{6,14},{7,15},{8,0},{9,1},... | collective-permute-start | bytes 1474568 | tf_op jit(solution)/shard_map/ppermute | solution.py:19
  8.2 1.5 collective-permute-start.2
  9.7 1.6 collective-permute-start.1
  12.4 5.4 %shard_map.91 = bf16[112,2048]{1,0:T(8,128)(2,1)S(1)} custom-call(s32[1]{0:T(128)} %bitcast.4.pair_ref, bf16[1,128,1920]{2,1,0:T(8,128)(2,1)S(1)} %bitcast.53, bf16[1,128,1920]{2,1,0:T(8,128)(2,1)S(1)} %bitcast.58, bf16[1792,2048]{1,0:T(8,128)(2,1)} %wu_ref.5), custom_call_target="tpu_custom_call" | custom-call | tf_op jit(solution)/shard_map/pallas_call | solution.py:160
  17.8 13.0 %collective-permute-done.other_ref = bf16[128,1920]{1,0:T(8,128)(2,1)S(1)} collective-permute-done((bf16[128,1920]{1,0:T(8,128)(2,1)S(1)}, bf16[128,1920]{1,0:T(8,128)(2,1)S(1)}, u32[]{:S(2)}, u32[]{:S(2)}) %collective-permute-start) | collective-permute-done | bytes 491552 | tf_op jit(solution)/shard_map/ppermute | solution.py:19
  30.7 1.5 collective-permute-done.1
  32.3 1.4 pad_maximum_fusion.5
  35.6 2.2 collective-permute-start.4
  37.8 6.5 %shard_map.92 = bf16[224,2048]{1,0:T(8,128)(2,1)S(1)} custom-call(s32[1]{0:T(128)} %bitcast.4.pair_ref, bf16[2,128,1920]{2,1,0:T(8,128)(2,1)S(1)} %get-tuple-element.202.first_ref, bf16[2,128,1920]{2,1,0:T(8,128)(2,1)S(1)} %collective-permute-done.7.second_ref, bf16[1792,2048]{1,0:T(8,128)(2,1)} %wu_ref.5), custom_call_target="tpu_custom_call" | custom-call | tf_op jit(solution)/shard_map/pallas_call | solution.py:160
  44.4 13.6 %collective-permute-done.6 = bf16[2,128,1920]{2,1,0:T(8,128)(2,1)S(1)} collective-permute-done((bf16[2,128,1920]{2,1,0:T(8,128)(2,1)S(1)}, bf16[2,128,1920]{2,1,0:T(8,128)(2,1)S(1)}, u32[]{:S(2)}, u32[]{:S(2)}) %collective-permute-start.6) | collective-permute-done | bytes 983072 | tf_op jit(solution)/shard_map/ppermute | solution.py:19
  58.4 1.3 collective-permute-start.11
  59.7 1.9 collective-permute-start.8
  61.6 28.7 %collective-permute-done.11 = bf16[1,224,1536]{2,1,0:T(8,128)(2,1)S(1)} collective-permute-done((bf16[1,224,1536]{2,1,0:T(8,128)(2,1)S(1)}, bf16[1,224,1536]{2,1,0:T(8,128)(2,1)S(1)}, u32[]{:S(2)}, u32[]{:S(2)}) %collective-permute-start.11) | collective-permute-done | bytes 688160 | tf_op jit(solution)/shard_map/ppermute | solution.py:19
  91.4 5.5 %shard_map.93 = bf16[112,2048]{1,0:T(8,128)(2,1)S(1)} custom-call(s32[1]{0:T(128)} %bitcast.4.pair_ref, bf16[1,128,1920]{2,1,0:T(8,128)(2,1)S(1)} %bitcast.56, bf16[1,128,1920]{2,1,0:T(8,128)(2,1)S(1)} %get-tuple-element.225.second_ref, bf16[1792,2048]{1,0:T(8,128)(2,1)} %wu_ref.5), custom_call_target="tpu_custom_call" | custom-call | tf_op jit(solution)/shard_map/pallas_call | solution.py:160
  97.0 5.4 %shard_map.94.hid_ref = bf16[112,1024]{1,0:T(8,128)(2,1)S(1)} custom-call(s32[1]{0:T(128)} %bitcast.4.pair_ref, bf16[1,128,1920]{2,1,0:T(8,128)(2,1)S(1)} %bitcast.51, bf16[1,128,1920]{2,1,0:T(8,128)(2,1)S(1)} %get-tuple-element.143.second_ref, bf16[1792,2048]{1,0:T(8,128)(2,1)} %wu_ref.5, bf16[1792,2048]{1,0:T(8,128)(2,1)} %wu_ref.5, ...), custom_call_target="tpu_custom_call" | custom-call | tf_op jit(solution)/shard_map/pallas_call | solution.py:183
  104.0 1.5 collective-permute-start.15
  105.6 1.2 collective-permute-start.12
  106.8 1.7 collective-permute-start.13
  108.5 6.3 %shard_map.95.hid_ref = bf16[224,1024]{1,0:T(8,128)(2,1)S(1)} custom-call(s32[1]{0:T(128)} %bitcast.4.pair_ref, bf16[2,128,1920]{2,1,0:T(8,128)(2,1)S(1)} %pad_maximum_fusion.6.first_ref, bf16[2,128,1920]{2,1,0:T(8,128)(2,1)S(1)} %slice.64.second_ref, bf16[1792,2048]{1,0:T(8,128)(2,1)} %wu_ref.5, bf16[1792,2048]{1,0:T(8,128)(2,1)} %wu_ref.5, ...), custom_call_target="tpu_custom_call" | custom-call | tf_op jit(solution)/shard_map/pallas_call | solution.py:183
  114.8 4.5 %shard_map.97 = (bf16[2,128,1792]{2,1,0:T(8,128)(2,1)S(1)}, bf16[2,128,1792]{2,1,0:T(8,128)(2,1)S(1)}) custom-call(s32[1]{0:T(128)} %bitcast.4.pair_ref, bf16[2,128,1920]{2,1,0:T(8,128)(2,1)S(1)} %pad_maximum_fusion.6.first_ref, bf16[2,128,1920]{2,1,0:T(8,128)(2,1)S(1)} %slice.64.second_ref, bf16[224,1024]{1,0:T(8,128)(2,1)S(1)} %shard_map.95.hid_ref, ...), custom_call_target="tpu_custom_call" | custom-call | tf_op jit(solution)/shard_map/pallas_call | solution.py:210
  119.3 2.1 shard_map.96
  121.5 12.8 %collective-permute-done.16 = bf16[2,224,1536]{2,1,0:T(8,128)(2,1)} collective-permute-done((bf16[2,224,1536]{2,1,0:T(8,128)(2,1)S(1)}, bf16[2,224,1536]{2,1,0:T(8,128)(2,1)}, u32[]{:S(2)}, u32[]{:S(2)}) %collective-permute-start.16) | collective-permute-done | bytes 1376288 | tf_op jit(solution)/shard_map/ppermute | solution.py:19
  136.6 3.5 %pad_maximum_fusion.refs_0_ = bf16[6,224,1536]{2,1,0:T(8,128)(2,1)} fusion(bf16[2,224,1536]{2,1,0:T(8,128)(2,1)} %collective-permute-done.16, bf16[2,224,1536]{2,1,0:T(8,128)(2,1)} %collective-permute-done.15, bf16[2,224,1536]{2,1,0:T(8,128)(2,1)S(1)} %pad_maximum_fusion.2), kind=kLoop, calls=%fused_computation | loop fusion | flops 4128768 | bytes 8257536 | tf_op jit(solution)/shard_map/concatenate | solution.py:528
  142.9 1.5 collective-permute-start.21
  144.4 4.5 %collective-permute-done.18 = bf16[3,128,1792]{2,1,0:T(8,128)(2,1)S(1)} collective-permute-done((bf16[3,128,1792]{2,1,0:T(8,128)(2,1)S(1)}, bf16[3,128,1792]{2,1,0:T(8,128)(2,1)S(1)}, u32[]{:S(2)}, u32[]{:S(2)}) %collective-permute-start.18) | collective-permute-done | bytes 1376288 | tf_op jit(solution)/shard_map/ppermute | solution.py:19
  148.9 5.9 %shard_map.99.hid_ref = bf16[112,1024]{1,0:T(8,128)(2,1)S(1)} custom-call(s32[1]{0:T(128)} %bitcast.4.pair_ref, bf16[1,128,1920]{2,1,0:T(8,128)(2,1)S(1)} %bitcast.61, bf16[1,128,1920]{2,1,0:T(8,128)(2,1)S(1)} %collective-permute-done.14.second_ref, bf16[1792,2048]{1,0:T(8,128)(2,1)} %wu_ref.5, bf16[1792,2048]{1,0:T(8,128)(2,1)} %wu_ref.5, ...), custom_call_target="tpu_custom_call" | custom-call | tf_op jit(solution)/shard_map/pallas_call | solution.py:183
  154.7 2.1 shard_map.100
  157.6 2.1 shard_map.98
  162.0 2.1 collective-permute-done.17.hid_ref
  165.0 2.6 %collective-permute-start.23 = (bf16[128,1792]{1,0:T(8,128)(2,1)}, bf16[128,1792]{1,0:T(8,128)(2,1)S(1)}, u32[]{:S(2)}, u32[]{:S(2)}) collective-permute-start(bf16[128,1792]{1,0:T(8,128)(2,1)} %get-tuple-element.191), channel_id=1, source_target_pairs={{0,4},{1,5},{2,6},{3,7},{4,0},{5,1},{6,2},{7,3},{8,12},{9,13},{10,... | collective-permute-start | bytes 1376264 | tf_op jit(solution)/shard_map/ppermute | solution.py:19
  168.5 2.0 fusion.9
  170.5 6.4 %shard_map.101 = (bf16[128,2048]{1,0:T(8,128)(2,1)S(1)}, f32[128,2048]{1,0:T(8,128)S(1)}) custom-call(s32[22]{0:T(128)S(1)} %pad_add_fusion.spots_ref, bf16[128,1920]{1,0:T(8,128)(2,1)S(1)} %concatenate.40.own_ref, bf16[128,1920]{1,0:T(8,128)(2,1)S(1)} %collective-permute-done.other_ref, bf16[6,224,1536]{2,1,0:T(8,128)(2,1)} %pad_maximum_fusion.refs_0_, ...), custom_call_target="tpu_custom_call" | custom-call | tf_op jit(solution)/shard_map/pallas_call | solution.py:274
  176.9 4.5 %shard_map.102 = (bf16[2,128,1792]{2,1,0:T(8,128)(2,1)S(1)}, bf16[2,128,1792]{2,1,0:T(8,128)(2,1)S(1)}) custom-call(s32[1]{0:T(128)} %bitcast.4.pair_ref, bf16[2,128,1920]{2,1,0:T(8,128)(2,1)S(1)} %copy-done.5, bf16[2,128,1920]{2,1,0:T(8,128)(2,1)S(1)} %copy-done.9, bf16[224,1024]{1,0:T(8,128)(2,1)S(1)} %copy-done.11, bf16[1024,1792]{1,0:T(8,128)(2,1)} %w_ref.17), custom_call_target="tpu_custom_call" | custom-call | tf_op jit(solution)/shard_map/pallas_call | solution.py:210
  181.4 2.2 collective-permute-done.23
  183.8 2.9 %collective-permute-start.28 = (bf16[128,1792]{1,0:T(8,128)(2,1)}, bf16[128,1792]{1,0:T(8,128)(2,1)S(1)}, u32[]{:S(2)}, u32[]{:S(2)}) collective-permute-start(bf16[128,1792]{1,0:T(8,128)(2,1)} %fusion.9), channel_id=1, source_target_pairs={{0,6},{1,7},{2,4},{3,5},{4,2},{5,3},{6,0},{7,1},{8,14},{9,15},{10,... | collective-permute-start | bytes 1376264 | tf_op jit(solution)/shard_map/ppermute | solution.py:19
  186.6 2.1 shard_map.103
  188.7 17.0 %collective-permute-done.28 = bf16[128,1792]{1,0:T(8,128)(2,1)S(1)} collective-permute-done((bf16[128,1792]{1,0:T(8,128)(2,1)}, bf16[128,1792]{1,0:T(8,128)(2,1)S(1)}, u32[]{:S(2)}, u32[]{:S(2)}) %collective-permute-start.28) | collective-permute-done | bytes 458784 | tf_op jit(solution)/shard_map/ppermute | solution.py:19
  205.8 3.5 %collective-permute-done.27 = bf16[128,2048]{1,0:T(8,128)(2,1)S(1)} collective-permute-done((bf16[128,2048]{1,0:T(8,128)(2,1)S(1)}, bf16[128,2048]{1,0:T(8,128)(2,1)S(1)}, u32[]{:S(2)}, u32[]{:S(2)}) %collective-permute-start.27) | collective-permute-done | bytes 524320 | tf_op jit(solution)/shard_map/ppermute | solution.py:19
  210.1 2.5 collective-permute-start.33
  213.5 4.9 %shard_map.104 = bf16[128,1792]{1,0:T(8,128)(2,1)S(1)} custom-call(s32[22]{0:T(128)S(1)} %pad_add_fusion.spots_ref, bf16[128,1024]{1,0:T(8,128)(2,1)S(1)} %fusion.8.hid_ref, bf16[6,224,1536]{2,1,0:T(8,128)(2,1)} %pad_maximum_fusion.refs_0_, bf16[4,112,1536]{2,1,0:T(8,128)(2,1)S(1)} %constant_dynamic-update-slice_fusion.refs_1_, ...), custom_call_target="tpu_custom_call" | custom-call | tf_op jit(solution)/shard_map/pallas_call | solution.py:308
  219.2 1.4 fusion.7
  220.7 2.3 collective-permute-start.30
  223.9 1.3 collective-permute-done.32
  225.2 4.9 %shard_map.105 = bf16[128,1792]{1,0:T(8,128)(2,1)S(1)} custom-call(s32[22]{0:T(128)S(1)} %pad_add_fusion.spots_ref, bf16[128,1024]{1,0:T(8,128)(2,1)S(1)} %collective-permute-done.31.hid_ref, bf16[6,224,1536]{2,1,0:T(8,128)(2,1)} %pad_maximum_fusion.refs_0_, bf16[4,112,1536]{2,1,0:T(8,128)(2,1)S(1)} %constant_dynamic-update-slice_fusion.refs_1_, ...), custom_call_target="tpu_custom_call" | custom-call | tf_op jit(solution)/shard_map/pallas_call | solution.py:308
  230.2 9.1 %collective-permute-done.33 = bf16[128,1792]{1,0:T(8,128)(2,1)S(1)} collective-permute-done((bf16[128,1792]{1,0:T(8,128)(2,1)S(1)}, bf16[128,1792]{1,0:T(8,128)(2,1)S(1)}, u32[]{:S(2)}, u32[]{:S(2)}) %collective-permute-start.33) | collective-permute-done | bytes 458784 | tf_op jit(solution)/shard_map/ppermute | solution.py:19
  239.3 10.0 %collective-permute-done.35 = bf16[128,1792]{1,0:T(8,128)(2,1)S(1)} collective-permute-done((bf16[128,1792]{1,0:T(8,128)(2,1)S(1)}, bf16[128,1792]{1,0:T(8,128)(2,1)S(1)}, u32[]{:S(2)}, u32[]{:S(2)}) %collective-permute-start.35) | collective-permute-done | bytes 458784 | tf_op jit(solution)/shard_map/ppermute | solution.py:19
  249.3 1.4 fusion.3
  (120 shorter events, 23.8 us)
Async XLA Ops:
  0.0 12.3 %copy-start = (bf16[224,2048]{1,0:T(8,128)(2,1)S(1)}, bf16[224,2048]{1,0:T(8,128)(2,1)}, u32[]{:S(2)}) copy-start(bf16[224,2048]{1,0:T(8,128)(2,1)} %param.12) | copy-start | bytes 2752516
  3.9 8.5 %collective-permute-start.3 = (bf16[128,1920]{1,0:T(8,128)(2,1)S(1)}, bf16[128,1920]{1,0:T(8,128)(2,1)S(1)}, u32[]{:S(2)}, u32[]{:S(2)}) collective-permute-start(bf16[128,1920]{1,0:T(8,128)(2,1)S(1)} %concatenate.40.own_ref), channel_id=1, source_target_pairs={{0,1},{1,0},{2,3},{3,2},{4,5},{5,4},{6,7},{7,6},{8,9},{9,8},{10,11... | collective-permute-start | bytes 1474568 | tf_op jit(solution)/shard_map/ppermute | solution.py:19
  4.6 26.2 %collective-permute-start = (bf16[128,1920]{1,0:T(8,128)(2,1)S(1)}, bf16[128,1920]{1,0:T(8,128)(2,1)S(1)}, u32[]{:S(2)}, u32[]{:S(2)}) collective-permute-start(bf16[128,1920]{1,0:T(8,128)(2,1)S(1)} %concatenate.39), channel_id=1, source_target_pairs={{0,8},{1,9},{2,10},{3,11},{4,12},{5,13},{6,14},{7,15},{8,0},{9,1},... | collective-permute-start | bytes 1474568 | tf_op jit(solution)/shard_map/ppermute | solution.py:19
  8.2 22.5 %collective-permute-start.2 = (bf16[128,1920]{1,0:T(8,128)(2,1)S(1)}, bf16[128,1920]{1,0:T(8,128)(2,1)S(1)}, u32[]{:S(2)}, u32[]{:S(2)}) collective-permute-start(bf16[128,1920]{1,0:T(8,128)(2,1)S(1)} %concatenate.40.own_ref), channel_id=1, source_target_pairs={{0,2},{1,3},{2,0},{3,1},{4,6},{5,7},{6,4},{7,5},{8,10},{9,11},{10,... | collective-permute-start | bytes 1474568 | tf_op jit(solution)/shard_map/ppermute | solution.py:19
  9.7 22.5 %collective-permute-start.1 = (bf16[128,1920]{1,0:T(8,128)(2,1)S(1)}, bf16[128,1920]{1,0:T(8,128)(2,1)}, u32[]{:S(2)}, u32[]{:S(2)}) collective-permute-start(bf16[128,1920]{1,0:T(8,128)(2,1)S(1)} %concatenate.40.own_ref), channel_id=1, source_target_pairs={{0,4},{1,5},{2,6},{3,7},{4,0},{5,1},{6,2},{7,3},{8,12},{9,13},{10,... | collective-permute-start | bytes 1474568 | tf_op jit(solution)/shard_map/ppermute | solution.py:19
  33.7 10.7 %copy-start.4 = (bf16[2,128,1920]{2,1,0:T(8,128)(2,1)}, bf16[2,128,1920]{2,1,0:T(8,128)(2,1)S(1)}, u32[]{:S(2)}) copy-start(bf16[2,128,1920]{2,1,0:T(8,128)(2,1)S(1)} %get-tuple-element.202.first_ref) | copy-start | bytes 2949124
  33.7 4.1 %collective-permute-start.7 = (bf16[2,128,1920]{2,1,0:T(8,128)(2,1)S(1)}, bf16[2,128,1920]{2,1,0:T(8,128)(2,1)S(1)}, u32[]{:S(2)}, u32[]{:S(2)}) collective-permute-start(bf16[2,128,1920]{2,1,0:T(8,128)(2,1)S(1)} %get-tuple-element.202.first_ref), channel_id=1, source_target_pairs={{0,1},{1,0},{2,3},{3,2},{4,5},{5,4},{6,7},{7,6},{8,9},{9,8},{10,11... | collective-permute-start | bytes 2949128 | tf_op jit(solution)/shard_map/ppermute | solution.py:19
  33.8 24.2 %collective-permute-start.6 = (bf16[2,128,1920]{2,1,0:T(8,128)(2,1)S(1)}, bf16[2,128,1920]{2,1,0:T(8,128)(2,1)S(1)}, u32[]{:S(2)}, u32[]{:S(2)}) collective-permute-start(bf16[2,128,1920]{2,1,0:T(8,128)(2,1)S(1)} %get-tuple-element.260), channel_id=1, source_target_pairs={{0,2},{1,3},{2,0},{3,1},{4,6},{5,7},{6,4},{7,5},{8,10},{9,11},{10,... | collective-permute-start | bytes 2949128 | tf_op jit(solution)/shard_map/ppermute | solution.py:19
  34.4 23.6 %collective-permute-start.5 = (bf16[128,1920]{1,0:T(8,128)(2,1)S(1)}, bf16[128,1920]{1,0:T(8,128)(2,1)S(1)}, u32[]{:S(2)}, u32[]{:S(2)}) collective-permute-start(bf16[128,1920]{1,0:T(8,128)(2,1)S(1)} %collective-permute-done.other_ref), channel_id=1, source_target_pairs={{0,4},{1,5},{2,6},{3,7},{4,0},{5,1},{6,2},{7,3},{8,12},{9,13},{10,... | collective-permute-start | bytes 1474568 | tf_op jit(solution)/shard_map/ppermute | solution.py:19
  35.6 22.4 %collective-permute-start.4 = (bf16[112,2048]{1,0:T(8,128)(2,1)S(1)}, bf16[112,2048]{1,0:T(8,128)(2,1)S(1)}, u32[]{:S(2)}, u32[]{:S(2)}) collective-permute-start(bf16[112,2048]{1,0:T(8,128)(2,1)S(1)} %shard_map.91), channel_id=1, source_target_pairs={{0,8},{1,9},{2,10},{3,11},{4,12},{5,13},{6,14},{7,15},{8,0},{9,1},... | collective-permute-start | bytes 1376264 | tf_op jit(solution)/shard_map/ppermute | solution.py:19
  37.8 6.6 %copy-start.8 = (bf16[2,128,1920]{2,1,0:T(8,128)(2,1)}, bf16[2,128,1920]{2,1,0:T(8,128)(2,1)S(1)}, u32[]{:S(2)}) copy-start(bf16[2,128,1920]{2,1,0:T(8,128)(2,1)S(1)} %collective-permute-done.7.second_ref) | copy-start | bytes 2949124
  58.3 33.0 %collective-permute-start.10 = (bf16[4,128,1920]{2,1,0:T(8,128)(2,1)S(1)}, bf16[4,128,1920]{2,1,0:T(8,128)(2,1)S(1)}, u32[]{:S(2)}, u32[]{:S(2)}) collective-permute-start(bf16[4,128,1920]{2,1,0:T(8,128)(2,1)S(1)} %pad_maximum_fusion.1), channel_id=1, source_target_pairs={{0,1},{1,0},{2,3},{3,2},{4,5},{5,4},{6,7},{7,6},{8,9},{9,8},{10,11... | collective-permute-start | bytes 5898248 | tf_op jit(solution)/shard_map/ppermute | solution.py:19
  58.4 31.9 %collective-permute-start.11 = (bf16[1,224,1536]{2,1,0:T(8,128)(2,1)S(1)}, bf16[1,224,1536]{2,1,0:T(8,128)(2,1)S(1)}, u32[]{:S(2)}, u32[]{:S(2)}) collective-permute-start(bf16[1,224,1536]{2,1,0:T(8,128)(2,1)S(1)} %maximum_bitcast_fusion), channel_id=1, source_target_pairs={{0,4},{1,5},{2,6},{3,7},{4,0},{5,1},{6,2},{7,3},{8,12},{9,13},{10,... | collective-permute-start | bytes 2064392 | tf_op jit(solution)/shard_map/ppermute | solution.py:19
  59.7 43.6 %collective-permute-start.8 = (bf16[224,2048]{1,0:T(8,128)(2,1)S(1)}, bf16[224,2048]{1,0:T(8,128)(2,1)S(1)}, u32[]{:S(2)}, u32[]{:S(2)}) collective-permute-start(bf16[224,2048]{1,0:T(8,128)(2,1)S(1)} %shard_map.92), channel_id=1, source_target_pairs={{0,8},{1,9},{2,10},{3,11},{4,12},{5,13},{6,14},{7,15},{8,0},{9,1},... | collective-permute-start | bytes 2752520 | tf_op jit(solution)/shard_map/ppermute | solution.py:19
  90.5 12.9 %collective-permute-start.9 = (bf16[128,1920]{1,0:T(8,128)(2,1)S(1)}, bf16[128,1920]{1,0:T(8,128)(2,1)S(1)}, u32[]{:S(2)}, u32[]{:S(2)}) collective-permute-start(bf16[128,1920]{1,0:T(8,128)(2,1)S(1)} %collective-permute-done.5), channel_id=1, source_target_pairs={{0,2},{1,3},{2,0},{3,1},{4,6},{5,7},{6,4},{7,5},{8,10},{9,11},{10,... | collective-permute-start | bytes 1474568 | tf_op jit(solution)/shard_map/ppermute | solution.py:19
  103.3 31.0 %collective-permute-start.16 = (bf16[2,224,1536]{2,1,0:T(8,128)(2,1)S(1)}, bf16[2,224,1536]{2,1,0:T(8,128)(2,1)}, u32[]{:S(2)}, u32[]{:S(2)}) collective-permute-start(bf16[2,224,1536]{2,1,0:T(8,128)(2,1)S(1)} %pad_maximum_fusion.2), channel_id=1, source_target_pairs={{0,2},{1,3},{2,0},{3,1},{4,6},{5,7},{6,4},{7,5},{8,10},{9,11},{10,... | collective-permute-start | bytes 4128776 | tf_op jit(solution)/shard_map/ppermute | solution.py:19
  104.0 31.4 %collective-permute-start.15 = (bf16[2,224,1536]{2,1,0:T(8,128)(2,1)S(1)}, bf16[2,224,1536]{2,1,0:T(8,128)(2,1)}, u32[]{:S(2)}, u32[]{:S(2)}) collective-permute-start(bf16[2,224,1536]{2,1,0:T(8,128)(2,1)S(1)} %pad_maximum_fusion.2), channel_id=1, source_target_pairs={{0,16},{16,0},{1,17},{17,1},{2,18},{18,2},{3,19},{19,3},{4,20},{20... | collective-permute-start | bytes 4128776 | tf_op jit(solution)/shard_map/ppermute | solution.py:19
  105.6 34.5 %collective-permute-start.14 = (bf16[1,128,1920]{2,1,0:T(8,128)(2,1)S(1)}, bf16[1,128,1920]{2,1,0:T(8,128)(2,1)S(1)}, u32[]{:S(2)}, u32[]{:S(2)}) collective-permute-start(bf16[1,128,1920]{2,1,0:T(8,128)(2,1)S(1)} %bitcast.60), channel_id=1, source_target_pairs={{0,1},{1,0},{2,3},{3,2},{4,5},{5,4},{6,7},{7,6},{8,9},{9,8},{10,11... | collective-permute-start | bytes 1474568 | tf_op jit(solution)/shard_map/ppermute | solution.py:19
  105.6 34.5 %collective-permute-start.12 = (bf16[112,2048]{1,0:T(8,128)(2,1)S(1)}, bf16[112,2048]{1,0:T(8,128)(2,1)S(1)}, u32[]{:S(2)}, u32[]{:S(2)}) collective-permute-start(bf16[112,2048]{1,0:T(8,128)(2,1)S(1)} %shard_map.93), channel_id=1, source_target_pairs={{0,8},{1,9},{2,10},{3,11},{4,12},{5,13},{6,14},{7,15},{8,0},{9,1},... | collective-permute-start | bytes 1376264 | tf_op jit(solution)/shard_map/ppermute | solution.py:19
  106.8 33.3 %collective-permute-start.13 = (bf16[112,1024]{1,0:T(8,128)(2,1)S(1)}, bf16[112,1024]{1,0:T(8,128)(2,1)S(1)}, u32[]{:S(2)}, u32[]{:S(2)}) collective-permute-start(bf16[112,1024]{1,0:T(8,128)(2,1)S(1)} %shard_map.94.hid_ref), channel_id=1, source_target_pairs={{0,8},{1,9},{2,10},{3,11},{4,12},{5,13},{6,14},{7,15},{8,0},{9,1},... | collective-permute-start | bytes 688136 | tf_op jit(solution)/shard_map/ppermute | solution.py:19
  121.5 18.6 %copy-start.12 = (bf16[1,128,1792]{2,1,0:T(8,128)(2,1)}, bf16[1,128,1792]{2,1,0:T(8,128)(2,1)S(1)}, u32[]{:S(2)}) copy-start(bf16[1,128,1792]{2,1,0:T(8,128)(2,1)S(1)} %get-tuple-element.234) | copy-start | bytes 1376260
  140.1 21.9 %collective-permute-start.19 = (bf16[6,224,1536]{2,1,0:T(8,128)(2,1)}, bf16[6,224,1536]{2,1,0:T(8,128)(2,1)}, u32[]{:S(2)}, u32[]{:S(2)}) collective-permute-start(bf16[6,224,1536]{2,1,0:T(8,128)(2,1)} %pad_maximum_fusion.refs_0_), channel_id=1, source_target_pairs={{0,1},{1,0},{2,3},{3,2},{4,5},{5,4},{6,7},{7,6},{8,9},{9,8},{10,11... | collective-permute-start | bytes 12386312 | tf_op jit(solution)/shard_map/ppermute | solution.py:19
  140.3 8.5 %collective-permute-start.18 = (bf16[3,128,1792]{2,1,0:T(8,128)(2,1)S(1)}, bf16[3,128,1792]{2,1,0:T(8,128)(2,1)S(1)}, u32[]{:S(2)}, u32[]{:S(2)}) collective-permute-start(bf16[3,128,1792]{2,1,0:T(8,128)(2,1)S(1)} %pad_maximum_fusion.3), channel_id=1, source_target_pairs={{0,1},{1,0},{2,3},{3,2},{4,5},{5,4},{6,7},{7,6},{8,9},{9,8},{10,11... | collective-permute-start | bytes 4128776 | tf_op jit(solution)/shard_map/ppermute | solution.py:19
  140.9 23.2 %collective-permute-start.17 = (bf16[224,1024]{1,0:T(8,128)(2,1)S(1)}, bf16[224,1024]{1,0:T(8,128)(2,1)S(1)}, u32[]{:S(2)}, u32[]{:S(2)}) collective-permute-start(bf16[224,1024]{1,0:T(8,128)(2,1)S(1)} %shard_map.95.hid_ref), channel_id=1, source_target_pairs={{0,8},{1,9},{2,10},{3,11},{4,12},{5,13},{6,14},{7,15},{8,0},{9,1},... | collective-permute-start | bytes 1376264 | tf_op jit(solution)/shard_map/ppermute | solution.py:19
  142.0 20.0 %collective-permute-start.20 = (bf16[2,112,1536]{2,1,0:T(8,128)(2,1)S(1)}, bf16[2,112,1536]{2,1,0:T(8,128)(2,1)S(1)}, u32[]{:S(2)}, u32[]{:S(2)}) collective-permute-start(bf16[2,112,1536]{2,1,0:T(8,128)(2,1)S(1)} %slice.67), channel_id=1, source_target_pairs={{0,2},{1,3},{2,0},{3,1},{4,6},{5,7},{6,4},{7,5},{8,10},{9,11},{10,... | collective-permute-start | bytes 2064392 | tf_op jit(solution)/shard_map/ppermute | solution.py:19
  142.9 19.1 %collective-permute-start.21 = (bf16[2,112,1536]{2,1,0:T(8,128)(2,1)S(1)}, bf16[2,112,1536]{2,1,0:T(8,128)(2,1)S(1)}, u32[]{:S(2)}, u32[]{:S(2)}) collective-permute-start(bf16[2,112,1536]{2,1,0:T(8,128)(2,1)S(1)} %slice.68), channel_id=1, source_target_pairs={{0,16},{16,0},{1,17},{17,1},{2,18},{18,2},{3,19},{19,3},{4,20},{20... | collective-permute-start | bytes 2064392 | tf_op jit(solution)/shard_map/ppermute | solution.py:19
  148.9 10.9 %copy-start.17 = (bf16[3,128,1792]{2,1,0:T(8,128)(2,1)}, bf16[3,128,1792]{2,1,0:T(8,128)(2,1)S(1)}, u32[]{:S(2)}) copy-start(bf16[3,128,1792]{2,1,0:T(8,128)(2,1)S(1)} %collective-permute-done.18) | copy-start | bytes 4128772
  164.1 4.3 %collective-permute-start.26 = (bf16[2,128,1792]{2,1,0:T(8,128)(2,1)}, bf16[2,128,1792]{2,1,0:T(8,128)(2,1)}, u32[]{:S(2)}, u32[]{:S(2)}) collective-permute-start(bf16[2,128,1792]{2,1,0:T(8,128)(2,1)} %pad_maximum_fusion.7), channel_id=1, source_target_pairs={{0,1},{1,0},{2,3},{3,2},{4,5},{5,4},{6,7},{7,6},{8,9},{9,8},{10,11... | collective-permute-start | bytes 2752520 | tf_op jit(solution)/shard_map/ppermute | solution.py:19
  164.9 5.6 %collective-permute-start.25 = (bf16[4,112,1536]{2,1,0:T(8,128)(2,1)S(1)}, bf16[4,112,1536]{2,1,0:T(8,128)(2,1)}, u32[]{:S(2)}, u32[]{:S(2)}) collective-permute-start(bf16[4,112,1536]{2,1,0:T(8,128)(2,1)S(1)} %constant_dynamic-update-slice_fusion.refs_1_), channel_id=1, source_target_pairs={{0,1},{1,0},{2,3},{3,2},{4,5},{5,4},{6,7},{7,6},{8,9},{9,8},{10,11... | collective-permute-start | bytes 4128776 | tf_op jit(solution)/shard_map/ppermute | solution.py:19
  165.0 16.4 %collective-permute-start.22 = (bf16[112,1024]{1,0:T(8,128)(2,1)S(1)}, bf16[112,1024]{1,0:T(8,128)(2,1)S(1)}, u32[]{:S(2)}, u32[]{:S(2)}) collective-permute-start(bf16[112,1024]{1,0:T(8,128)(2,1)S(1)} %shard_map.99.hid_ref), channel_id=1, source_target_pairs={{0,8},{1,9},{2,10},{3,11},{4,12},{5,13},{6,14},{7,15},{8,0},{9,1},... | collective-permute-start | bytes 688136 | tf_op jit(solution)/shard_map/ppermute | solution.py:19
  165.0 18.6 %collective-permute-start.23 = (bf16[128,1792]{1,0:T(8,128)(2,1)}, bf16[128,1792]{1,0:T(8,128)(2,1)S(1)}, u32[]{:S(2)}, u32[]{:S(2)}) collective-permute-start(bf16[128,1792]{1,0:T(8,128)(2,1)} %get-tuple-element.191), channel_id=1, source_target_pairs={{0,4},{1,5},{2,6},{3,7},{4,0},{5,1},{6,2},{7,3},{8,12},{9,13},{10,... | collective-permute-start | bytes 1376264 | tf_op jit(solution)/shard_map/ppermute | solution.py:19
  167.6 16.0 %collective-permute-start.24 = (bf16[128,1792]{1,0:T(8,128)(2,1)}, bf16[128,1792]{1,0:T(8,128)(2,1)S(1)}, u32[]{:S(2)}, u32[]{:S(2)}) collective-permute-start(bf16[128,1792]{1,0:T(8,128)(2,1)} %get-tuple-element.192), channel_id=1, source_target_pairs={{0,2},{1,3},{2,0},{3,1},{4,6},{5,7},{6,4},{7,5},{8,10},{9,11},{10,... | collective-permute-start | bytes 1376264 | tf_op jit(solution)/shard_map/ppermute | solution.py:19
  170.5 6.4 %copy-start.9 = (bf16[2,128,1920]{2,1,0:T(8,128)(2,1)S(1)}, bf16[2,128,1920]{2,1,0:T(8,128)(2,1)}, u32[]{:S(2)}) copy-start(bf16[2,128,1920]{2,1,0:T(8,128)(2,1)} %copy-done.8) | copy-start | bytes 2949124
  170.5 6.4 %copy-start.11 = (bf16[224,1024]{1,0:T(8,128)(2,1)S(1)}, bf16[224,1024]{1,0:T(8,128)(2,1)}, u32[]{:S(2)}) copy-start(bf16[224,1024]{1,0:T(8,128)(2,1)} %copy-done.10) | copy-start | bytes 1376260
  176.9 9.7 %copy-start.3 = (bf16[1024,1792]{1,0:T(8,128)(2,1)S(1)}, bf16[1024,1792]{1,0:T(8,128)(2,1)}, u32[]{:S(2)}) copy-start(bf16[1024,1792]{1,0:T(8,128)(2,1)} %w_ref.17) | copy-start | bytes 11010052
  176.9 9.7 %copy-start.7 = (bf16[1,128,1920]{2,1,0:T(8,128)(2,1)S(1)}, bf16[1,128,1920]{2,1,0:T(8,128)(2,1)}, u32[]{:S(2)}) copy-start(bf16[1,128,1920]{2,1,0:T(8,128)(2,1)} %copy-done.6) | copy-start | bytes 1474564
  183.6 25.6 %collective-permute-start.29 = (bf16[2,128,1792]{2,1,0:T(8,128)(2,1)S(1)}, bf16[2,128,1792]{2,1,0:T(8,128)(2,1)S(1)}, u32[]{:S(2)}, u32[]{:S(2)}) collective-permute-start(bf16[2,128,1792]{2,1,0:T(8,128)(2,1)S(1)} %get-tuple-element.223), channel_id=1, source_target_pairs={{0,1},{1,0},{2,3},{3,2},{4,5},{5,4},{6,7},{7,6},{8,9},{9,8},{10,11... | collective-permute-start | bytes 2752520 | tf_op jit(solution)/shard_map/ppermute | solution.py:19
  183.6 25.6 %collective-permute-start.27 = (bf16[128,2048]{1,0:T(8,128)(2,1)S(1)}, bf16[128,2048]{1,0:T(8,128)(2,1)S(1)}, u32[]{:S(2)}, u32[]{:S(2)}) collective-permute-start(bf16[128,2048]{1,0:T(8,128)(2,1)S(1)} %get-tuple-element.219), channel_id=1, source_target_pairs={{0,8},{1,9},{2,10},{3,11},{4,12},{5,13},{6,14},{7,15},{8,0},{9,1},... | collective-permute-start | bytes 1572872 | tf_op jit(solution)/shard_map/ppermute | solution.py:19
  183.8 22.0 %collective-permute-start.28 = (bf16[128,1792]{1,0:T(8,128)(2,1)}, bf16[128,1792]{1,0:T(8,128)(2,1)S(1)}, u32[]{:S(2)}, u32[]{:S(2)}) collective-permute-start(bf16[128,1792]{1,0:T(8,128)(2,1)} %fusion.9), channel_id=1, source_target_pairs={{0,6},{1,7},{2,4},{3,5},{4,2},{5,3},{6,0},{7,1},{8,14},{9,15},{10,... | collective-permute-start | bytes 1376264 | tf_op jit(solution)/shard_map/ppermute | solution.py:19
  209.5 14.4 %collective-permute-start.31 = (bf16[128,1024]{1,0:T(8,128)(2,1)S(1)}, bf16[128,1024]{1,0:T(8,128)(2,1)S(1)}, u32[]{:S(2)}, u32[]{:S(2)}) collective-permute-start(bf16[128,1024]{1,0:T(8,128)(2,1)S(1)} %fusion.8.hid_ref), channel_id=1, source_target_pairs={{0,8},{1,9},{2,10},{3,11},{4,12},{5,13},{6,14},{7,15},{8,0},{9,1},... | collective-permute-start | bytes 786440 | tf_op jit(solution)/shard_map/ppermute | solution.py:19
  209.6 8.8 %collective-permute-start.34 = (bf16[1,128,1792]{2,1,0:T(8,128)(2,1)S(1)}, bf16[1,128,1792]{2,1,0:T(8,128)(2,1)S(1)}, u32[]{:S(2)}, u32[]{:S(2)}) collective-permute-start(bf16[1,128,1792]{2,1,0:T(8,128)(2,1)S(1)} %get-tuple-element.246), channel_id=1, source_target_pairs={{0,1},{1,0},{2,3},{3,2},{4,5},{5,4},{6,7},{7,6},{8,9},{9,8},{10,11... | collective-permute-start | bytes 1376264 | tf_op jit(solution)/shard_map/ppermute | solution.py:19
  210.1 29.2 %collective-permute-start.33 = (bf16[128,1792]{1,0:T(8,128)(2,1)S(1)}, bf16[128,1792]{1,0:T(8,128)(2,1)S(1)}, u32[]{:S(2)}, u32[]{:S(2)}) collective-permute-start(bf16[128,1792]{1,0:T(8,128)(2,1)S(1)} %get-tuple-element.253), channel_id=1, source_target_pairs={{0,4},{1,5},{2,6},{3,7},{4,0},{5,1},{6,2},{7,3},{8,12},{9,13},{10,... | collective-permute-start | bytes 1376264 | tf_op jit(solution)/shard_map/ppermute | solution.py:19
  212.6 6.7 %copy-start.13 = (bf16[1,128,1792]{2,1,0:T(8,128)(2,1)S(1)}, bf16[1,128,1792]{2,1,0:T(8,128)(2,1)}, u32[]{:S(2)}) copy-start(bf16[1,128,1792]{2,1,0:T(8,128)(2,1)} %copy-done.12) | copy-start | bytes 1376260
  212.6 12.7 %collective-permute-start.32 = (bf16[128,1792]{1,0:T(8,128)(2,1)S(1)}, bf16[128,1792]{1,0:T(8,128)(2,1)S(1)}, u32[]{:S(2)}, u32[]{:S(2)}) collective-permute-start(bf16[128,1792]{1,0:T(8,128)(2,1)S(1)} %get-tuple-element.254), channel_id=1, source_target_pairs={{0,2},{1,3},{2,0},{3,1},{4,6},{5,7},{6,4},{7,5},{8,10},{9,11},{10,... | collective-permute-start | bytes 1376264 | tf_op jit(solution)/shard_map/ppermute | solution.py:19
  218.5 30.8 %collective-permute-start.35 = (bf16[128,1792]{1,0:T(8,128)(2,1)S(1)}, bf16[128,1792]{1,0:T(8,128)(2,1)S(1)}, u32[]{:S(2)}, u32[]{:S(2)}) collective-permute-start(bf16[128,1792]{1,0:T(8,128)(2,1)S(1)} %fusion.10), channel_id=1, source_target_pairs={{0,6},{1,7},{2,4},{3,5},{4,2},{5,3},{6,0},{7,1},{8,14},{9,15},{10,... | collective-permute-start | bytes 1376264 | tf_op jit(solution)/shard_map/ppermute | solution.py:19
  220.7 28.7 %copy-start.15 = (bf16[1,128,1792]{2,1,0:T(8,128)(2,1)S(1)}, bf16[1,128,1792]{2,1,0:T(8,128)(2,1)}, u32[]{:S(2)}) copy-start(bf16[1,128,1792]{2,1,0:T(8,128)(2,1)} %copy-done.14) | copy-start | bytes 1376260
  220.7 30.1 %collective-permute-start.30 = (bf16[128,1792]{1,0:T(8,128)(2,1)S(1)}, bf16[128,1792]{1,0:T(8,128)(2,1)S(1)}, u32[]{:S(2)}, u32[]{:S(2)}) collective-permute-start(bf16[128,1792]{1,0:T(8,128)(2,1)S(1)} %fusion.7), channel_id=1, source_target_pairs={{0,8},{1,9},{2,10},{3,11},{4,12},{5,13},{6,14},{7,15},{8,0},{9,1},... | collective-permute-start | bytes 1376264 | tf_op jit(solution)/shard_map/ppermute | solution.py:19
  225.2 26.6 %copy-start.1 = (bf16[224,2048]{1,0:T(8,128)(2,1)S(1)}, bf16[224,2048]{1,0:T(8,128)(2,1)}, u32[]{:S(2)}) copy-start(bf16[224,2048]{1,0:T(8,128)(2,1)} %param.12) | copy-start | bytes 2752516
  (7 other events, 22.1 us)
